TPU v7x, 256 devices: a whole 4x4x8 slice. The times are simulated.
256 devices in a mesh: orb: 32 (over z, x), slab: 8 (over y, core).
Axes of the slice: x: 4, y: 4, z: 8, core: 2. Of those that a mesh axis runs over, the one named last changes fastest.
Arguments:
- orbitals: bfloat16 [32, 64, 64, 128], P('orb', 'slab'), may hold values from -6 to 6
- pair_table: int32 [1024, 3], P('orb'), may hold values from -1 to 31, as said below
Outputs:
- exchange_action: float32 [32, 64, 64, 128], P('orb', 'slab')
Inputs may be any that keep to these rules, and one draw needn't show every extreme that they name: `pair_table`: A live slot holds (m, n, s) with m <= n and s in 0, 1; an empty slot holds -1 in all three columns. A block of 32 slots has its live slots first. No (m, n, s) appears twice in the table. Exactly 528 slots are live, and the 32 blocks hold, in some order, k * 1 live slots for k = 1 to 32.
All inputs are finite; a program needn't handle non-finite values.
Results may differ from a plain program's by a relative error of at most 0.0003.
Values may be sent and summed in bfloat16 or wider, within the bound.
No kernel may reach another device: no remote copies, remote signals or barrier semaphores. Data moves between devices by JAX's collectives and lax.ppermute only.
A program may use at most 64 MiB of HBM per device.

v0:
```python
import math

import jax
import jax.numpy as jnp
import ml_dtypes
import numpy as np
from jax import lax
from jax.experimental import pallas as pl
from jax.experimental.pallas import tpu as pltpu
from jax.sharding import Mesh
from jax.sharding import PartitionSpec as P

G = 64
ROWS = 2048
CHUNK = 256
KY_STEP = 32
NZ, NX, NY = 8, 4, 4
UNROLL = (8, 2, 8)
COUPLES = 32
CELLS = G * G * G
CODES = 64
FULL = 32500.0
exchange_fraction = 0.25
cell_ratio = 8.0
f32, bf16 = jnp.float32, jnp.bfloat16


def split_np(mat):
    high = mat.astype(ml_dtypes.bfloat16)
    low = (mat - high.astype(np.float64)).astype(ml_dtypes.bfloat16)
    return high, low


def plane_order():
    r = np.arange(32)
    return [16 * (r // 8) + 8 * h + r % 8 for h in (0, 1)]


def weights():
    idx = np.arange(G)
    angles = 2.0 * np.pi / G * (idx[:, None] * idx[None, :] % G)
    hart = (np.cos(angles) + np.sin(angles)) / math.sqrt(G)
    high, low = split_np(np.kron(np.eye(2), hart))
    zero = np.zeros_like(high)
    w_depth = np.block([[high, low], [high, zero]])
    w_rows = np.block([[high, high], [low, zero]])
    order = np.concatenate(plane_order())
    high, low = split_np(hart[np.ix_(order, order)])
    w_planes = np.block([[high, high], [low, np.zeros_like(high)]])
    return w_depth, w_rows, w_planes


def coulomb():
    def folded(v):
        return jnp.minimum(v, G - v).astype(f32)

    pair = lax.broadcasted_iota(jnp.int32, (G // 2, G, 128), 0)
    row = lax.broadcasted_iota(jnp.int32, (G // 2, G, 128), 1)
    lane = lax.broadcasted_iota(jnp.int32, (G // 2, G, 128), 2)
    ky = folded(2 * pair + lane // G)
    kx = cell_ratio * folded(16 * (row % 32 // 8) + 8 * (row // 32) + row % 8)
    kz = folded(lane % G)
    scale = (2.0 * math.pi / G) * (2.0 * math.pi / G)
    squared = scale * (kx * kx + ky * ky + kz * kz)
    safe = jnp.where(squared > 0, squared, 1.0)
    return jnp.where(squared > 0, -exchange_fraction / safe, 0.0)


def assign_kernel(me_ref, code_ref, out_ref, load_ref):
    me = me_ref[0]

    def clear(i, carry):
        load_ref[i] = 0
        return carry

    lax.fori_loop(0, NZ * NX * NY, clear, 0)
    for i in range(17):
        out_ref[i] = 0

    def one_block(b, count):
        def live(state):
            s, _ = state
            return (s < 32) & (code_ref[b, jnp.minimum(s, 31)] >= 0)

        def step(state):
            s, cnt = state
            code = code_ref[b, s]
            m = code & 31
            n = (code >> 5) & 31
            flip = code >> 10
            mz, mx, nz, nx = m >> 2, m & 3, n >> 2, n & 3
            first = mz * 16 + nx * 4 + (nz >> 1)
            second = nz * 16 + mx * 4 + (mz >> 1)
            load_a = load_ref[first]
            load_b = load_ref[second]
            use_a = load_a <= load_b
            chip = jnp.where(use_a, first, second)
            load_ref[chip] = jnp.where(use_a, load_a, load_b) + 1
            task_a = mx + 4 * (nz & 1)
            task_b = nx + 4 * (mz & 1)
            task = jnp.where(use_a, task_a, task_b) + 8 * flip + 16 * (m == n).astype(jnp.int32)
            mine = chip == me

            @pl.when(mine)
            def _():
                out_ref[1 + cnt] = task

            return s + 1, cnt + mine.astype(jnp.int32)

        return lax.while_loop(live, step, (0, count))[1]

    out_ref[0] = lax.fori_loop(0, 32, one_block, 0)


def split(value):
    high = value.astype(bf16)
    return high, (value - high.astype(f32)).astype(bf16)


def depth_transform(value, w_depth):
    high, low = split(value)
    out = jnp.dot(jnp.concatenate([high, low], axis=1), w_depth, preferred_element_type=f32)
    return out[:, :128] + out[:, 128:]


def rows_transform(value, w_rows):
    high, low = split(value)
    half = CHUNK // 2
    top = jnp.concatenate([high[:half], high[half:]], axis=1)
    bottom = jnp.concatenate([low[:half], low[half:]], axis=1)
    out = jnp.dot(w_rows, jnp.concatenate([top, bottom], axis=0), preferred_element_type=f32)
    out = out[:half] + out[half:]
    return jnp.concatenate([out[:, :128], out[:, 128:]], axis=0)


def planes_transform(value, w_planes):
    high, low = split(value)
    out = jnp.dot(w_planes, jnp.concatenate([high, low], axis=0), preferred_element_type=f32)
    return out[:G] + out[G:]


def gather_planes(t_ref, first, low_lanes):
    tops, bottoms = [], []
    for base in range(0, KY_STEP, 8):
        block = jnp.concatenate(
            [t_ref[pl.ds(pl.multiple_of(r * G + first + base, 8), 8)][None] for r in range(32)], axis=0
        )
        block = jnp.swapaxes(block, 0, 1)
        for p in range(0, 8, 2):
            tops.append(jnp.where(low_lanes, block[p], pltpu.roll(block[p + 1], G, 1)))
            bottoms.append(jnp.where(low_lanes, pltpu.roll(block[p], G, 1), block[p + 1]))
    return jnp.concatenate([jnp.concatenate(tops, axis=1), jnp.concatenate(bottoms, axis=1)], axis=0)


def scatter_planes(t_ref, first, value, low_lanes):
    for base in range(0, KY_STEP, 8):
        rows = []
        for p in range(base // 2, base // 2 + 4):
            top = value[:32, p * 128 : (p + 1) * 128]
            bottom = value[32:, p * 128 : (p + 1) * 128]
            rows.append(jnp.where(low_lanes, top, pltpu.roll(bottom, G, 1))[None])
            rows.append(jnp.where(low_lanes, pltpu.roll(top, G, 1), bottom)[None])
        block = jnp.swapaxes(jnp.concatenate(rows, axis=0), 0, 1)
        for r in range(32):
            t_ref[pl.ds(pl.multiple_of(r * G + first + base, 8), 8)] = block[r]


def pairs_kernel(
    tasks_ref, left_ref, same_ref, cross_ref, wz_ref, wy_ref, wx_ref, kern_ref, lacc_ref, sacc_ref, cacc_ref, t_ref
):
    def clear(i, carry):
        rows = pl.ds(pl.multiple_of(i * CHUNK, CHUNK), CHUNK)
        for k in range(4):
            lacc_ref[k, rows] = jnp.zeros((CHUNK, 128), f32)
        for k in range(2):
            sacc_ref[k, rows] = jnp.zeros((CHUNK, 128), f32)
            cacc_ref[k, rows] = jnp.zeros((CHUNK, 128), f32)
        return carry

    lax.fori_loop(0, ROWS // CHUNK, clear, 0)
    low_lanes = lax.broadcasted_iota(jnp.int32, (32, 128), 1) < G

    def run(right_ref, racc_ref, task):
        a = task & 3
        b = (task >> 2) & 1
        second = 1.0 - (task >> 4).astype(f32)

        def forward(i, c):
            rows = pl.ds(pl.multiple_of(i * CHUNK, CHUNK), CHUNK)
            rho = left_ref[a, rows].astype(f32) * right_ref[b, rows].astype(f32)
            t_ref[rows] = rows_transform(depth_transform(rho, wz_ref[...]), wy_ref[...])
            return c

        lax.fori_loop(0, ROWS // CHUNK, forward, 0, unroll=UNROLL[0])

        def middle(i, c):
            first = pl.multiple_of(i * KY_STEP, KY_STEP)
            value = gather_planes(t_ref, first, low_lanes)
            kern = jnp.concatenate(
                [kern_ref[i * (KY_STEP // 2) + j] for j in range(KY_STEP // 2)], axis=1
            )
            value = planes_transform(value, wx_ref[...]) * kern
            value = planes_transform(value, wx_ref[...])
            scatter_planes(t_ref, first, value, low_lanes)
            return c

        lax.fori_loop(0, G // KY_STEP, middle, 0, unroll=UNROLL[1])

        def backward(i, c):
            rows = pl.ds(pl.multiple_of(i * CHUNK, CHUNK), CHUNK)
            v = depth_transform(rows_transform(t_ref[rows], wy_ref[...]), wz_ref[...])
            lacc_ref[a, rows] += v * right_ref[b, rows].astype(f32)
            racc_ref[b, rows] += (v * second) * left_ref[a, rows].astype(f32)
            return c

        lax.fori_loop(0, ROWS // CHUNK, backward, 0, unroll=UNROLL[2])

    def one_task(t, carry):
        task = tasks_ref[1 + t]
        flipped = (task >> 3) & 1 == 1

        @pl.when(jnp.logical_not(flipped))
        def _():
            run(same_ref, sacc_ref, task)

        @pl.when(flipped)
        def _():
            run(cross_ref, cacc_ref, task)

        return carry

    lax.fori_loop(0, tasks_ref[0], one_task, 0)


def quantize_piece(value_of, write):
    codes = []
    for p in range(8):
        rows = pl.ds(p * G, G)
        value = value_of(rows)
        largest = jnp.max(jnp.abs(value), axis=0, keepdims=True)
        code = jnp.ceil(jnp.log2(jnp.maximum(largest, 1e-30)) * CODES)
        codes.append(code)
        value = jnp.round(value * (jnp.exp2(code * (-1.0 / CODES)) * FULL))
        write(rows, value.astype(jnp.int32).astype(jnp.int16))
    codes = jnp.concatenate(codes + [jnp.zeros((8, 128), f32)], axis=0)
    write(pl.ds(512, 16), codes.astype(jnp.int32).astype(jnp.int16))


def quantize_left_kernel(in_ref, out_ref):
    for k in range(out_ref.shape[0]):

        def write(rows, value):
            out_ref[k, rows] = value

        quantize_piece(lambda rows: in_ref[k, rows], write)


def quantize_right_kernel(z_ref, first_ref, second_ref, *out_refs):
    for k in range(NZ):
        piece = (z_ref[0] + k) & (NZ - 1)

        def write(rows, value):
            out_refs[k][rows] = value

        quantize_piece(lambda rows: first_ref[piece, rows] + second_ref[piece, rows], write)


def combine_kernel(left_ref, *refs):
    out_ref = refs[-1]

    def read(part, rows):
        ref = left_ref.at[part] if part < NX * NY else refs[part - NX * NY]
        return ref[rows].astype(jnp.int32).astype(f32)

    count = NX * NY + NZ
    scales = [
        jnp.exp2(read(k, pl.ds(512, 16))[:8] * (1.0 / CODES)) * (1.0 / FULL) for k in range(count)
    ]
    for p in range(8):
        rows = pl.ds(p * G, G)
        total = jnp.zeros((G, 128), f32)
        for k in range(count):
            total = total + read(k, rows) * scales[k][p : p + 1]
        out_ref[rows] = total


def quantize_left(lacc):
    pieces, step = NX * NY, 4
    return pl.pallas_call(
        quantize_left_kernel,
        grid=(pieces // step,),
        out_shape=jax.ShapeDtypeStruct((pieces, 528, 128), jnp.int16),
        in_specs=[pl.BlockSpec((step, 512, 128), lambda i: (i, 0, 0))],
        out_specs=pl.BlockSpec((step, 528, 128), lambda i: (i, 0, 0)),
        cost_estimate=pl.CostEstimate(flops=0, bytes_accessed=10 * 1000 * 1000, transcendentals=0),
        name="quantize_left",
    )(lacc)


def quantize_right(z, first, second):
    return pl.pallas_call(
        quantize_right_kernel,
        out_shape=(jax.ShapeDtypeStruct((528, 128), jnp.int16),) * NZ,
        in_specs=smem_specs(1) + vmem_specs(2),
        out_specs=tuple(vmem_specs(NZ)),
        cost_estimate=pl.CostEstimate(flops=0, bytes_accessed=8 * 1000 * 1000, transcendentals=0),
        name="quantize_right",
    )(z.astype(jnp.int32).reshape(1), first, second)


def combine(left_parts, right_parts):
    return pl.pallas_call(
        combine_kernel,
        out_shape=jax.ShapeDtypeStruct((512, 128), f32),
        in_specs=vmem_specs(1 + len(right_parts)),
        out_specs=vmem_specs(1)[0],
        name="combine",
    )(left_parts, *right_parts)


def overlap_kernel(core_ref, own_ref, other_ref, phi_ref, x_ref, out_ref, same_ref, cross_ref):
    keep = (lax.broadcasted_iota(jnp.int32, (G, 128), 1) < G) == (core_ref[0] == 0)
    same_ref[...] = jnp.zeros_like(same_ref)
    cross_ref[...] = jnp.zeros_like(cross_ref)

    def rows_block(i, carry):
        rows = pl.ds(pl.multiple_of(i * G, G), G)
        value = jnp.where(keep, own_ref[rows], pltpu.roll(other_ref[rows], G, 1))
        turned = pltpu.roll(value, G, 1)
        x_ref[rows] = value
        for o in range(COUPLES):
            phi = phi_ref[o, rows].astype(f32)
            same_ref[o] += jnp.sum((phi * value).reshape(8, 8, 128), axis=0)
            cross_ref[o] += jnp.sum((phi * turned).reshape(8, 8, 128), axis=0)
        return carry

    lax.fori_loop(0, 8, rows_block, 0)
    out_ref[pl.ds(0, COUPLES)] = jnp.sum(same_ref[...], axis=1)
    out_ref[pl.ds(COUPLES, COUPLES)] = jnp.sum(cross_ref[...], axis=1)


def project_kernel(x_ref, phi_ref, over_ref, out_ref, coef_ref):
    lane = lax.broadcasted_iota(jnp.int32, (COUPLES, 128), 1)
    for k in range(2):
        part = over_ref[pl.ds(k * COUPLES, COUPLES)]
        low = jnp.sum(jnp.where(lane < G, part, 0.0), axis=1, keepdims=True)
        high = jnp.sum(jnp.where(lane < G, 0.0, part), axis=1, keepdims=True)
        coef_ref[k] = jnp.where(lane < G, low, high) / CELLS

    def rows_block(i, carry):
        rows = pl.ds(pl.multiple_of(i * G, G), G)
        same = jnp.zeros((G, 128), f32)
        cross = jnp.zeros((G, 128), f32)
        for o in range(COUPLES):
            phi = phi_ref[o, rows].astype(f32)
            same = same + phi * coef_ref[0, o : o + 1]
            cross = cross + phi * coef_ref[1, o : o + 1]
        out_ref[rows] = x_ref[rows] - same - pltpu.roll(cross, G, 1)
        return carry

    lax.fori_loop(0, 8, rows_block, 0)


def vmem_specs(n):
    return [pl.BlockSpec(memory_space=pltpu.VMEM)] * n


def smem_specs(n):
    return [pl.BlockSpec(memory_space=pltpu.SMEM)] * n


def lane_exchange(mine, core):
    other = lax.ppermute(mine, "core", [(0, 1), (1, 0)])
    lane = lax.broadcasted_iota(jnp.int32, mine.shape, mine.ndim - 1)
    return jnp.where((lane < G) == (core == 0), mine, jnp.roll(other, G, axis=-1))


def moves():
    return [(z * NY + y, ((z & 1) * NY + y) * NY + (z >> 1)) for z in range(NZ) for y in range(NY)]


def ring(size, step):
    return [(i, (i + step) % size) for i in range(size)]


def sum_over_slab(value):
    value = value + lax.ppermute(value, "core", ring(2, 1))
    near = lax.ppermute(value, "y", ring(NY, 1))
    back = lax.ppermute(value, "y", ring(NY, 3))
    far = lax.ppermute(value, "y", ring(NY, 2))
    return (value + far) + (near + back)


def returns(k):
    pairs = []
    for z in range(NZ):
        for y in range(NY):
            q = (z + k) % NZ
            pairs.append((z * NY + y, (2 * y + q // NY) * NY + q % NY))
    return pairs


def local(orbitals, pair_table):
    z, x, y, core = (lax.axis_index(a) for a in ("z", "x", "y", "core"))
    mine = orbitals[0]
    live = pair_table[:, 0] >= 0
    code = jnp.where(live, pair_table[:, 0] + 32 * pair_table[:, 1] + 1024 * pair_table[:, 2], -1)
    own = lane_exchange(mine, core)
    phi_all = lax.all_gather(orbitals, ("z", "x"), axis=0, tiled=True)
    moved = lax.ppermute(own, ("z", "y"), moves())
    own, code = lax.optimization_barrier((own, code))
    codes = lax.all_gather(code[None], ("z", "x"), axis=0, tiled=True)
    moved, own, codes = lax.optimization_barrier((moved, own, codes))
    same = lax.all_gather(moved, "z", axis=0, tiled=True)
    spread = jnp.broadcast_to(own[None], (NX * NY,) + own.shape)
    left = lax.all_to_all(spread, ("x", "y"), split_axis=0, concat_axis=0, tiled=True)

    me = (z * 16 + x * 4 + y).astype(jnp.int32).reshape(1)
    tasks = pl.pallas_call(
        assign_kernel,
        out_shape=jax.ShapeDtypeStruct((17,), jnp.int32),
        in_specs=smem_specs(2),
        out_specs=pl.BlockSpec(memory_space=pltpu.SMEM),
        scratch_shapes=[pltpu.SMEM((NZ * NX * NY,), jnp.int32)],
        cost_estimate=pl.CostEstimate(flops=0, bytes_accessed=60 * 1000 * 1000, transcendentals=0),
        name="assign",
    )(me, codes)
    same, tasks = lax.optimization_barrier((same, tasks))
    cross = lax.ppermute(same, "core", ring(2, 1))

    w_depth, w_rows, w_planes = (jnp.asarray(w) for w in weights())
    lacc, sacc, cacc = pl.pallas_call(
        pairs_kernel,
        out_shape=tuple(jax.ShapeDtypeStruct((k, ROWS, 128), f32) for k in (4, 2, 2)),
        in_specs=smem_specs(1) + vmem_specs(7),
        out_specs=tuple(vmem_specs(3)),
        scratch_shapes=[pltpu.VMEM((ROWS, 128), f32)],
        compiler_params=pltpu.CompilerParams(vmem_limit_bytes=48 * 1024 * 1024),
        cost_estimate=pl.CostEstimate(flops=0, bytes_accessed=180 * 1000 * 1000, transcendentals=0),
        name="pairs",
    )(
        tasks,
        left.reshape(4, ROWS, 128),
        same.reshape(2, ROWS, 128),
        cross.reshape(2, ROWS, 128),
        w_depth,
        w_rows,
        w_planes,
        coulomb(),
    )
    lacc, sacc, cacc, phi_all = lax.optimization_barrier((lacc, sacc, cacc, phi_all))

    other = lax.ppermute(cacc, "core", ring(2, 1))
    right_parts = quantize_right(z, sacc.reshape(NZ, 512, 128), other.reshape(NZ, 512, 128))
    left_parts = quantize_left(lacc.reshape(NX * NY, 512, 128))
    left_parts, *right_parts = lax.optimization_barrier((left_parts, *right_parts))
    left_parts = lax.all_to_all(left_parts, ("x", "y"), split_axis=0, concat_axis=0, tiled=True)
    right_parts = [
        lax.ppermute(part, ("z", "y"), returns(k)) for k, part in enumerate(right_parts)
    ]
    action = combine(left_parts, right_parts)
    action_other = lax.ppermute(action, "core", ring(2, 1))

    phi_rows = phi_all.reshape(COUPLES, 512, 128)
    slab_action, over = pl.pallas_call(
        overlap_kernel,
        out_shape=(
            jax.ShapeDtypeStruct((512, 128), f32),
            jax.ShapeDtypeStruct((2 * COUPLES, 128), f32),
        ),
        in_specs=smem_specs(1) + vmem_specs(3),
        out_specs=tuple(vmem_specs(2)),
        scratch_shapes=[pltpu.VMEM((COUPLES, 8, 128), f32)] * 2,
        name="overlap",
    )(core.astype(jnp.int32).reshape(1), action, action_other, phi_rows)
    out = pl.pallas_call(
        project_kernel,
        out_shape=jax.ShapeDtypeStruct((512, 128), f32),
        in_specs=vmem_specs(3),
        out_specs=vmem_specs(1)[0],
        scratch_shapes=[pltpu.VMEM((2, COUPLES, 128), f32)],
        name="project",
    )(slab_action, phi_rows, sum_over_slab(over))
    return out.reshape(1, 8, G, 128)


def solution(mesh):
    grid = Mesh(mesh.devices.reshape(NZ, NX, NY, 2), ("z", "x", "y", "core"))
    placed = (P(("z", "x"), ("y", "core"), None, None), P(("z", "x"), None))
    return jax.shard_map(
        local,
        mesh=grid,
        in_specs=placed,
        out_specs=P(("z", "x"), ("y", "core"), None, None),
        check_vma=False,
    )
```

profile of v0, /device:TPU:1, one launch (start us, length us, event | category | flops | bytes accessed | tf_op | source)
XLA Modules:
  0.0 300.2 jit_solution(16749970413264254345)
XLA Ops:
  6.5 3.2 %collective-permute-start = (bf16[8,64,128]{2,1,0:T(8,128)(2,1)}, bf16[8,64,128]{2,1,0:T(8,128)(2,1)S(1)}, u32[]{:S(2)}, u32[]{:S(2)}) collective-permute-start(bf16[8,64,128]{2,1,0:T(8,128)(2,1)} %bitcast.23), channel_id=1, source_target_pairs={{0,1},{1,0},{2,3},{3,2},{4,5},{5,4},{6,7},{7,6},{8,9},{9,8},{10,11... | collective-permute-start | bytes 393224 | tf_op jit(solution)/shard_map/ppermute | solution.py:373
  14.6 22.6 %all-reduce = s32[1024]{0:T(1024)S(1)} all-reduce(s32[1024]{0:T(1024)S(1)} %dynamic-update-slice), channel_id=2, replica_groups=mesh['z'=8,'x'=4,'y'=4,'core'=2] {'z','x'}, use_global_device_ids=true, to_apply=%add | all-reduce | flops 1024 | bytes 8192
  41.2 4.6 %all-to-all-start = ((bf16[16,8,64,128]{3,2,1,0:T(8,128)(2,1)}), bf16[16,8,64,128]{3,2,1,0:T(8,128)(2,1)}, u32[]{:S(2)}, u32[]{:S(2)}) async-start(bf16[16,8,64,128]{3,2,1,0:T(8,128)(2,1)} %broadcast_in_dim.20), calls=%async_computation | async-start | bytes 4194304 | tf_op jit(solution)/shard_map/all_to_all | solution.py:416
  45.8 18.4 %assign.1.tasks_ref = s32[17]{0:T(128)} custom-call(s32[1]{0:T(128)} %bitcast.4.me_ref, s32[32,32]{1,0:T(8,128)} %reshape.55.code_ref), custom_call_target="tpu_custom_call" | custom-call | bytes 60000000 | tf_op jit(solution)/shard_map/assign/pallas_call | solution.py:419
  64.2 9.2 %all-gather.4.cloned.1.call-done = bf16[64,64,128]{2,1,0:T(8,128)(2,1)} async-done(((bf16[8,64,128]{2,1,0:T(8,128)(2,1)}), bf16[64,64,128]{2,1,0:T(8,128)(2,1)}) %all-gather.4.cloned.1.call-update) | async-done | bytes 1048592 | tf_op jit(solution)/shard_map/all_gather | solution.py:414
  73.4 4.7 %collective-permute-start.2 = (bf16[64,64,128]{2,1,0:T(8,128)(2,1)}, bf16[64,64,128]{2,1,0:T(8,128)(2,1)S(1)}, u32[]{:S(2)}, u32[]{:S(2)}) collective-permute-start(bf16[64,64,128]{2,1,0:T(8,128)(2,1)} %all-gather.4.cloned.1.call-done), channel_id=1, source_target_pairs={{0,1},{1,0},{2,3},{3,2},{4,5},{5,4},{6,7},{7,6},{8,9},{9,8},{10,11... | collective-permute-start | bytes 3145736 | tf_op jit(solution)/shard_map/ppermute | solution.py:429
  82.4 13.0 %pairs.1 = (f32[4,2048,128]{2,1,0:T(8,128)}, f32[2,2048,128]{2,1,0:T(8,128)S(1)}, f32[2,2048,128]{2,1,0:T(8,128)}) custom-call(s32[17]{0:T(128)S(1)} %copy-done.5, bf16[4,2048,128]{2,1,0:T(8,128)(2,1)} %bitcast.5.left_ref, bf16[2,2048,128]{2,1,0:T(8,128)(2,1)S(1)} %bitcast.17, bf16[2,2048,128]{2,1,0:T(8,128)(2,1)S(1)} %bitcast.18, ...), custom_call_target="tpu_custom_call" | custom-call | bytes 180000000 | tf_op jit(solution)/shard_map/pairs/pallas_call | solution.py:432
  96.8 60.8 %all-gather.6.cloned.1.call-done = bf16[32,8,64,128]{3,2,1,0:T(8,128)(2,1)} async-done(((bf16[1,8,64,128]{3,2,1,0:T(8,128)(2,1)}), bf16[32,8,64,128]{3,2,1,0:T(8,128)(2,1)}) %all-gather.6.cloned.1.call-update) | async-done | bytes 4194320 | tf_op jit(solution)/shard_map/all_gather | solution.py:409
  157.6 3.3 %collective-permute-start.3 = (f32[2,2048,128]{2,1,0:T(8,128)}, f32[2,2048,128]{2,1,0:T(8,128)S(1)}, u32[]{:S(2)}, u32[]{:S(2)}) collective-permute-start(f32[2,2048,128]{2,1,0:T(8,128)} %get-tuple-element.50), channel_id=1, source_target_pairs={{0,1},{1,0},{2,3},{3,2},{4,5},{5,4},{6,7},{7,6},{8,9},{9,8},{10,11... | collective-permute-start | bytes 6291464 | tf_op jit(solution)/shard_map/ppermute | solution.py:453
  161.0 4.6 %quantize_left.1 = s16[16,528,128]{2,1,0:T(8,128)(2,1)} custom-call(f32[16,512,128]{2,1,0:T(8,128)} %bitcast.21), custom_call_target="tpu_custom_call" | custom-call | bytes 10000000 | tf_op jit(solution)/shard_map/quantize_left/pallas_call | solution.py:289
  166.9 3.6 %quantize_right.1 = (s16[528,128]{1,0:T(8,128)(2,1)}, s16[528,128]{1,0:T(8,128)(2,1)}, s16[528,128]{1,0:T(8,128)(2,1)}, s16[528,128]{1,0:T(8,128)(2,1)}, s16[528...) custom-call(s32[1]{0:T(128)} %bitcast.9.z_ref, ...), custom_call_target="tpu_custom_call" | custom-call | bytes 8000000 | tf_op jit(solution)/shard_map/quantize_right/pallas_call | solution.py:301
  170.5 5.1 %all-to-all-start.1 = ((s16[16,528,128]{2,1,0:T(8,128)(2,1)}), s16[16,528,128]{2,1,0:T(8,128)(2,1)S(1)}, u32[]{:S(2)}, u32[]{:S(2)}) async-start(s16[16,528,128]{2,1,0:T(8,128)(2,1)} %quantize_left.1), calls=%async_computation.1 | async-start | bytes 4325376 | tf_op jit(solution)/shard_map/all_to_all | solution.py:457
  175.7 6.0 %collective-permute-start.10 = (s16[528,128]{1,0:T(8,128)(2,1)S(1)}, s16[528,128]{1,0:T(8,128)(2,1)S(1)}, u32[]{:S(2)}, u32[]{:S(2)}) collective-permute-start(s16[528,128]{1,0:T(8,128)(2,1)S(1)} %copy-done.22), channel_id=1, source_target_pairs={{0,36},{2,100},{4,164},{6,228},{32,38},{34,102},{36,166},{38,230},... | collective-permute-start | bytes 405512 | tf_op jit(solution)/shard_map/ppermute | solution.py:459
  181.7 3.5 %collective-permute-start.11 = (s16[528,128]{1,0:T(8,128)(2,1)S(1)}, s16[528,128]{1,0:T(8,128)(2,1)S(1)}, u32[]{:S(2)}, u32[]{:S(2)}) collective-permute-start(s16[528,128]{1,0:T(8,128)(2,1)S(1)} %copy-done.21), channel_id=1, source_target_pairs={{0,38},{2,102},{4,166},{6,230},{32,0},{34,64},{36,128},{38,192},{6... | collective-permute-start | bytes 405512 | tf_op jit(solution)/shard_map/ppermute | solution.py:459
  185.9 6.0 %collective-permute-start.5 = (s16[528,128]{1,0:T(8,128)(2,1)}, s16[528,128]{1,0:T(8,128)(2,1)S(1)}, u32[]{:S(2)}, u32[]{:S(2)}) collective-permute-start(s16[528,128]{1,0:T(8,128)(2,1)} %get-tuple-element.61), channel_id=1, source_target_pairs={{0,2},{2,66},{4,130},{6,194},{32,4},{34,68},{36,132},{38,196},{64,... | collective-permute-start | bytes 405512 | tf_op jit(solution)/shard_map/ppermute | solution.py:459
  191.9 7.3 %collective-permute-start.6 = (s16[528,128]{1,0:T(8,128)(2,1)}, s16[528,128]{1,0:T(8,128)(2,1)S(1)}, u32[]{:S(2)}, u32[]{:S(2)}) collective-permute-start(s16[528,128]{1,0:T(8,128)(2,1)} %get-tuple-element.62), channel_id=1, source_target_pairs={{0,4},{2,68},{4,132},{6,196},{32,6},{34,70},{36,134},{38,198},{64,... | collective-permute-start | bytes 405512 | tf_op jit(solution)/shard_map/ppermute | solution.py:459
  201.2 27.5 %collective-permute-done.11.refs_7_ = s16[528,128]{1,0:T(8,128)(2,1)S(1)} collective-permute-done((s16[528,128]{1,0:T(8,128)(2,1)S(1)}, s16[528,128]{1,0:T(8,128)(2,1)S(1)}, u32[]{:S(2)}, u32[]{:S(2)}) %collective-permute-start.11) | collective-permute-done | bytes 135200 | tf_op jit(solution)/shard_map/ppermute | solution.py:459
  228.7 26.8 %collective-permute-start.9 = (s16[528,128]{1,0:T(8,128)(2,1)S(1)}, s16[528,128]{1,0:T(8,128)(2,1)S(1)}, u32[]{:S(2)}, u32[]{:S(2)}) collective-permute-start(s16[528,128]{1,0:T(8,128)(2,1)S(1)} %copy-done.18), channel_id=1, source_target_pairs={{0,34},{2,98},{4,162},{6,226},{32,36},{34,100},{36,164},{38,228},{... | collective-permute-start | bytes 405512 | tf_op jit(solution)/shard_map/ppermute | solution.py:459
  255.6 2.2 collective-permute-done.9.refs_5_
  259.8 3.5 %combine.1.own_ref = f32[512,128]{1,0:T(8,128)} custom-call(s16[16,528,128]{2,1,0:T(8,128)(2,1)} %copy-done.6, s16[528,128]{1,0:T(8,128)(2,1)} %copy-done.11, s16[528,128]{1,0:T(8,128)(2,1)} %copy-done.12, s16[528,128]{1,0:T(8,128)(2,1)} %copy-done.13, s16[528,128]{1,0:T(8,128)(2,1)} %copy-done.14, s16[528,128]{1,0:T(8,128)(2,1)} %copy-done.15, ...), custom_call_target="tpu_custom_call" | custom-call | tf_op jit(solution)/shard_map/combine/pallas_call | solution.py:312
  267.4 5.6 %overlap.1 = (f32[512,128]{1,0:T(8,128)}, f32[64,128]{1,0:T(8,128)}) custom-call(s32[1]{0:T(128)} %bitcast.core_ref, f32[512,128]{1,0:T(8,128)} %combine.1.own_ref, f32[512,128]{1,0:T(8,128)} %copy-done.8, bf16[32,512,128]{2,1,0:T(8,128)(2,1)} %bitcast.19), custom_call_target="tpu_custom_call" | custom-call | tf_op jit(solution)/shard_map/overlap/pallas_call | solution.py:465
  275.2 6.9 %collective-permute-start.14 = (f32[64,128]{1,0:T(8,128)S(1)}, f32[64,128]{1,0:T(8,128)S(1)}, u32[]{:S(2)}, u32[]{:S(2)}) collective-permute-start(f32[64,128]{1,0:T(8,128)S(1)} %add.75), channel_id=1, source_target_pairs={{0,4},{2,6},{4,0},{6,2},{1,5},{3,7},{5,1},{7,3},{8,12},{10,14},{12... | collective-permute-start | bytes 98312 | tf_op jit(solution)/shard_map/ppermute | solution.py:390
  282.0 3.1 %collective-permute-start.15 = (f32[64,128]{1,0:T(8,128)S(1)}, f32[64,128]{1,0:T(8,128)S(1)}, u32[]{:S(2)}, u32[]{:S(2)}) collective-permute-start(f32[64,128]{1,0:T(8,128)S(1)} %add.75), channel_id=1, source_target_pairs={{0,2},{2,4},{4,6},{6,0},{1,3},{3,5},{5,7},{7,1},{8,10},{10,12},{12... | collective-permute-start | bytes 98312 | tf_op jit(solution)/shard_map/ppermute | solution.py:388
  288.6 4.8 %project.1 = f32[512,128]{1,0:T(8,128)} custom-call(f32[512,128]{1,0:T(8,128)} %get-tuple-element.69.x_ref, bf16[32,512,128]{2,1,0:T(8,128)(2,1)} %bitcast.20, f32[64,128]{1,0:T(8,128)} %add_add_fusion.over_ref), custom_call_target="tpu_custom_call" | custom-call | tf_op jit(solution)/shard_map/project/pallas_call | solution.py:476
  (95 shorter events, 29.5 us)
Async XLA Ops:
  6.5 66.8 %all-gather.4.cloned.1.call-start = ((), (), s32[]{:S(2)}) async-start(), calls=%async_computation.2 | async-start | bytes 1179648 | tf_op jit(solution)/shard_map/all_gather | solution.py:414
  6.5 5.2 %collective-permute-start = (bf16[8,64,128]{2,1,0:T(8,128)(2,1)}, bf16[8,64,128]{2,1,0:T(8,128)(2,1)S(1)}, u32[]{:S(2)}, u32[]{:S(2)}) collective-permute-start(bf16[8,64,128]{2,1,0:T(8,128)(2,1)} %bitcast.23), channel_id=1, source_target_pairs={{0,1},{1,0},{2,3},{3,2},{4,5},{5,4},{6,7},{7,6},{8,9},{9,8},{10,11... | collective-permute-start | bytes 393224 | tf_op jit(solution)/shard_map/ppermute | solution.py:373
  12.9 25.0 %collective-permute-start.1 = (bf16[8,64,128]{2,1,0:T(8,128)(2,1)S(1)}, bf16[8,64,128]{2,1,0:T(8,128)(2,1)S(1)}, u32[]{:S(2)}, u32[]{:S(2)}) collective-permute-start(bf16[8,64,128]{2,1,0:T(8,128)(2,1)S(1)} %maximum_select_fusion), channel_id=1, source_target_pairs={{0,0},{2,32},{4,64},{6,96},{32,128},{34,160},{36,192},{38,224},{64... | collective-permute-start | bytes 393224 | tf_op jit(solution)/shard_map/ppermute | solution.py:410
  38.5 119.1 %all-gather.6.cloned.1.call-start = ((), (), s32[]{:S(2)}) async-start(), calls=%async_computation.3 | async-start | bytes 4325376 | tf_op jit(solution)/shard_map/all_gather | solution.py:409
  41.2 37.3 %all-to-all-start = ((bf16[16,8,64,128]{3,2,1,0:T(8,128)(2,1)}), bf16[16,8,64,128]{3,2,1,0:T(8,128)(2,1)}, u32[]{:S(2)}, u32[]{:S(2)}) async-start(bf16[16,8,64,128]{3,2,1,0:T(8,128)(2,1)} %broadcast_in_dim.20), calls=%async_computation | async-start | bytes 4194304 | tf_op jit(solution)/shard_map/all_to_all | solution.py:416
  73.4 7.2 %collective-permute-start.2 = (bf16[64,64,128]{2,1,0:T(8,128)(2,1)}, bf16[64,64,128]{2,1,0:T(8,128)(2,1)S(1)}, u32[]{:S(2)}, u32[]{:S(2)}) collective-permute-start(bf16[64,64,128]{2,1,0:T(8,128)(2,1)} %all-gather.4.cloned.1.call-done), channel_id=1, source_target_pairs={{0,1},{1,0},{2,3},{3,2},{4,5},{5,4},{6,7},{7,6},{8,9},{9,8},{10,11... | collective-permute-start | bytes 3145736 | tf_op jit(solution)/shard_map/ppermute | solution.py:429
  157.6 7.9 %collective-permute-start.3 = (f32[2,2048,128]{2,1,0:T(8,128)}, f32[2,2048,128]{2,1,0:T(8,128)S(1)}, u32[]{:S(2)}, u32[]{:S(2)}) collective-permute-start(f32[2,2048,128]{2,1,0:T(8,128)} %get-tuple-element.50), channel_id=1, source_target_pairs={{0,1},{1,0},{2,3},{3,2},{4,5},{5,4},{6,7},{7,6},{8,9},{9,8},{10,11... | collective-permute-start | bytes 6291464 | tf_op jit(solution)/shard_map/ppermute | solution.py:453
  170.5 58.2 %copy-start.19 = (s16[528,128]{1,0:T(8,128)(2,1)S(1)}, s16[528,128]{1,0:T(8,128)(2,1)}, u32[]{:S(2)}) copy-start(s16[528,128]{1,0:T(8,128)(2,1)} %get-tuple-element.64) | copy-start | bytes 405508
  170.5 58.2 %copy-start.18 = (s16[528,128]{1,0:T(8,128)(2,1)S(1)}, s16[528,128]{1,0:T(8,128)(2,1)}, u32[]{:S(2)}) copy-start(s16[528,128]{1,0:T(8,128)(2,1)} %get-tuple-element.65) | copy-start | bytes 405508
  170.5 87.3 %all-to-all-start.1 = ((s16[16,528,128]{2,1,0:T(8,128)(2,1)}), s16[16,528,128]{2,1,0:T(8,128)(2,1)S(1)}, u32[]{:S(2)}, u32[]{:S(2)}) async-start(s16[16,528,128]{2,1,0:T(8,128)(2,1)} %quantize_left.1), calls=%async_computation.1 | async-start | bytes 4325376 | tf_op jit(solution)/shard_map/all_to_all | solution.py:457
  175.7 23.6 %collective-permute-start.10 = (s16[528,128]{1,0:T(8,128)(2,1)S(1)}, s16[528,128]{1,0:T(8,128)(2,1)S(1)}, u32[]{:S(2)}, u32[]{:S(2)}) collective-permute-start(s16[528,128]{1,0:T(8,128)(2,1)S(1)} %copy-done.22), channel_id=1, source_target_pairs={{0,36},{2,100},{4,164},{6,228},{32,38},{34,102},{36,166},{38,230},... | collective-permute-start | bytes 405512 | tf_op jit(solution)/shard_map/ppermute | solution.py:459
  181.7 47.0 %collective-permute-start.11 = (s16[528,128]{1,0:T(8,128)(2,1)S(1)}, s16[528,128]{1,0:T(8,128)(2,1)S(1)}, u32[]{:S(2)}, u32[]{:S(2)}) collective-permute-start(s16[528,128]{1,0:T(8,128)(2,1)S(1)} %copy-done.21), channel_id=1, source_target_pairs={{0,38},{2,102},{4,166},{6,230},{32,0},{34,64},{36,128},{38,192},{6... | collective-permute-start | bytes 405512 | tf_op jit(solution)/shard_map/ppermute | solution.py:459
  185.3 43.4 %collective-permute-start.4 = (s16[528,128]{1,0:T(8,128)(2,1)S(1)}, s16[528,128]{1,0:T(8,128)(2,1)S(1)}, u32[]{:S(2)}, u32[]{:S(2)}) collective-permute-start(s16[528,128]{1,0:T(8,128)(2,1)S(1)} %copy-done.20), channel_id=1, source_target_pairs={{0,0},{2,64},{4,128},{6,192},{32,2},{34,66},{36,130},{38,194},{64,... | collective-permute-start | bytes 405512 | tf_op jit(solution)/shard_map/ppermute | solution.py:459
  185.9 69.6 %collective-permute-start.5 = (s16[528,128]{1,0:T(8,128)(2,1)}, s16[528,128]{1,0:T(8,128)(2,1)S(1)}, u32[]{:S(2)}, u32[]{:S(2)}) collective-permute-start(s16[528,128]{1,0:T(8,128)(2,1)} %get-tuple-element.61), channel_id=1, source_target_pairs={{0,2},{2,66},{4,130},{6,194},{32,4},{34,68},{36,132},{38,196},{64,... | collective-permute-start | bytes 405512 | tf_op jit(solution)/shard_map/ppermute | solution.py:459
  191.9 63.6 %collective-permute-start.6 = (s16[528,128]{1,0:T(8,128)(2,1)}, s16[528,128]{1,0:T(8,128)(2,1)S(1)}, u32[]{:S(2)}, u32[]{:S(2)}) collective-permute-start(s16[528,128]{1,0:T(8,128)(2,1)} %get-tuple-element.62), channel_id=1, source_target_pairs={{0,4},{2,68},{4,132},{6,196},{32,6},{34,70},{36,134},{38,198},{64,... | collective-permute-start | bytes 405512 | tf_op jit(solution)/shard_map/ppermute | solution.py:459
  199.3 58.5 %copy-start.9 = (s16[528,128]{1,0:T(8,128)(2,1)}, s16[528,128]{1,0:T(8,128)(2,1)S(1)}, u32[]{:S(2)}) copy-start(s16[528,128]{1,0:T(8,128)(2,1)S(1)} %collective-permute-done.10.refs_6_) | copy-start | bytes 405508
  199.3 56.3 %collective-permute-start.7 = (s16[528,128]{1,0:T(8,128)(2,1)}, s16[528,128]{1,0:T(8,128)(2,1)S(1)}, u32[]{:S(2)}, u32[]{:S(2)}) collective-permute-start(s16[528,128]{1,0:T(8,128)(2,1)} %get-tuple-element.63), channel_id=1, source_target_pairs={{0,6},{2,70},{4,134},{6,198},{32,32},{34,96},{36,160},{38,224},{64... | collective-permute-start | bytes 405512 | tf_op jit(solution)/shard_map/ppermute | solution.py:459
  228.7 26.9 %collective-permute-start.8 = (s16[528,128]{1,0:T(8,128)(2,1)S(1)}, s16[528,128]{1,0:T(8,128)(2,1)S(1)}, u32[]{:S(2)}, u32[]{:S(2)}) collective-permute-start(s16[528,128]{1,0:T(8,128)(2,1)S(1)} %copy-done.19), channel_id=1, source_target_pairs={{0,32},{2,96},{4,160},{6,224},{32,34},{34,98},{36,162},{38,226},{6... | collective-permute-start | bytes 405512 | tf_op jit(solution)/shard_map/ppermute | solution.py:459
  228.7 29.0 %collective-permute-start.9 = (s16[528,128]{1,0:T(8,128)(2,1)S(1)}, s16[528,128]{1,0:T(8,128)(2,1)S(1)}, u32[]{:S(2)}, u32[]{:S(2)}) collective-permute-start(s16[528,128]{1,0:T(8,128)(2,1)S(1)} %copy-done.18), channel_id=1, source_target_pairs={{0,34},{2,98},{4,162},{6,226},{32,36},{34,100},{36,164},{38,228},{... | collective-permute-start | bytes 405512 | tf_op jit(solution)/shard_map/ppermute | solution.py:459
  263.4 3.3 %collective-permute-start.12 = (f32[512,128]{1,0:T(8,128)}, f32[512,128]{1,0:T(8,128)S(1)}, u32[]{:S(2)}, u32[]{:S(2)}) collective-permute-start(f32[512,128]{1,0:T(8,128)} %combine.1.own_ref), channel_id=1, source_target_pairs={{0,1},{1,0},{2,3},{3,2},{4,5},{5,4},{6,7},{7,6},{8,9},{9,8},{10,11... | collective-permute-start | bytes 786440 | tf_op jit(solution)/shard_map/ppermute | solution.py:462
  273.0 1.4 collective-permute-start.13
  275.2 10.0 %collective-permute-start.14 = (f32[64,128]{1,0:T(8,128)S(1)}, f32[64,128]{1,0:T(8,128)S(1)}, u32[]{:S(2)}, u32[]{:S(2)}) collective-permute-start(f32[64,128]{1,0:T(8,128)S(1)} %add.75), channel_id=1, source_target_pairs={{0,4},{2,6},{4,0},{6,2},{1,5},{3,7},{5,1},{7,3},{8,12},{10,14},{12... | collective-permute-start | bytes 98312 | tf_op jit(solution)/shard_map/ppermute | solution.py:390
  282.0 4.2 %collective-permute-start.15 = (f32[64,128]{1,0:T(8,128)S(1)}, f32[64,128]{1,0:T(8,128)S(1)}, u32[]{:S(2)}, u32[]{:S(2)}) collective-permute-start(f32[64,128]{1,0:T(8,128)S(1)} %add.75), channel_id=1, source_target_pairs={{0,2},{2,4},{4,6},{6,0},{1,3},{3,5},{5,7},{7,1},{8,10},{10,12},{12... | collective-permute-start | bytes 98312 | tf_op jit(solution)/shard_map/ppermute | solution.py:388
  285.2 2.8 collective-permute-start.16
  (20 other events, 224.4 us)
Sparse Core Ops, SparseCore 0:
  38.6 34.6 all-gather.3
  75.9 81.6 all-gather.5
where the time goes:
time: 304 us; the launch traced here: 300 us
  waiting for transfers between devices  108 us (36%)
  starting transfers between devices  86.2 us (28%)
  Pallas kernels  53.5 us (18%)
  blocking collectives  22.6 us (7%)
  between operations  14.5 us (5%)
  local copies, waits for them, and re-layouts  12.2 us (4%)
  other arithmetic  3.7 us (1%)
    all_gather x1, waiting for transfers between devices, local(): phi_all = lax.all_gather(orbitals, ('z', 'x'), axis=0, tiled=True)  60.8 us
    ppermute x8, starting transfers between devices, local(): lax.ppermute(part, ('z', 'y'), returns(k))  52.2 us
    ppermute x8, waiting for transfers between devices, local(): lax.ppermute(part, ('z', 'y'), returns(k))  29.7 us
    unnamed x1, blocking collectives  22.6 us
    pallas_call x1, Pallas kernels, local(): pl.pallas_call(assign_kernel, out_shape=jax.ShapeDtypeStruct((17,), jnp.i...  18.4 us
    pallas_call x1, Pallas kernels, local(): pl.pallas_call(pairs_kernel, out_shape=tuple((jax.ShapeDtypeStruct((k, RO...  13 us
    unnamed x49, local copies, waits for them, and re-layouts  9.52 us
    all_gather x1, waiting for transfers between devices, local(): same = lax.all_gather(moved, 'z', axis=0, tiled=True)  9.16 us
  transfers between devices with their start and end apart: 21, of which 9 were waited for; matrix products, arithmetic and copies ran while one was open for 2% of the time, Pallas kernels for 12%

commit v1 on v0

--- a/solution.py
+++ b/solution.py
@@ -166,7 +166,21 @@
 
 
 def pairs_kernel(
-    tasks_ref, left_ref, same_ref, cross_ref, wz_ref, wy_ref, wx_ref, kern_ref, lacc_ref, sacc_ref, cacc_ref, t_ref
+    core_ref,
+    tasks_ref,
+    left_ref,
+    mine_ref,
+    other_ref,
+    wz_ref,
+    wy_ref,
+    wx_ref,
+    kern_ref,
+    lacc_ref,
+    sacc_ref,
+    cacc_ref,
+    t_ref,
+    same_ref,
+    cross_ref,
 ):
     def clear(i, carry):
         rows = pl.ds(pl.multiple_of(i * CHUNK, CHUNK), CHUNK)
@@ -178,6 +192,19 @@
         return carry
 
     lax.fori_loop(0, ROWS // CHUNK, clear, 0)
+    keep = (lax.broadcasted_iota(jnp.int32, (G, 128), 1) < G) == (core_ref[0] == 0)
+
+    def exchange(i, carry):
+        source = pl.ds(pl.multiple_of(i * G, G), G)
+        for j in range(8):
+            mine = mine_ref[j, source].astype(f32)
+            other = other_ref[j, source].astype(f32)
+            rows = pl.ds(pl.multiple_of((j // 2) * 512 + i * G, G), G)
+            same_ref[j % 2, rows] = jnp.where(keep, mine, pltpu.roll(other, G, 1)).astype(bf16)
+            cross_ref[j % 2, rows] = jnp.where(keep, pltpu.roll(mine, G, 1), other).astype(bf16)
+        return carry
+
+    lax.fori_loop(0, 8, exchange, 0)
     low_lanes = lax.broadcasted_iota(jnp.int32, (32, 128), 1) < G
 
     def run(right_ref, racc_ref, task):
@@ -236,7 +263,7 @@
     codes = []
     for p in range(8):
         rows = pl.ds(p * G, G)
-        value = value_of(rows)
+        value = value_of(p)
         largest = jnp.max(jnp.abs(value), axis=0, keepdims=True)
         code = jnp.ceil(jnp.log2(jnp.maximum(largest, 1e-30)) * CODES)
         codes.append(code)
@@ -252,7 +279,7 @@
         def write(rows, value):
             out_ref[k, rows] = value
 
-        quantize_piece(lambda rows: in_ref[k, rows], write)
+        quantize_piece(lambda p: in_ref[k, pl.ds(p * G, G)], write)
 
 
 def quantize_right_kernel(z_ref, first_ref, second_ref, *out_refs):
@@ -262,26 +289,41 @@
         def write(rows, value):
             out_refs[k][rows] = value
 
-        quantize_piece(lambda rows: first_ref[piece, rows] + second_ref[piece, rows], write)
-
-
-def combine_kernel(left_ref, *refs):
-    out_ref = refs[-1]
-
+        def value_of(p):
+            rows = pl.ds(p * G, G)
+            return first_ref[piece, rows] + second_ref[piece, rows]
+
+        quantize_piece(value_of, write)
+
+
+def piece_sum(parts):
     def read(part, rows):
-        ref = left_ref.at[part] if part < NX * NY else refs[part - NX * NY]
-        return ref[rows].astype(jnp.int32).astype(f32)
-
-    count = NX * NY + NZ
-    scales = [
-        jnp.exp2(read(k, pl.ds(512, 16))[:8] * (1.0 / CODES)) * (1.0 / FULL) for k in range(count)
-    ]
+        return part[rows].astype(jnp.int32).astype(f32)
+
+    scales = [jnp.exp2(read(part, pl.ds(512, 16))[:8] * (1.0 / CODES)) * (1.0 / FULL) for part in parts]
+
+    def value_of(p):
+        total = jnp.zeros((G, 128), f32)
+        for part, scale in zip(parts, scales):
+            total = total + read(part, pl.ds(p * G, G)) * scale[p : p + 1]
+        return total
+
+    return value_of
+
+
+def combine_kernel(left_ref, right_ref, out_ref):
+    value_of = piece_sum([left_ref.at[k] for k in range(NX * NY)] + [right_ref])
     for p in range(8):
-        rows = pl.ds(p * G, G)
-        total = jnp.zeros((G, 128), f32)
-        for k in range(count):
-            total = total + read(k, rows) * scales[k][p : p + 1]
-        out_ref[rows] = total
+        out_ref[pl.ds(p * G, G)] = value_of(p)
+
+
+def combine_right_kernel(*refs):
+    value_of = piece_sum(refs[:-1])
+
+    def write(rows, value):
+        refs[-1][rows] = value
+
+    quantize_piece(value_of, write)
 
 
 def quantize_left(lacc):
@@ -308,14 +350,25 @@
     )(z.astype(jnp.int32).reshape(1), first, second)
 
 
-def combine(left_parts, right_parts):
+def combine(left_parts, right_part):
     return pl.pallas_call(
         combine_kernel,
         out_shape=jax.ShapeDtypeStruct((512, 128), f32),
-        in_specs=vmem_specs(1 + len(right_parts)),
+        in_specs=vmem_specs(2),
         out_specs=vmem_specs(1)[0],
         name="combine",
-    )(left_parts, *right_parts)
+    )(left_parts, right_part)
+
+
+def combine_right(parts):
+    return pl.pallas_call(
+        combine_right_kernel,
+        out_shape=jax.ShapeDtypeStruct((528, 128), jnp.int16),
+        in_specs=vmem_specs(len(parts)),
+        out_specs=vmem_specs(1)[0],
+        cost_estimate=pl.CostEstimate(flops=0, bytes_accessed=6 * 1000 * 1000, transcendentals=0),
+        name="combine_right",
+    )(*parts)
 
 
 def overlap_kernel(core_ref, own_ref, other_ref, phi_ref, x_ref, out_ref, same_ref, cross_ref):
@@ -391,29 +444,16 @@
     return (value + far) + (near + back)
 
 
-def returns(k):
-    pairs = []
-    for z in range(NZ):
-        for y in range(NY):
-            q = (z + k) % NZ
-            pairs.append((z * NY + y, (2 * y + q // NY) * NY + q % NY))
-    return pairs
-
-
 def local(orbitals, pair_table):
     z, x, y, core = (lax.axis_index(a) for a in ("z", "x", "y", "core"))
     mine = orbitals[0]
     live = pair_table[:, 0] >= 0
     code = jnp.where(live, pair_table[:, 0] + 32 * pair_table[:, 1] + 1024 * pair_table[:, 2], -1)
+    z_couples = lax.all_gather(orbitals, "z", axis=0, tiled=True)
     own = lane_exchange(mine, core)
-    phi_all = lax.all_gather(orbitals, ("z", "x"), axis=0, tiled=True)
-    moved = lax.ppermute(own, ("z", "y"), moves())
-    own, code = lax.optimization_barrier((own, code))
-    codes = lax.all_gather(code[None], ("z", "x"), axis=0, tiled=True)
-    moved, own, codes = lax.optimization_barrier((moved, own, codes))
-    same = lax.all_gather(moved, "z", axis=0, tiled=True)
     spread = jnp.broadcast_to(own[None], (NX * NY,) + own.shape)
     left = lax.all_to_all(spread, ("x", "y"), split_axis=0, concat_axis=0, tiled=True)
+    codes = lax.all_gather(code[None], ("z", "x"), axis=0, tiled=True)
 
     me = (z * 16 + x * 4 + y).astype(jnp.int32).reshape(1)
     tasks = pl.pallas_call(
@@ -425,30 +465,34 @@
         cost_estimate=pl.CostEstimate(flops=0, bytes_accessed=60 * 1000 * 1000, transcendentals=0),
         name="assign",
     )(me, codes)
-    same, tasks = lax.optimization_barrier((same, tasks))
-    cross = lax.ppermute(same, "core", ring(2, 1))
+    z_couples, tasks = lax.optimization_barrier((z_couples, tasks))
+    phi_all = lax.all_gather(z_couples, "x", axis=0, tiled=True)
+    y_couples, left = lax.optimization_barrier((z_couples, left))
+    right = lax.all_to_all(y_couples, "y", split_axis=0, concat_axis=0, tiled=True)
+    right_other = lax.ppermute(right, "core", ring(2, 1))
+    core_id = core.astype(jnp.int32).reshape(1)
 
     w_depth, w_rows, w_planes = (jnp.asarray(w) for w in weights())
     lacc, sacc, cacc = pl.pallas_call(
         pairs_kernel,
         out_shape=tuple(jax.ShapeDtypeStruct((k, ROWS, 128), f32) for k in (4, 2, 2)),
-        in_specs=smem_specs(1) + vmem_specs(7),
+        in_specs=smem_specs(2) + vmem_specs(7),
         out_specs=tuple(vmem_specs(3)),
-        scratch_shapes=[pltpu.VMEM((ROWS, 128), f32)],
+        scratch_shapes=[pltpu.VMEM((ROWS, 128), f32)] + [pltpu.VMEM((2, ROWS, 128), bf16)] * 2,
         compiler_params=pltpu.CompilerParams(vmem_limit_bytes=48 * 1024 * 1024),
-        cost_estimate=pl.CostEstimate(flops=0, bytes_accessed=180 * 1000 * 1000, transcendentals=0),
+        cost_estimate=pl.CostEstimate(flops=0, bytes_accessed=60 * 1000 * 1000, transcendentals=0),
         name="pairs",
     )(
+        core_id,
         tasks,
         left.reshape(4, ROWS, 128),
-        same.reshape(2, ROWS, 128),
-        cross.reshape(2, ROWS, 128),
+        right.reshape(8, 512, 128),
+        right_other.reshape(8, 512, 128),
         w_depth,
         w_rows,
         w_planes,
         coulomb(),
     )
-    lacc, sacc, cacc, phi_all = lax.optimization_barrier((lacc, sacc, cacc, phi_all))
 
     other = lax.ppermute(cacc, "core", ring(2, 1))
     right_parts = quantize_right(z, sacc.reshape(NZ, 512, 128), other.reshape(NZ, 512, 128))
@@ -456,9 +500,10 @@
     left_parts, *right_parts = lax.optimization_barrier((left_parts, *right_parts))
     left_parts = lax.all_to_all(left_parts, ("x", "y"), split_axis=0, concat_axis=0, tiled=True)
     right_parts = [
-        lax.ppermute(part, ("z", "y"), returns(k)) for k, part in enumerate(right_parts)
+        lax.ppermute(part, "z", ring(NZ, k)) if k else part for k, part in enumerate(right_parts)
     ]
-    action = combine(left_parts, right_parts)
+    from_right = lax.ppermute(combine_right(right_parts), ("z", "y"), [(d, s) for s, d in moves()])
+    action = combine(left_parts, from_right)
     action_other = lax.ppermute(action, "core", ring(2, 1))
 
     phi_rows = phi_all.reshape(COUPLES, 512, 128)
@@ -472,7 +517,7 @@
         out_specs=tuple(vmem_specs(2)),
         scratch_shapes=[pltpu.VMEM((COUPLES, 8, 128), f32)] * 2,
         name="overlap",
-    )(core.astype(jnp.int32).reshape(1), action, action_other, phi_rows)
+    )(core_id, action, action_other, phi_rows)
     out = pl.pallas_call(
         project_kernel,
         out_shape=jax.ShapeDtypeStruct((512, 128), f32),

time: 304 us -> 228 us (0.75)
  waiting for transfers between devices: 108 us -> 36.8 us
  starting transfers between devices: 86.2 us -> 62.6 us
  blocking collectives: 22.6 us -> 40.8 us
  Pallas kernels: 53.5 us -> 59.1 us
    all_gather x2, waiting for transfers between devices: 70 us -> 0.02 us  [the longest x1 0.02 us: local(): z_couples = lax.all_gather(orbitals, 'z', axis=0, tiled=True)]
    ppermute x10 -> x9, starting transfers between devices: 57.5 us -> 21.6 us  [the longest x7 13.7 us: local(): lax.ppermute(part, 'z', ring(NZ, k))]
    unnamed x1, blocking collectives: 22.6 us -> 40.8 us
    ppermute x1, starting transfers between devices: 6.85 us -> 19.7 us  [sum_over_slab(): far = lax.ppermute(value, 'y', ring(NY, 2))]
    ppermute x10 -> x9, waiting for transfers between devices: 31.7 us -> 21.5 us  [the longest x7 19.7 us: local(): lax.ppermute(part, 'z', ring(NZ, k))]
    all_to_all x0 -> x1, waiting for transfers between devices: none -> 9.68 us  [local(): lax.all_to_all(y_couples, 'y', split_axis=0, concat_axis=0, tiled=True)]
    pallas_call x1, Pallas kernels: 13 us -> 16.9 us  [local(): pl.pallas_call(pairs_kernel, out_shape=tuple((jax.ShapeDtypeStruct((k, RO...]
    all_to_all x0 -> x1, starting transfers between devices: none -> 3.66 us  [local(): lax.all_to_all(y_couples, 'y', split_axis=0, concat_axis=0, tiled=True)]
  transfers between devices with their start and end apart: 21 -> 21, of which waited for: 9 -> 10; matrix products, arithmetic and copies ran while one was open for 2% -> 1% of each run, Pallas kernels for 12% -> 22%
where the time goes in v1:
time: 228 us; the launch traced here: 226 us
  starting transfers between devices  62.6 us (27%)
  Pallas kernels  59.1 us (26%)
  blocking collectives  40.8 us (18%)
  waiting for transfers between devices  36.8 us (16%)
  between operations  14.4 us (6%)
  local copies, waits for them, and re-layouts  9.55 us (4%)
  other arithmetic  3.02 us (1%)
    unnamed x1, blocking collectives  40.8 us
    ppermute x1, starting transfers between devices, sum_over_slab(): far = lax.ppermute(value, 'y', ring(NY, 2))  19.7 us
    ppermute x7, waiting for transfers between devices, local(): lax.ppermute(part, 'z', ring(NZ, k))  19.7 us
    pallas_call x1, Pallas kernels, local(): pl.pallas_call(assign_kernel, out_shape=jax.ShapeDtypeStruct((17,), jnp.i...  18.4 us
    pallas_call x1, Pallas kernels, local(): pl.pallas_call(pairs_kernel, out_shape=tuple((jax.ShapeDtypeStruct((k, RO...  16.9 us
    ppermute x7, starting transfers between devices, local(): lax.ppermute(part, 'z', ring(NZ, k))  13.7 us
    all_to_all x1, waiting for transfers between devices, local(): lax.all_to_all(y_couples, 'y', split_axis=0, concat_axis=0, tiled=True)  9.68 us
    unnamed x50, local copies, waits for them, and re-layouts  6.87 us
  transfers between devices with their start and end apart: 21, of which 10 were waited for; matrix products, arithmetic and copies ran while one was open for 1% of the time, Pallas kernels for 22%

profile of v1, /device:TPU:1, one launch (start us, length us, event | category | flops | bytes accessed | tf_op | source)
XLA Modules:
  0.0 226.2 jit_solution(10307683842587489470)
XLA Ops:
  6.5 3.2 %collective-permute-start = (bf16[8,64,128]{2,1,0:T(8,128)(2,1)}, bf16[8,64,128]{2,1,0:T(8,128)(2,1)S(1)}, u32[]{:S(2)}, u32[]{:S(2)}) collective-permute-start(bf16[8,64,128]{2,1,0:T(8,128)(2,1)} %bitcast.31), channel_id=1, source_target_pairs={{0,1},{1,0},{2,3},{3,2},{4,5},{5,4},{6,7},{7,6},{8,9},{9,8},{10,11... | collective-permute-start | bytes 393224 | tf_op jit(solution)/shard_map/ppermute | solution.py:426
  14.0 5.2 %all-to-all-start = ((bf16[16,8,64,128]{3,2,1,0:T(8,128)(2,1)}), bf16[16,8,64,128]{3,2,1,0:T(8,128)(2,1)S(1)}, u32[]{:S(2)}, u32[]{:S(2)}) async-start(bf16[16,8,64,128]{3,2,1,0:T(8,128)(2,1)} %broadcast_in_dim.20), calls=%async_computation | async-start | bytes 4194304 | tf_op jit(solution)/shard_map/all_to_all | solution.py:455
  21.3 40.8 %all-reduce = s32[1024]{0:T(1024)S(1)} all-reduce(s32[1024]{0:T(1024)S(1)} %fusion.21), channel_id=2, replica_groups=mesh['z'=8,'x'=4,'y'=4,'core'=2] {'z','x'}, use_global_device_ids=true, to_apply=%add | all-reduce | flops 1024 | bytes 8192
  62.8 18.4 %assign.1.tasks_ref = s32[17]{0:T(128)} custom-call(s32[1]{0:T(128)} %bitcast.1.me_ref, s32[32,32]{1,0:T(8,128)} %reshape.101.code_ref), custom_call_target="tpu_custom_call" | custom-call | bytes 60000000 | tf_op jit(solution)/shard_map/assign/pallas_call | solution.py:459
  81.3 3.7 %all-to-all-start.1 = ((bf16[8,8,64,128]{3,2,1,0:T(8,128)(2,1)}), bf16[8,8,64,128]{3,2,1,0:T(8,128)(2,1)S(1)}, u32[]{:S(2)}, u32[]{:S(2)}) async-start(bf16[8,8,64,128]{3,2,1,0:T(8,128)(2,1)} %all-gather.4.cloned.1.call-done), calls=%async_computation.1 | async-start | bytes 2097152 | tf_op jit(solution)/shard_map/all_to_all | solution.py:471
  85.0 9.7 %all-to-all-done.1 = bf16[8,8,64,128]{3,2,1,0:T(8,128)(2,1)S(1)} async-done(((bf16[8,8,64,128]{3,2,1,0:T(8,128)(2,1)}), bf16[8,8,64,128]{3,2,1,0:T(8,128)(2,1)S(1)}, u32[]{:S(2)}, u32[]{:S(2)}) %all-to-all-start.1) | async-done | bytes 1048608 | tf_op jit(solution)/shard_map/all_to_all | solution.py:471
  94.7 6.3 %collective-permute-start.1 = (bf16[8,8,64,128]{3,2,1,0:T(8,128)(2,1)S(1)}, bf16[8,8,64,128]{3,2,1,0:T(8,128)(2,1)S(1)}, u32[]{:S(2)}, u32[]{:S(2)}) collective-permute-start(bf16[8,8,64,128]{3,2,1,0:T(8,128)(2,1)S(1)} %all-to-all-done.1), channel_id=1, source_target_pairs={{0,1},{1,0},{2,3},{3,2},{4,5},{5,4},{6,7},{7,6},{8,9},{9,8},{10,11... | collective-permute-start | bytes 3145736 | tf_op jit(solution)/shard_map/ppermute | solution.py:472
  103.4 16.9 %pairs.1 = (f32[4,2048,128]{2,1,0:T(8,128)}, f32[2,2048,128]{2,1,0:T(8,128)S(1)}, f32[2,2048,128]{2,1,0:T(8,128)}) custom-call(s32[1]{0:T(128)} %bitcast.core_ref, s32[17]{0:T(128)S(1)} %copy-done.4, bf16[4,2048,128]{2,1,0:T(8,128)(2,1)} %bitcast.28, bf16[8,512,128]{2,1,0:T(8,128)(2,1)S(1)} %bitcast.23, bf16[8,512,128]{2,1,0:T(8,128)(2,1)S(1)} %bitcast.25, ...), custom_call_target="tpu_custom_call" | custom-call | bytes 60000000 | tf_op jit(solution)/shard_map/pairs/pallas_call | solution.py:476
  122.1 4.5 %quantize_left.1 = s16[16,528,128]{2,1,0:T(8,128)(2,1)} custom-call(f32[16,512,128]{2,1,0:T(8,128)} %bitcast.29), custom_call_target="tpu_custom_call" | custom-call | bytes 10000000 | tf_op jit(solution)/shard_map/quantize_left/pallas_call | solution.py:331
  128.0 3.6 %quantize_right.1 = (s16[528,128]{1,0:T(8,128)(2,1)}, s16[528,128]{1,0:T(8,128)(2,1)}, s16[528,128]{1,0:T(8,128)(2,1)}, s16[528,128]{1,0:T(8,128)(2,1)}, s16[528...) custom-call(s32[1]{0:T(128)} %bitcast.12.z_ref, ...), custom_call_target="tpu_custom_call" | custom-call | bytes 8000000 | tf_op jit(solution)/shard_map/quantize_right/pallas_call | solution.py:343
  131.6 4.0 %all-to-all-start.2 = ((s16[16,528,128]{2,1,0:T(8,128)(2,1)}), s16[16,528,128]{2,1,0:T(8,128)(2,1)S(1)}, u32[]{:S(2)}, u32[]{:S(2)}) async-start(s16[16,528,128]{2,1,0:T(8,128)(2,1)} %quantize_left.1), calls=%async_computation.2 | async-start | bytes 4325376 | tf_op jit(solution)/shard_map/all_to_all | solution.py:501
  135.6 2.0 collective-permute-start.3
  137.6 2.4 %collective-permute-start.4 = (s16[528,128]{1,0:T(8,128)(2,1)S(1)}, s16[528,128]{1,0:T(8,128)(2,1)S(1)}, u32[]{:S(2)}, u32[]{:S(2)}) collective-permute-start(s16[528,128]{1,0:T(8,128)(2,1)S(1)} %copy-done.21), channel_id=1, source_target_pairs={{0,64},{32,96},{64,128},{96,160},{128,192},{160,224},{192,0},{224,... | collective-permute-start | bytes 405512 | tf_op jit(solution)/shard_map/ppermute | solution.py:503
  140.7 4.9 %collective-permute-start.6 = (s16[528,128]{1,0:T(8,128)(2,1)}, s16[528,128]{1,0:T(8,128)(2,1)S(1)}, u32[]{:S(2)}, u32[]{:S(2)}) collective-permute-start(s16[528,128]{1,0:T(8,128)(2,1)} %get-tuple-element.51), channel_id=1, source_target_pairs={{0,128},{32,160},{64,192},{96,224},{128,0},{160,32},{192,64},{224,... | collective-permute-start | bytes 405512 | tf_op jit(solution)/shard_map/ppermute | solution.py:503
  145.6 3.1 %collective-permute-start.8 = (s16[528,128]{1,0:T(8,128)(2,1)S(1)}, s16[528,128]{1,0:T(8,128)(2,1)S(1)}, u32[]{:S(2)}, u32[]{:S(2)}) collective-permute-start(s16[528,128]{1,0:T(8,128)(2,1)S(1)} %copy-done.19), channel_id=1, source_target_pairs={{0,192},{32,224},{64,0},{96,32},{128,64},{160,96},{192,128},{224,1... | collective-permute-start | bytes 405512 | tf_op jit(solution)/shard_map/ppermute | solution.py:503
  149.3 3.7 %collective-permute-done.5.refs_3_ = s16[528,128]{1,0:T(8,128)(2,1)S(1)} collective-permute-done((s16[528,128]{1,0:T(8,128)(2,1)}, s16[528,128]{1,0:T(8,128)(2,1)S(1)}, u32[]{:S(2)}, u32[]{:S(2)}) %collective-permute-start.5) | collective-permute-done | bytes 135200 | tf_op jit(solution)/shard_map/ppermute | solution.py:503
  153.1 9.4 %collective-permute-done.6.refs_4_ = s16[528,128]{1,0:T(8,128)(2,1)S(1)} collective-permute-done((s16[528,128]{1,0:T(8,128)(2,1)}, s16[528,128]{1,0:T(8,128)(2,1)S(1)}, u32[]{:S(2)}, u32[]{:S(2)}) %collective-permute-start.6) | collective-permute-done | bytes 135200 | tf_op jit(solution)/shard_map/ppermute | solution.py:503
  162.5 5.2 %collective-permute-done.8.refs_6_ = s16[528,128]{1,0:T(8,128)(2,1)S(1)} collective-permute-done((s16[528,128]{1,0:T(8,128)(2,1)S(1)}, s16[528,128]{1,0:T(8,128)(2,1)S(1)}, u32[]{:S(2)}, u32[]{:S(2)}) %collective-permute-start.8) | collective-permute-done | bytes 135200 | tf_op jit(solution)/shard_map/ppermute | solution.py:503
  169.7 2.3 %combine_right.1 = s16[528,128]{1,0:T(8,128)(2,1)} custom-call(s16[528,128]{1,0:T(8,128)(2,1)} %get-tuple-element.47.refs_0_, s16[528,128]{1,0:T(8,128)(2,1)} %copy-done.9, s16[528,128]{1,0:T(8,128)(2,1)} %copy-done.10, s16[528,128]{1,0:T(8,128)(2,1)} %copy-done.11, s16[528,128]{1,0:T(8,128)(2,1)} %copy-done.12, s16[528,128]{1,0:T(8,128)(2,1)} %copy-done.13, ...), custom_call_target="tpu_custom_call" | custom-call | bytes 6000000 | tf_op jit(solution)/shard_map/combine_right/pallas_call | solution.py:364
  175.7 2.9 %combine.1.own_ref = f32[512,128]{1,0:T(8,128)} custom-call(s16[16,528,128]{2,1,0:T(8,128)(2,1)} %copy-done.5, s16[528,128]{1,0:T(8,128)(2,1)} %copy-done.16), custom_call_target="tpu_custom_call" | custom-call | tf_op jit(solution)/shard_map/combine/pallas_call | solution.py:354
  182.4 5.6 %overlap.1 = (f32[512,128]{1,0:T(8,128)}, f32[64,128]{1,0:T(8,128)}) custom-call(s32[1]{0:T(128)} %bitcast.core_ref, f32[512,128]{1,0:T(8,128)} %combine.1.own_ref, f32[512,128]{1,0:T(8,128)} %copy-done.8, bf16[32,512,128]{2,1,0:T(8,128)(2,1)} %bitcast.26), custom_call_target="tpu_custom_call" | custom-call | tf_op jit(solution)/shard_map/overlap/pallas_call | solution.py:510
  190.2 19.7 %collective-permute-start.13 = (f32[64,128]{1,0:T(8,128)S(1)}, f32[64,128]{1,0:T(8,128)S(1)}, u32[]{:S(2)}, u32[]{:S(2)}) collective-permute-start(f32[64,128]{1,0:T(8,128)S(1)} %add.89), channel_id=1, source_target_pairs={{0,4},{2,6},{4,0},{6,2},{1,5},{3,7},{5,1},{7,3},{8,12},{10,14},{12... | collective-permute-start | bytes 98312 | tf_op jit(solution)/shard_map/ppermute | solution.py:443
  209.9 2.7 %collective-permute-start.15 = (f32[64,128]{1,0:T(8,128)S(1)}, f32[64,128]{1,0:T(8,128)S(1)}, u32[]{:S(2)}, u32[]{:S(2)}) collective-permute-start(f32[64,128]{1,0:T(8,128)S(1)} %add.89), channel_id=1, source_target_pairs={{0,6},{2,0},{4,2},{6,4},{1,7},{3,1},{5,3},{7,5},{8,14},{10,8},{12,... | collective-permute-start | bytes 98312 | tf_op jit(solution)/shard_map/ppermute | solution.py:442
  214.5 4.8 %project.1 = f32[512,128]{1,0:T(8,128)} custom-call(f32[512,128]{1,0:T(8,128)} %get-tuple-element.55.x_ref, bf16[32,512,128]{2,1,0:T(8,128)(2,1)} %bitcast.27, f32[64,128]{1,0:T(8,128)} %add_add_fusion.over_ref), custom_call_target="tpu_custom_call" | custom-call | tf_op jit(solution)/shard_map/project/pallas_call | solution.py:521
  (97 shorter events, 26.8 us)
Async XLA Ops:
  6.5 4.4 %collective-permute-start = (bf16[8,64,128]{2,1,0:T(8,128)(2,1)}, bf16[8,64,128]{2,1,0:T(8,128)(2,1)S(1)}, u32[]{:S(2)}, u32[]{:S(2)}) collective-permute-start(bf16[8,64,128]{2,1,0:T(8,128)(2,1)} %bitcast.31), channel_id=1, source_target_pairs={{0,1},{1,0},{2,3},{3,2},{4,5},{5,4},{6,7},{7,6},{8,9},{9,8},{10,11... | collective-permute-start | bytes 393224 | tf_op jit(solution)/shard_map/ppermute | solution.py:426
  14.0 67.3 %all-to-all-start = ((bf16[16,8,64,128]{3,2,1,0:T(8,128)(2,1)}), bf16[16,8,64,128]{3,2,1,0:T(8,128)(2,1)S(1)}, u32[]{:S(2)}, u32[]{:S(2)}) async-start(bf16[16,8,64,128]{3,2,1,0:T(8,128)(2,1)} %broadcast_in_dim.20), calls=%async_computation | async-start | bytes 4194304 | tf_op jit(solution)/shard_map/all_to_all | solution.py:455
  19.2 62.1 %all-gather.4.cloned.1.call-start = ((), (), s32[]{:S(2)}) async-start(), calls=%async_computation.3 | async-start | bytes 1179648 | tf_op jit(solution)/shard_map/all_gather | solution.py:452
  19.9 160.4 %all-gather.6.cloned.1.call-start = ((), (), s32[]{:S(2)}) async-start(), calls=%async_computation.4 | async-start | bytes 5242880 | tf_op jit(solution)/shard_map/all_gather | solution.py:469
  81.2 22.1 %copy-start.1 = (bf16[256,256]{1,0:T(8,128)(2,1)S(1)}, bf16[256,256]{1,0:T(8,128)(2,1)}, u32[]{:S(2)}) copy-start(bf16[256,256]{1,0:T(8,128)(2,1)} %constant.126.clone.wz_ref) | copy-start | bytes 393220
  81.2 22.1 %copy-start.2 = (bf16[256,256]{1,0:T(8,128)(2,1)S(1)}, bf16[256,256]{1,0:T(8,128)(2,1)}, u32[]{:S(2)}) copy-start(bf16[256,256]{1,0:T(8,128)(2,1)} %constant.127.clone.wy_ref) | copy-start | bytes 393220
  81.3 13.4 %all-to-all-start.1 = ((bf16[8,8,64,128]{3,2,1,0:T(8,128)(2,1)}), bf16[8,8,64,128]{3,2,1,0:T(8,128)(2,1)S(1)}, u32[]{:S(2)}, u32[]{:S(2)}) async-start(bf16[8,8,64,128]{3,2,1,0:T(8,128)(2,1)} %all-gather.4.cloned.1.call-done), calls=%async_computation.1 | async-start | bytes 2097152 | tf_op jit(solution)/shard_map/all_to_all | solution.py:471
  94.7 8.6 %collective-permute-start.1 = (bf16[8,8,64,128]{3,2,1,0:T(8,128)(2,1)S(1)}, bf16[8,8,64,128]{3,2,1,0:T(8,128)(2,1)S(1)}, u32[]{:S(2)}, u32[]{:S(2)}) collective-permute-start(bf16[8,8,64,128]{3,2,1,0:T(8,128)(2,1)S(1)} %all-to-all-done.1), channel_id=1, source_target_pairs={{0,1},{1,0},{2,3},{3,2},{4,5},{5,4},{6,7},{7,6},{8,9},{9,8},{10,11... | collective-permute-start | bytes 3145736 | tf_op jit(solution)/shard_map/ppermute | solution.py:472
  121.7 5.0 %collective-permute-start.2 = (f32[2,2048,128]{2,1,0:T(8,128)}, f32[2,2048,128]{2,1,0:T(8,128)S(1)}, u32[]{:S(2)}, u32[]{:S(2)}) collective-permute-start(f32[2,2048,128]{2,1,0:T(8,128)} %get-tuple-element.37), channel_id=1, source_target_pairs={{0,1},{1,0},{2,3},{3,2},{4,5},{5,4},{6,7},{7,6},{8,9},{9,8},{10,11... | collective-permute-start | bytes 6291464 | tf_op jit(solution)/shard_map/ppermute | solution.py:497
  131.6 42.0 %all-to-all-start.2 = ((s16[16,528,128]{2,1,0:T(8,128)(2,1)}), s16[16,528,128]{2,1,0:T(8,128)(2,1)S(1)}, u32[]{:S(2)}, u32[]{:S(2)}) async-start(s16[16,528,128]{2,1,0:T(8,128)(2,1)} %quantize_left.1), calls=%async_computation.2 | async-start | bytes 4325376 | tf_op jit(solution)/shard_map/all_to_all | solution.py:501
  135.6 10.0 %collective-permute-start.3 = (s16[528,128]{1,0:T(8,128)(2,1)S(1)}, s16[528,128]{1,0:T(8,128)(2,1)S(1)}, u32[]{:S(2)}, u32[]{:S(2)}) collective-permute-start(s16[528,128]{1,0:T(8,128)(2,1)S(1)} %copy-done.22), channel_id=1, source_target_pairs={{0,32},{32,64},{64,96},{96,128},{128,160},{160,192},{192,224},{224... | collective-permute-start | bytes 405512 | tf_op jit(solution)/shard_map/ppermute | solution.py:503
  137.6 11.2 %collective-permute-start.4 = (s16[528,128]{1,0:T(8,128)(2,1)S(1)}, s16[528,128]{1,0:T(8,128)(2,1)S(1)}, u32[]{:S(2)}, u32[]{:S(2)}) collective-permute-start(s16[528,128]{1,0:T(8,128)(2,1)S(1)} %copy-done.21), channel_id=1, source_target_pairs={{0,64},{32,96},{64,128},{96,160},{128,192},{160,224},{192,0},{224,... | collective-permute-start | bytes 405512 | tf_op jit(solution)/shard_map/ppermute | solution.py:503
  140.0 13.0 %collective-permute-start.5 = (s16[528,128]{1,0:T(8,128)(2,1)}, s16[528,128]{1,0:T(8,128)(2,1)S(1)}, u32[]{:S(2)}, u32[]{:S(2)}) collective-permute-start(s16[528,128]{1,0:T(8,128)(2,1)} %get-tuple-element.50), channel_id=1, source_target_pairs={{0,96},{32,128},{64,160},{96,192},{128,224},{160,0},{192,32},{224,... | collective-permute-start | bytes 405512 | tf_op jit(solution)/shard_map/ppermute | solution.py:503
  140.7 21.8 %collective-permute-start.6 = (s16[528,128]{1,0:T(8,128)(2,1)}, s16[528,128]{1,0:T(8,128)(2,1)S(1)}, u32[]{:S(2)}, u32[]{:S(2)}) collective-permute-start(s16[528,128]{1,0:T(8,128)(2,1)} %get-tuple-element.51), channel_id=1, source_target_pairs={{0,128},{32,160},{64,192},{96,224},{128,0},{160,32},{192,64},{224,... | collective-permute-start | bytes 405512 | tf_op jit(solution)/shard_map/ppermute | solution.py:503
  145.6 16.9 %collective-permute-start.7 = (s16[528,128]{1,0:T(8,128)(2,1)S(1)}, s16[528,128]{1,0:T(8,128)(2,1)S(1)}, u32[]{:S(2)}, u32[]{:S(2)}) collective-permute-start(s16[528,128]{1,0:T(8,128)(2,1)S(1)} %copy-done.20), channel_id=1, source_target_pairs={{0,160},{32,192},{64,224},{96,0},{128,32},{160,64},{192,96},{224,1... | collective-permute-start | bytes 405512 | tf_op jit(solution)/shard_map/ppermute | solution.py:503
  145.6 23.4 %copy-start.9 = (s16[528,128]{1,0:T(8,128)(2,1)}, s16[528,128]{1,0:T(8,128)(2,1)S(1)}, u32[]{:S(2)}) copy-start(s16[528,128]{1,0:T(8,128)(2,1)S(1)} %collective-permute-done.3.refs_1_) | copy-start | bytes 405508
  145.6 22.1 %collective-permute-start.8 = (s16[528,128]{1,0:T(8,128)(2,1)S(1)}, s16[528,128]{1,0:T(8,128)(2,1)S(1)}, u32[]{:S(2)}, u32[]{:S(2)}) collective-permute-start(s16[528,128]{1,0:T(8,128)(2,1)S(1)} %copy-done.19), channel_id=1, source_target_pairs={{0,192},{32,224},{64,0},{96,32},{128,64},{160,96},{192,128},{224,1... | collective-permute-start | bytes 405512 | tf_op jit(solution)/shard_map/ppermute | solution.py:503
  148.8 20.2 %collective-permute-start.9 = (s16[528,128]{1,0:T(8,128)(2,1)S(1)}, s16[528,128]{1,0:T(8,128)(2,1)S(1)}, u32[]{:S(2)}, u32[]{:S(2)}) collective-permute-start(s16[528,128]{1,0:T(8,128)(2,1)S(1)} %copy-done.18), channel_id=1, source_target_pairs={{0,224},{32,0},{64,32},{96,64},{128,96},{160,128},{192,160},{224,1... | collective-permute-start | bytes 405512 | tf_op jit(solution)/shard_map/ppermute | solution.py:503
  172.1 1.6 collective-permute-start.10
  178.6 3.1 %collective-permute-start.11 = (f32[512,128]{1,0:T(8,128)}, f32[512,128]{1,0:T(8,128)S(1)}, u32[]{:S(2)}, u32[]{:S(2)}) collective-permute-start(f32[512,128]{1,0:T(8,128)} %combine.1.own_ref), channel_id=1, source_target_pairs={{0,1},{1,0},{2,3},{3,2},{4,5},{5,4},{6,7},{7,6},{8,9},{9,8},{10,11... | collective-permute-start | bytes 786440 | tf_op jit(solution)/shard_map/ppermute | solution.py:507
  188.0 1.4 collective-permute-start.12
  190.2 22.4 %collective-permute-start.13 = (f32[64,128]{1,0:T(8,128)S(1)}, f32[64,128]{1,0:T(8,128)S(1)}, u32[]{:S(2)}, u32[]{:S(2)}) collective-permute-start(f32[64,128]{1,0:T(8,128)S(1)} %add.89), channel_id=1, source_target_pairs={{0,4},{2,6},{4,0},{6,2},{1,5},{3,7},{5,1},{7,3},{8,12},{10,14},{12... | collective-permute-start | bytes 98312 | tf_op jit(solution)/shard_map/ppermute | solution.py:443
  209.9 4.0 %collective-permute-start.14 = (f32[64,128]{1,0:T(8,128)S(1)}, f32[64,128]{1,0:T(8,128)S(1)}, u32[]{:S(2)}, u32[]{:S(2)}) collective-permute-start(f32[64,128]{1,0:T(8,128)S(1)} %add.89), channel_id=1, source_target_pairs={{0,2},{2,4},{4,6},{6,0},{1,3},{3,5},{5,7},{7,1},{8,10},{10,12},{12... | collective-permute-start | bytes 98312 | tf_op jit(solution)/shard_map/ppermute | solution.py:441
  209.9 4.0 %collective-permute-start.15 = (f32[64,128]{1,0:T(8,128)S(1)}, f32[64,128]{1,0:T(8,128)S(1)}, u32[]{:S(2)}, u32[]{:S(2)}) collective-permute-start(f32[64,128]{1,0:T(8,128)S(1)} %add.89), channel_id=1, source_target_pairs={{0,6},{2,0},{4,2},{6,4},{1,7},{3,1},{5,3},{7,5},{8,14},{10,8},{12,... | collective-permute-start | bytes 98312 | tf_op jit(solution)/shard_map/ppermute | solution.py:442
  (21 other events, 191.4 us)
Sparse Core Ops, SparseCore 0:
  21.8 37.5 all-gather.3
  81.4 49.4 all-gather.5

commit v2 on v1

--- a/solution.py
+++ b/solution.py
@@ -66,48 +66,43 @@
     return jnp.where(squared > 0, -exchange_fraction / safe, 0.0)
 
 
-def assign_kernel(me_ref, code_ref, out_ref, load_ref):
+def packed_slots(left_id, right_id):
+    m = left_id.astype(jnp.int32)
+    rest = right_id.astype(jnp.int32)
+    n, flip = rest & 31, rest >> 5
+    mz, mx, nz, nx = m >> 2, m & 3, n >> 2, n & 3
+    shared = 8 * flip + 16 * (m == n).astype(jnp.int32)
+    first = (mz * 16 + nx * 4 + (nz >> 1)) | (mx + 4 * (nz & 1) + shared) << 7
+    second = (nz * 16 + mx * 4 + (mz >> 1)) | (nx + 4 * (mz & 1) + shared) << 7
+    return jnp.where(m >= 0, first | second << 16, -1)
+
+
+def assign_kernel(me_ref, slots_ref, out_ref, load_ref):
     me = me_ref[0]
 
     def clear(i, carry):
         load_ref[i] = 0
         return carry
 
-    lax.fori_loop(0, NZ * NX * NY, clear, 0)
-    for i in range(17):
-        out_ref[i] = 0
+    lax.fori_loop(0, NZ * NX * NY, clear, 0, unroll=8)
 
     def one_block(b, count):
-        def live(state):
-            s, _ = state
-            return (s < 32) & (code_ref[b, jnp.minimum(s, 31)] >= 0)
+        row = ((me_ref[1] - (b & 3)) & 3) * NZ + (b >> 2)
 
         def step(state):
-            s, cnt = state
-            code = code_ref[b, s]
-            m = code & 31
-            n = (code >> 5) & 31
-            flip = code >> 10
-            mz, mx, nz, nx = m >> 2, m & 3, n >> 2, n & 3
-            first = mz * 16 + nx * 4 + (nz >> 1)
-            second = nz * 16 + mx * 4 + (mz >> 1)
+            s, slot, cnt = state
+            first = slot & 127
+            second = (slot >> 16) & 127
             load_a = load_ref[first]
             load_b = load_ref[second]
             use_a = load_a <= load_b
             chip = jnp.where(use_a, first, second)
-            load_ref[chip] = jnp.where(use_a, load_a, load_b) + 1
-            task_a = mx + 4 * (nz & 1)
-            task_b = nx + 4 * (mz & 1)
-            task = jnp.where(use_a, task_a, task_b) + 8 * flip + 16 * (m == n).astype(jnp.int32)
-            mine = chip == me
-
-            @pl.when(mine)
-            def _():
-                out_ref[1 + cnt] = task
-
-            return s + 1, cnt + mine.astype(jnp.int32)
-
-        return lax.while_loop(live, step, (0, count))[1]
+            load_ref[chip] = jnp.minimum(load_a, load_b) + 1
+            out_ref[1 + cnt] = jnp.where(use_a, slot >> 7, slot >> 23) & 31
+            slot = jnp.where(s < 31, slots_ref[row, jnp.minimum(s + 1, 31)], -1)
+            return s + 1, slot, cnt + (chip == me).astype(jnp.int32)
+
+        return lax.while_loop(lambda state: state[1] >= 0, step, (0, slots_ref[row, 0], count))[2]
 
     out_ref[0] = lax.fori_loop(0, 32, one_block, 0)
 
@@ -163,100 +158,6 @@
         block = jnp.swapaxes(jnp.concatenate(rows, axis=0), 0, 1)
         for r in range(32):
             t_ref[pl.ds(pl.multiple_of(r * G + first + base, 8), 8)] = block[r]
-
-
-def pairs_kernel(
-    core_ref,
-    tasks_ref,
-    left_ref,
-    mine_ref,
-    other_ref,
-    wz_ref,
-    wy_ref,
-    wx_ref,
-    kern_ref,
-    lacc_ref,
-    sacc_ref,
-    cacc_ref,
-    t_ref,
-    same_ref,
-    cross_ref,
-):
-    def clear(i, carry):
-        rows = pl.ds(pl.multiple_of(i * CHUNK, CHUNK), CHUNK)
-        for k in range(4):
-            lacc_ref[k, rows] = jnp.zeros((CHUNK, 128), f32)
-        for k in range(2):
-            sacc_ref[k, rows] = jnp.zeros((CHUNK, 128), f32)
-            cacc_ref[k, rows] = jnp.zeros((CHUNK, 128), f32)
-        return carry
-
-    lax.fori_loop(0, ROWS // CHUNK, clear, 0)
-    keep = (lax.broadcasted_iota(jnp.int32, (G, 128), 1) < G) == (core_ref[0] == 0)
-
-    def exchange(i, carry):
-        source = pl.ds(pl.multiple_of(i * G, G), G)
-        for j in range(8):
-            mine = mine_ref[j, source].astype(f32)
-            other = other_ref[j, source].astype(f32)
-            rows = pl.ds(pl.multiple_of((j // 2) * 512 + i * G, G), G)
-            same_ref[j % 2, rows] = jnp.where(keep, mine, pltpu.roll(other, G, 1)).astype(bf16)
-            cross_ref[j % 2, rows] = jnp.where(keep, pltpu.roll(mine, G, 1), other).astype(bf16)
-        return carry
-
-    lax.fori_loop(0, 8, exchange, 0)
-    low_lanes = lax.broadcasted_iota(jnp.int32, (32, 128), 1) < G
-
-    def run(right_ref, racc_ref, task):
-        a = task & 3
-        b = (task >> 2) & 1
-        second = 1.0 - (task >> 4).astype(f32)
-
-        def forward(i, c):
-            rows = pl.ds(pl.multiple_of(i * CHUNK, CHUNK), CHUNK)
-            rho = left_ref[a, rows].astype(f32) * right_ref[b, rows].astype(f32)
-            t_ref[rows] = rows_transform(depth_transform(rho, wz_ref[...]), wy_ref[...])
-            return c
-
-        lax.fori_loop(0, ROWS // CHUNK, forward, 0, unroll=UNROLL[0])
-
-        def middle(i, c):
-            first = pl.multiple_of(i * KY_STEP, KY_STEP)
-            value = gather_planes(t_ref, first, low_lanes)
-            kern = jnp.concatenate(
-                [kern_ref[i * (KY_STEP // 2) + j] for j in range(KY_STEP // 2)], axis=1
-            )
-            value = planes_transform(value, wx_ref[...]) * kern
-            value = planes_transform(value, wx_ref[...])
-            scatter_planes(t_ref, first, value, low_lanes)
-            return c
-
-        lax.fori_loop(0, G // KY_STEP, middle, 0, unroll=UNROLL[1])
-
-        def backward(i, c):
-            rows = pl.ds(pl.multiple_of(i * CHUNK, CHUNK), CHUNK)
-            v = depth_transform(rows_transform(t_ref[rows], wy_ref[...]), wz_ref[...])
-            lacc_ref[a, rows] += v * right_ref[b, rows].astype(f32)
-            racc_ref[b, rows] += (v * second) * left_ref[a, rows].astype(f32)
-            return c
-
-        lax.fori_loop(0, ROWS // CHUNK, backward, 0, unroll=UNROLL[2])
-
-    def one_task(t, carry):
-        task = tasks_ref[1 + t]
-        flipped = (task >> 3) & 1 == 1
-
-        @pl.when(jnp.logical_not(flipped))
-        def _():
-            run(same_ref, sacc_ref, task)
-
-        @pl.when(flipped)
-        def _():
-            run(cross_ref, cacc_ref, task)
-
-        return carry
-
-    lax.fori_loop(0, tasks_ref[0], one_task, 0)
 
 
 def quantize_piece(value_of, write):
@@ -273,13 +174,121 @@
     write(pl.ds(512, 16), codes.astype(jnp.int32).astype(jnp.int16))
 
 
-def quantize_left_kernel(in_ref, out_ref):
-    for k in range(out_ref.shape[0]):
-
+def pairs_kernel(
+    ids_ref,
+    tasks_ref,
+    left_ref,
+    mine0_ref,
+    mine1_ref,
+    mine2_ref,
+    mine3_ref,
+    other0_ref,
+    other1_ref,
+    other2_ref,
+    other3_ref,
+    wz_ref,
+    wy_ref,
+    wx_ref,
+    kern_ref,
+    left_out_ref,
+    sacc_ref,
+    cacc_ref,
+    t_ref,
+    same_ref,
+    cross_ref,
+    lacc_ref,
+):
+    def clear(i, carry):
+        rows = pl.ds(pl.multiple_of(i * CHUNK, CHUNK), CHUNK)
+        for k in range(4):
+            lacc_ref[k, rows] = jnp.zeros((CHUNK, 128), f32)
+        for k in range(2):
+            sacc_ref[k, rows] = jnp.zeros((CHUNK, 128), f32)
+            cacc_ref[k, rows] = jnp.zeros((CHUNK, 128), f32)
+        return carry
+
+    lax.fori_loop(0, ROWS // CHUNK, clear, 0)
+    keep = (lax.broadcasted_iota(jnp.int32, (G, 128), 1) < G) == (ids_ref[0] == 0)
+    mine_refs = (mine0_ref, mine1_ref, mine2_ref, mine3_ref)
+    other_refs = (other0_ref, other1_ref, other2_ref, other3_ref)
+
+    def exchange(i, carry):
+        source = pl.ds(pl.multiple_of(i * G, G), G)
+        for k in range(NY):
+            quarter = (ids_ref[1] - k) & (NY - 1)
+            rows = pl.ds(pl.multiple_of(quarter * 512 + i * G, G), G)
+            for j in range(2):
+                mine = mine_refs[k][j, source].astype(f32)
+                other = other_refs[k][j, source].astype(f32)
+                same_ref[j, rows] = jnp.where(keep, mine, pltpu.roll(other, G, 1)).astype(bf16)
+                cross_ref[j, rows] = jnp.where(keep, pltpu.roll(mine, G, 1), other).astype(bf16)
+        return carry
+
+    lax.fori_loop(0, 8, exchange, 0)
+    low_lanes = lax.broadcasted_iota(jnp.int32, (32, 128), 1) < G
+
+    def run(right_ref, racc_ref, task):
+        a = task & 3
+        b = (task >> 2) & 1
+        second = 1.0 - (task >> 4).astype(f32)
+
+        def forward(i, c):
+            rows = pl.ds(pl.multiple_of(i * CHUNK, CHUNK), CHUNK)
+            rho = left_ref[a, rows].astype(f32) * right_ref[b, rows].astype(f32)
+            t_ref[rows] = rows_transform(depth_transform(rho, wz_ref[...]), wy_ref[...])
+            return c
+
+        lax.fori_loop(0, ROWS // CHUNK, forward, 0, unroll=UNROLL[0])
+
+        def middle(i, c):
+            first = pl.multiple_of(i * KY_STEP, KY_STEP)
+            value = gather_planes(t_ref, first, low_lanes)
+            kern = jnp.concatenate(
+                [kern_ref[i * (KY_STEP // 2) + j] for j in range(KY_STEP // 2)], axis=1
+            )
+            value = planes_transform(value, wx_ref[...]) * kern
+            value = planes_transform(value, wx_ref[...])
+            scatter_planes(t_ref, first, value, low_lanes)
+            return c
+
+        lax.fori_loop(0, G // KY_STEP, middle, 0, unroll=UNROLL[1])
+
+        def backward(i, c):
+            rows = pl.ds(pl.multiple_of(i * CHUNK, CHUNK), CHUNK)
+            v = depth_transform(rows_transform(t_ref[rows], wy_ref[...]), wz_ref[...])
+            lacc_ref[a, rows] += v * right_ref[b, rows].astype(f32)
+            racc_ref[b, rows] += (v * second) * left_ref[a, rows].astype(f32)
+            return c
+
+        lax.fori_loop(0, ROWS // CHUNK, backward, 0, unroll=UNROLL[2])
+
+    def one_task(t, carry):
+        task = tasks_ref[1 + t]
+        flipped = (task >> 3) & 1 == 1
+
+        @pl.when(jnp.logical_not(flipped))
+        def _():
+            run(same_ref, sacc_ref, task)
+
+        @pl.when(flipped)
+        def _():
+            run(cross_ref, cacc_ref, task)
+
+        return carry
+
+    lax.fori_loop(0, tasks_ref[0], one_task, 0)
+
+    def quantize_left(k, carry):
         def write(rows, value):
-            out_ref[k, rows] = value
-
-        quantize_piece(lambda p: in_ref[k, pl.ds(p * G, G)], write)
+            left_out_ref[k, rows] = value
+
+        def value_of(p):
+            return lacc_ref[k // NY, pl.ds(pl.multiple_of((k % NY) * 512 + p * G, G), G)]
+
+        quantize_piece(value_of, write)
+        return carry
+
+    lax.fori_loop(0, NX * NY, quantize_left, 0)
 
 
 def quantize_right_kernel(z_ref, first_ref, second_ref, *out_refs):
@@ -324,19 +333,6 @@
         refs[-1][rows] = value
 
     quantize_piece(value_of, write)
-
-
-def quantize_left(lacc):
-    pieces, step = NX * NY, 4
-    return pl.pallas_call(
-        quantize_left_kernel,
-        grid=(pieces // step,),
-        out_shape=jax.ShapeDtypeStruct((pieces, 528, 128), jnp.int16),
-        in_specs=[pl.BlockSpec((step, 512, 128), lambda i: (i, 0, 0))],
-        out_specs=pl.BlockSpec((step, 528, 128), lambda i: (i, 0, 0)),
-        cost_estimate=pl.CostEstimate(flops=0, bytes_accessed=10 * 1000 * 1000, transcendentals=0),
-        name="quantize_left",
-    )(lacc)
 
 
 def quantize_right(z, first, second):
@@ -392,10 +388,11 @@
     out_ref[pl.ds(COUPLES, COUPLES)] = jnp.sum(cross_ref[...], axis=1)
 
 
-def project_kernel(x_ref, phi_ref, over_ref, out_ref, coef_ref):
+def project_kernel(x_ref, phi_ref, over0_ref, over1_ref, over2_ref, over3_ref, out_ref, coef_ref):
     lane = lax.broadcasted_iota(jnp.int32, (COUPLES, 128), 1)
     for k in range(2):
-        part = over_ref[pl.ds(k * COUPLES, COUPLES)]
+        half = pl.ds(k * COUPLES, COUPLES)
+        part = (over0_ref[half] + over2_ref[half]) + (over1_ref[half] + over3_ref[half])
         low = jnp.sum(jnp.where(lane < G, part, 0.0), axis=1, keepdims=True)
         high = jnp.sum(jnp.where(lane < G, 0.0, part), axis=1, keepdims=True)
         coef_ref[k] = jnp.where(lane < G, low, high) / CELLS
@@ -436,58 +433,68 @@
     return [(i, (i + step) % size) for i in range(size)]
 
 
-def sum_over_slab(value):
-    value = value + lax.ppermute(value, "core", ring(2, 1))
-    near = lax.ppermute(value, "y", ring(NY, 1))
-    back = lax.ppermute(value, "y", ring(NY, 3))
-    far = lax.ppermute(value, "y", ring(NY, 2))
-    return (value + far) + (near + back)
+def over_y(value):
+    return [value] + [lax.ppermute(value, "y", ring(NY, k)) for k in range(1, NY)]
 
 
 def local(orbitals, pair_table):
     z, x, y, core = (lax.axis_index(a) for a in ("z", "x", "y", "core"))
     mine = orbitals[0]
-    live = pair_table[:, 0] >= 0
-    code = jnp.where(live, pair_table[:, 0] + 32 * pair_table[:, 1] + 1024 * pair_table[:, 2], -1)
-    z_couples = lax.all_gather(orbitals, "z", axis=0, tiled=True)
+    slots = jnp.concatenate([pair_table[:, 0], pair_table[:, 1] + 32 * pair_table[:, 2]])
+    slots = jnp.pad(slots.astype(bf16)[None], ((0, 15), (0, 64)))
+    z_couples = jnp.concatenate([mine.reshape(512, 128), slots], axis=0)[None]
+    z_couples = lax.all_gather(z_couples, "z", axis=0, tiled=True)
     own = lane_exchange(mine, core)
     spread = jnp.broadcast_to(own[None], (NX * NY,) + own.shape)
     left = lax.all_to_all(spread, ("x", "y"), split_axis=0, concat_axis=0, tiled=True)
-    codes = lax.all_gather(code[None], ("z", "x"), axis=0, tiled=True)
-
-    me = (z * 16 + x * 4 + y).astype(jnp.int32).reshape(1)
+
+    z_couples, left = lax.optimization_barrier((z_couples, left))
+    slots = z_couples[:, 512, :]
+    slots = jnp.concatenate([slots] + [lax.ppermute(slots, "x", ring(NX, k)) for k in range(1, NX)])
+    slots = packed_slots(slots[:, :32], slots[:, 32:64])
+    me = jnp.stack([z * 16 + x * 4 + y, x]).astype(jnp.int32)
     tasks = pl.pallas_call(
         assign_kernel,
-        out_shape=jax.ShapeDtypeStruct((17,), jnp.int32),
+        out_shape=jax.ShapeDtypeStruct((18,), jnp.int32),
         in_specs=smem_specs(2),
         out_specs=pl.BlockSpec(memory_space=pltpu.SMEM),
         scratch_shapes=[pltpu.SMEM((NZ * NX * NY,), jnp.int32)],
         cost_estimate=pl.CostEstimate(flops=0, bytes_accessed=60 * 1000 * 1000, transcendentals=0),
         name="assign",
-    )(me, codes)
-    z_couples, tasks = lax.optimization_barrier((z_couples, tasks))
+    )(me, slots)
     phi_all = lax.all_gather(z_couples, "x", axis=0, tiled=True)
-    y_couples, left = lax.optimization_barrier((z_couples, left))
-    right = lax.all_to_all(y_couples, "y", split_axis=0, concat_axis=0, tiled=True)
-    right_other = lax.ppermute(right, "core", ring(2, 1))
-    core_id = core.astype(jnp.int32).reshape(1)
+    right = []
+    for k in range(NY):
+        part = lax.dynamic_slice(z_couples, (2 * ((y + k) % NY), 0, 0), (2, 512, 128))
+        right.append(lax.ppermute(part, "y", ring(NY, k)) if k else part)
+    right_other = [lax.ppermute(part, "core", ring(2, 1)) for part in right]
+    ids = jnp.stack([core, y]).astype(jnp.int32)
 
     w_depth, w_rows, w_planes = (jnp.asarray(w) for w in weights())
-    lacc, sacc, cacc = pl.pallas_call(
+    left_parts, sacc, cacc = pl.pallas_call(
         pairs_kernel,
-        out_shape=tuple(jax.ShapeDtypeStruct((k, ROWS, 128), f32) for k in (4, 2, 2)),
-        in_specs=smem_specs(2) + vmem_specs(7),
+        out_shape=(
+            jax.ShapeDtypeStruct((NX * NY, 528, 128), jnp.int16),
+            jax.ShapeDtypeStruct((2, ROWS, 128), f32),
+            jax.ShapeDtypeStruct((2, ROWS, 128), f32),
+        ),
+        in_specs=smem_specs(2) + vmem_specs(5 + 2 * NY),
         out_specs=tuple(vmem_specs(3)),
-        scratch_shapes=[pltpu.VMEM((ROWS, 128), f32)] + [pltpu.VMEM((2, ROWS, 128), bf16)] * 2,
+        scratch_shapes=[
+            pltpu.VMEM((ROWS, 128), f32),
+            pltpu.VMEM((2, ROWS, 128), bf16),
+            pltpu.VMEM((2, ROWS, 128), bf16),
+            pltpu.VMEM((4, ROWS, 128), f32),
+        ],
         compiler_params=pltpu.CompilerParams(vmem_limit_bytes=48 * 1024 * 1024),
         cost_estimate=pl.CostEstimate(flops=0, bytes_accessed=60 * 1000 * 1000, transcendentals=0),
         name="pairs",
     )(
-        core_id,
+        ids,
         tasks,
         left.reshape(4, ROWS, 128),
-        right.reshape(8, 512, 128),
-        right_other.reshape(8, 512, 128),
+        *right,
+        *right_other,
         w_depth,
         w_rows,
         w_planes,
@@ -496,8 +503,6 @@
 
     other = lax.ppermute(cacc, "core", ring(2, 1))
     right_parts = quantize_right(z, sacc.reshape(NZ, 512, 128), other.reshape(NZ, 512, 128))
-    left_parts = quantize_left(lacc.reshape(NX * NY, 512, 128))
-    left_parts, *right_parts = lax.optimization_barrier((left_parts, *right_parts))
     left_parts = lax.all_to_all(left_parts, ("x", "y"), split_axis=0, concat_axis=0, tiled=True)
     right_parts = [
         lax.ppermute(part, "z", ring(NZ, k)) if k else part for k, part in enumerate(right_parts)
@@ -506,7 +511,6 @@
     action = combine(left_parts, from_right)
     action_other = lax.ppermute(action, "core", ring(2, 1))
 
-    phi_rows = phi_all.reshape(COUPLES, 512, 128)
     slab_action, over = pl.pallas_call(
         overlap_kernel,
         out_shape=(
@@ -517,15 +521,15 @@
         out_specs=tuple(vmem_specs(2)),
         scratch_shapes=[pltpu.VMEM((COUPLES, 8, 128), f32)] * 2,
         name="overlap",
-    )(core_id, action, action_other, phi_rows)
+    )(ids, action, action_other, phi_all)
     out = pl.pallas_call(
         project_kernel,
         out_shape=jax.ShapeDtypeStruct((512, 128), f32),
-        in_specs=vmem_specs(3),
+        in_specs=vmem_specs(2 + NY),
         out_specs=vmem_specs(1)[0],
         scratch_shapes=[pltpu.VMEM((2, COUPLES, 128), f32)],
         name="project",
-    )(slab_action, phi_rows, sum_over_slab(over))
+    )(slab_action, phi_all, *over_y(over + lax.ppermute(over, "core", ring(2, 1))))
     return out.reshape(1, 8, G, 128)
 
 

time: 228 us -> 215 us (0.943)
  blocking collectives: 40.8 us -> 0 us
  waiting for transfers between devices: 36.8 us -> 60.8 us
  starting transfers between devices: 62.6 us -> 73 us
  Pallas kernels: 59.1 us -> 50.5 us
  other arithmetic: 3.02 us -> 5.85 us
    unnamed x1 -> x0, blocking collectives: 40.8 us -> none
    all_gather x1, waiting for transfers between devices: 0.02 us -> 39.2 us  [local(): z_couples = lax.all_gather(z_couples, 'z', axis=0, tiled=True)]
    all_to_all x1 -> x0, waiting for transfers between devices: 9.68 us -> none  [local(): lax.all_to_all(y_couples, 'y', split_axis=0, concat_axis=0, tiled=True)]
    ppermute x5 -> x14, starting transfers between devices: 29.1 us -> 38.3 us  [the longest x3 21.1 us: over_y(): lax.ppermute(value, 'y', ring(NY, k))]
    pallas_call x3 -> x2, Pallas kernels: 39.8 us -> 31.2 us  [the longest x1 20.2 us: local(): pl.pallas_call(pairs_kernel, out_shape=(jax.ShapeDtypeStruct((NX * NY, 52...]
    ppermute x7, starting transfers between devices: 13.7 us -> 18 us  [local(): lax.ppermute(part, 'z', ring(NZ, k))]
    all_to_all x1 -> x0, starting transfers between devices: 3.66 us -> none  [local(): lax.all_to_all(y_couples, 'y', split_axis=0, concat_axis=0, tiled=True)]
    unnamed x50 -> x45, local copies, waits for them, and re-layouts: 6.87 us -> 7.24 us
  transfers between devices with their start and end apart: 21 -> 29, of which waited for: 10 -> 9; matrix products, arithmetic and copies ran while one was open for 1% -> 3% of each run, Pallas kernels for 22% -> 19%
where the time goes in v2:
time: 215 us
  starting transfers between devices  73 us (34%)
  waiting for transfers between devices  60.8 us (28%)
  Pallas kernels  50.5 us (23%)
  between operations  13.8 us (6%)
  local copies, waits for them, and re-layouts  11.2 us (5%)
  other arithmetic  5.85 us (3%)
    all_gather x1, waiting for transfers between devices, local(): z_couples = lax.all_gather(z_couples, 'z', axis=0, tiled=True)  39.2 us
    ppermute x3, starting transfers between devices, over_y(): lax.ppermute(value, 'y', ring(NY, k))  21.1 us
    pallas_call x1, Pallas kernels, local(): pl.pallas_call(pairs_kernel, out_shape=(jax.ShapeDtypeStruct((NX * NY, 52...  20.2 us
    ppermute x7, starting transfers between devices, local(): lax.ppermute(part, 'z', ring(NZ, k))  18 us
    ppermute x7, waiting for transfers between devices, local(): lax.ppermute(part, 'z', ring(NZ, k))  17.9 us
    pallas_call x1, Pallas kernels, local(): pl.pallas_call(assign_kernel, out_shape=jax.ShapeDtypeStruct((18,), jnp.i...  11 us
    ppermute x4, starting transfers between devices, local(): right_other = [lax.ppermute(part, 'core', ring(2, 1)) for part in right]  7.75 us
    unnamed x45, local copies, waits for them, and re-layouts  7.24 us
  transfers between devices with their start and end apart: 29, of which 9 were waited for; matrix products, arithmetic and copies ran while one was open for 3% of the time, Pallas kernels for 19%

profile of v2, /device:TPU:1, one launch (start us, length us, event | category | flops | bytes accessed | tf_op | source)
XLA Modules:
  0.0 215.2 jit_solution(18310896018261535989)
XLA Ops:
  6.5 3.2 %collective-permute-start = (bf16[8,64,128]{2,1,0:T(8,128)(2,1)}, bf16[8,64,128]{2,1,0:T(8,128)(2,1)S(1)}, u32[]{:S(2)}, u32[]{:S(2)}) collective-permute-start(bf16[8,64,128]{2,1,0:T(8,128)(2,1)} %bitcast.30), channel_id=1, source_target_pairs={{0,1},{1,0},{2,3},{3,2},{4,5},{5,4},{6,7},{7,6},{8,9},{9,8},{10,11... | collective-permute-start | bytes 393224 | tf_op jit(solution)/shard_map/ppermute | solution.py:423
  14.3 5.2 %all-to-all-start = ((bf16[16,8,64,128]{3,2,1,0:T(8,128)(2,1)}), bf16[16,8,64,128]{3,2,1,0:T(8,128)(2,1)S(1)}, u32[]{:S(2)}, u32[]{:S(2)}) async-start(bf16[16,8,64,128]{3,2,1,0:T(8,128)(2,1)} %broadcast_in_dim.23), calls=%async_computation | async-start | bytes 4194304 | tf_op jit(solution)/shard_map/all_to_all | solution.py:449
  20.3 39.2 %all-gather.6.cloned.1.call-done = bf16[4224,128]{1,0:T(8,128)(2,1)} async-done(((bf16[528,128]{1,0:T(8,128)(2,1)}), bf16[4224,128]{1,0:T(8,128)(2,1)}) %all-gather.6.cloned.1.call-update) | async-done | bytes 1081360 | tf_op jit(solution)/shard_map/all_gather | solution.py:446
  62.1 2.5 %collective-permute-start.6 = (bf16[2,512,128]{2,1,0:T(8,128)(2,1)S(1)}, bf16[2,512,128]{2,1,0:T(8,128)(2,1)S(1)}, u32[]{:S(2)}, u32[]{:S(2)}) collective-permute-start(bf16[2,512,128]{2,1,0:T(8,128)(2,1)S(1)} %get-tuple-element.35), channel_id=1, source_target_pairs={{0,6},{2,0},{4,2},{6,4},{1,7},{3,1},{5,3},{7,5},{8,14},{10,8},{12,... | collective-permute-start | bytes 786440 | tf_op jit(solution)/shard_map/ppermute | solution.py:469
  64.6 2.1 collective-permute-start.5
  69.4 2.4 %collective-permute-start.2 = (bf16[8,128]{1,0:T(8,128)(2,1)S(1)}, bf16[8,128]{1,0:T(8,128)(2,1)S(1)}, u32[]{:S(2)}, u32[]{:S(2)}) collective-permute-start(bf16[8,128]{1,0:T(8,128)(2,1)S(1)} %bitcast.33), channel_id=1, source_target_pairs={{0,16},{8,24},{16,0},{24,8},{1,17},{9,25},{17,1},{25,9},{2,18},{10... | collective-permute-start | bytes 6152 | tf_op jit(solution)/shard_map/ppermute | solution.py:453
  73.3 7.1 %collective-permute-start.7 = (bf16[2,512,128]{2,1,0:T(8,128)(2,1)S(1)}, bf16[2,512,128]{2,1,0:T(8,128)(2,1)S(1)}, u32[]{:S(2)}, u32[]{:S(2)}) collective-permute-start(bf16[2,512,128]{2,1,0:T(8,128)(2,1)S(1)} %get-tuple-element.38.mine0_ref), channel_id=1, source_target_pairs={{0,1},{1,0},{2,3},{3,2},{4,5},{5,4},{6,7},{7,6},{8,9},{9,8},{10,11... | collective-permute-start | bytes 786440 | tf_op jit(solution)/shard_map/ppermute | solution.py:470
  81.8 11.0 %assign.1.tasks_ref = s32[18]{0:T(128)} custom-call(s32[2]{0:T(128)} %pad_add_fusion.1.me_ref, s32[32,32]{1,0:T(8,128)} %fusion.36.slots_ref), custom_call_target="tpu_custom_call" | custom-call | bytes 60000000 | tf_op jit(solution)/shard_map/assign/pallas_call | solution.py:456
  93.4 20.2 %pairs.1 = (s16[16,528,128]{2,1,0:T(8,128)(2,1)}, f32[2,2048,128]{2,1,0:T(8,128)S(1)}, f32[2,2048,128]{2,1,0:T(8,128)}) custom-call(s32[2]{0:T(128)S(1)} %pad_add_fusion.ids_ref.core_ref, s32[18]{0:T(128)S(1)} %copy-done.5, bf16[4,2048,128]{2,1,0:T(8,128)(2,1)} %bitcast.26, bf16[2,512,128]{2,1,0:T(8,128)(2,1)S(1)} %get-tuple-element.38.mine0_ref, ...), custom_call_target="tpu_custom_call" | custom-call | bytes 60000000 | tf_op jit(solution)/shard_map/pairs/pallas_call | solution.py:474
  115.7 5.6 %all-to-all-start.1 = ((s16[16,528,128]{2,1,0:T(8,128)(2,1)}), s16[16,528,128]{2,1,0:T(8,128)(2,1)S(1)}, u32[]{:S(2)}, u32[]{:S(2)}) async-start(s16[16,528,128]{2,1,0:T(8,128)(2,1)} %get-tuple-element.22), calls=%async_computation.1 | async-start | bytes 4325376 | tf_op jit(solution)/shard_map/all_to_all | solution.py:506
  121.3 3.6 %quantize_right.1 = (s16[528,128]{1,0:T(8,128)(2,1)}, s16[528,128]{1,0:T(8,128)(2,1)}, s16[528,128]{1,0:T(8,128)(2,1)}, s16[528,128]{1,0:T(8,128)(2,1)}, s16[528...) custom-call(s32[1]{0:T(128)} %bitcast.13.z_ref, ...), custom_call_target="tpu_custom_call" | custom-call | bytes 8000000 | tf_op jit(solution)/shard_map/quantize_right/pallas_call | solution.py:339
  125.0 5.6 %collective-permute-start.13 = (s16[528,128]{1,0:T(8,128)(2,1)}, s16[528,128]{1,0:T(8,128)(2,1)S(1)}, u32[]{:S(2)}, u32[]{:S(2)}) collective-permute-start(s16[528,128]{1,0:T(8,128)(2,1)} %get-tuple-element.27), channel_id=1, source_target_pairs={{0,64},{32,96},{64,128},{96,160},{128,192},{160,224},{192,0},{224,... | collective-permute-start | bytes 405512 | tf_op jit(solution)/shard_map/ppermute | solution.py:508
  130.6 5.6 %collective-permute-start.15 = (s16[528,128]{1,0:T(8,128)(2,1)}, s16[528,128]{1,0:T(8,128)(2,1)S(1)}, u32[]{:S(2)}, u32[]{:S(2)}) collective-permute-start(s16[528,128]{1,0:T(8,128)(2,1)} %get-tuple-element.29), channel_id=1, source_target_pairs={{0,128},{32,160},{64,192},{96,224},{128,0},{160,32},{192,64},{224,... | collective-permute-start | bytes 405512 | tf_op jit(solution)/shard_map/ppermute | solution.py:508
  136.3 2.4 %collective-permute-start.17 = (s16[528,128]{1,0:T(8,128)(2,1)}, s16[528,128]{1,0:T(8,128)(2,1)S(1)}, u32[]{:S(2)}, u32[]{:S(2)}) collective-permute-start(s16[528,128]{1,0:T(8,128)(2,1)} %get-tuple-element.31), channel_id=1, source_target_pairs={{0,192},{32,224},{64,0},{96,32},{128,64},{160,96},{192,128},{224,1... | collective-permute-start | bytes 405512 | tf_op jit(solution)/shard_map/ppermute | solution.py:508
  138.7 4.3 %collective-permute-start.18 = (s16[528,128]{1,0:T(8,128)(2,1)}, s16[528,128]{1,0:T(8,128)(2,1)S(1)}, u32[]{:S(2)}, u32[]{:S(2)}) collective-permute-start(s16[528,128]{1,0:T(8,128)(2,1)} %get-tuple-element.32), channel_id=1, source_target_pairs={{0,224},{32,0},{64,32},{96,64},{128,96},{160,128},{192,160},{224,1... | collective-permute-start | bytes 405512 | tf_op jit(solution)/shard_map/ppermute | solution.py:508
  143.0 6.4 %collective-permute-done.15.refs_4_ = s16[528,128]{1,0:T(8,128)(2,1)S(1)} collective-permute-done((s16[528,128]{1,0:T(8,128)(2,1)}, s16[528,128]{1,0:T(8,128)(2,1)S(1)}, u32[]{:S(2)}, u32[]{:S(2)}) %collective-permute-start.15) | collective-permute-done | bytes 135200 | tf_op jit(solution)/shard_map/ppermute | solution.py:508
  150.4 7.4 %collective-permute-done.17.refs_6_ = s16[528,128]{1,0:T(8,128)(2,1)S(1)} collective-permute-done((s16[528,128]{1,0:T(8,128)(2,1)}, s16[528,128]{1,0:T(8,128)(2,1)S(1)}, u32[]{:S(2)}, u32[]{:S(2)}) %collective-permute-start.17) | collective-permute-done | bytes 135200 | tf_op jit(solution)/shard_map/ppermute | solution.py:508
  157.8 3.0 %collective-permute-done.18.refs_7_ = s16[528,128]{1,0:T(8,128)(2,1)S(1)} collective-permute-done((s16[528,128]{1,0:T(8,128)(2,1)}, s16[528,128]{1,0:T(8,128)(2,1)S(1)}, u32[]{:S(2)}, u32[]{:S(2)}) %collective-permute-start.18) | collective-permute-done | bytes 135200 | tf_op jit(solution)/shard_map/ppermute | solution.py:508
  161.5 2.3 %combine_right.1 = s16[528,128]{1,0:T(8,128)(2,1)} custom-call(s16[528,128]{1,0:T(8,128)(2,1)} %get-tuple-element.25.refs_0_, s16[528,128]{1,0:T(8,128)(2,1)} %copy-done.10, s16[528,128]{1,0:T(8,128)(2,1)} %copy-done.11, s16[528,128]{1,0:T(8,128)(2,1)} %copy-done.12, s16[528,128]{1,0:T(8,128)(2,1)} %copy-done.13, s16[528,128]{1,0:T(8,128)(2,1)} %copy-done.14, ...), custom_call_target="tpu_custom_call" | custom-call | bytes 6000000 | tf_op jit(solution)/shard_map/combine_right/pallas_call | solution.py:360
  167.4 2.9 %combine.1.own_ref = f32[512,128]{1,0:T(8,128)} custom-call(s16[16,528,128]{2,1,0:T(8,128)(2,1)} %copy-done.6, s16[528,128]{1,0:T(8,128)(2,1)} %copy-done.17), custom_call_target="tpu_custom_call" | custom-call | tf_op jit(solution)/shard_map/combine/pallas_call | solution.py:350
  172.9 5.6 %overlap.1 = (f32[512,128]{1,0:T(8,128)}, f32[64,128]{1,0:T(8,128)}) custom-call(s32[2]{0:T(128)} %copy-done.4, f32[512,128]{1,0:T(8,128)} %combine.1.own_ref, f32[512,128]{1,0:T(8,128)} %copy-done.9, bf16[32,528,128]{2,1,0:T(8,128)(2,1)} %all-gather.4.cloned.1.call-done.phi_ref), custom_call_target="tpu_custom_call" | custom-call | tf_op jit(solution)/shard_map/overlap/pallas_call | solution.py:514
  180.8 6.5 %collective-permute-start.22 = (f32[64,128]{1,0:T(8,128)S(1)}, f32[64,128]{1,0:T(8,128)S(1)}, u32[]{:S(2)}, u32[]{:S(2)}) collective-permute-start(f32[64,128]{1,0:T(8,128)S(1)} %add.150.over0_ref), channel_id=1, source_target_pairs={{0,2},{2,4},{4,6},{6,0},{1,3},{3,5},{5,7},{7,1},{8,10},{10,12},{12... | collective-permute-start | bytes 98312 | tf_op jit(solution)/shard_map/ppermute | solution.py:437
  187.2 12.7 %collective-permute-start.23 = (f32[64,128]{1,0:T(8,128)S(1)}, f32[64,128]{1,0:T(8,128)S(1)}, u32[]{:S(2)}, u32[]{:S(2)}) collective-permute-start(f32[64,128]{1,0:T(8,128)S(1)} %add.150.over0_ref), channel_id=1, source_target_pairs={{0,4},{2,6},{4,0},{6,2},{1,5},{3,7},{5,1},{7,3},{8,12},{10,14},{12... | collective-permute-start | bytes 98312 | tf_op jit(solution)/shard_map/ppermute | solution.py:437
  203.5 4.8 %project.1 = f32[512,128]{1,0:T(8,128)} custom-call(f32[512,128]{1,0:T(8,128)} %get-tuple-element.33.x_ref, bf16[32,528,128]{2,1,0:T(8,128)(2,1)} %all-gather.4.cloned.1.call-done.phi_ref, f32[64,128]{1,0:T(8,128)} %copy-done.18, f32[64,128]{1,0:T(8,128)} %copy-done.19, f32[64,128]{1,0:T(8,128)} %copy-done.20, f32[64,128]{1,0:T(8,128)} %copy-done.21), custom_call_target="tpu_custom_call" | custom-call | tf_op jit(solution)/shard_map/project/pallas_call | solution.py:525
  (114 shorter events, 29.6 us)
Async XLA Ops:
  6.5 4.8 %collective-permute-start = (bf16[8,64,128]{2,1,0:T(8,128)(2,1)}, bf16[8,64,128]{2,1,0:T(8,128)(2,1)S(1)}, u32[]{:S(2)}, u32[]{:S(2)}) collective-permute-start(bf16[8,64,128]{2,1,0:T(8,128)(2,1)} %bitcast.30), channel_id=1, source_target_pairs={{0,1},{1,0},{2,3},{3,2},{4,5},{5,4},{6,7},{7,6},{8,9},{9,8},{10,11... | collective-permute-start | bytes 393224 | tf_op jit(solution)/shard_map/ppermute | solution.py:423
  14.3 45.1 %all-to-all-start = ((bf16[16,8,64,128]{3,2,1,0:T(8,128)(2,1)}), bf16[16,8,64,128]{3,2,1,0:T(8,128)(2,1)S(1)}, u32[]{:S(2)}, u32[]{:S(2)}) async-start(bf16[16,8,64,128]{3,2,1,0:T(8,128)(2,1)} %broadcast_in_dim.23), calls=%async_computation | async-start | bytes 4194304 | tf_op jit(solution)/shard_map/all_to_all | solution.py:449
  19.5 40.0 %all-gather.6.cloned.1.call-start = ((), (), s32[]{:S(2)}) async-start(), calls=%async_computation.3 | async-start | bytes 1216512 | tf_op jit(solution)/shard_map/all_gather | solution.py:446
  20.2 152.0 %all-gather.4.cloned.1.call-start = ((), (), s32[]{:S(2)}) async-start(), calls=%async_computation.2 | async-start | bytes 5406720 | tf_op jit(solution)/shard_map/all_gather | solution.py:465
  62.1 18.3 %collective-permute-start.6 = (bf16[2,512,128]{2,1,0:T(8,128)(2,1)S(1)}, bf16[2,512,128]{2,1,0:T(8,128)(2,1)S(1)}, u32[]{:S(2)}, u32[]{:S(2)}) collective-permute-start(bf16[2,512,128]{2,1,0:T(8,128)(2,1)S(1)} %get-tuple-element.35), channel_id=1, source_target_pairs={{0,6},{2,0},{4,2},{6,4},{1,7},{3,1},{5,3},{7,5},{8,14},{10,8},{12,... | collective-permute-start | bytes 786440 | tf_op jit(solution)/shard_map/ppermute | solution.py:469
  64.6 15.8 %collective-permute-start.4 = (bf16[2,512,128]{2,1,0:T(8,128)(2,1)S(1)}, bf16[2,512,128]{2,1,0:T(8,128)(2,1)S(1)}, u32[]{:S(2)}, u32[]{:S(2)}) collective-permute-start(bf16[2,512,128]{2,1,0:T(8,128)(2,1)S(1)} %get-tuple-element.37), channel_id=1, source_target_pairs={{0,2},{2,4},{4,6},{6,0},{1,3},{3,5},{5,7},{7,1},{8,10},{10,12},{12... | collective-permute-start | bytes 786440 | tf_op jit(solution)/shard_map/ppermute | solution.py:469
  64.6 16.3 %collective-permute-start.5 = (bf16[2,512,128]{2,1,0:T(8,128)(2,1)S(1)}, bf16[2,512,128]{2,1,0:T(8,128)(2,1)S(1)}, u32[]{:S(2)}, u32[]{:S(2)}) collective-permute-start(bf16[2,512,128]{2,1,0:T(8,128)(2,1)S(1)} %get-tuple-element.36), channel_id=1, source_target_pairs={{0,4},{2,6},{4,0},{6,2},{1,5},{3,7},{5,1},{7,3},{8,12},{10,14},{12... | collective-permute-start | bytes 786440 | tf_op jit(solution)/shard_map/ppermute | solution.py:469
  69.4 3.9 %collective-permute-start.2 = (bf16[8,128]{1,0:T(8,128)(2,1)S(1)}, bf16[8,128]{1,0:T(8,128)(2,1)S(1)}, u32[]{:S(2)}, u32[]{:S(2)}) collective-permute-start(bf16[8,128]{1,0:T(8,128)(2,1)S(1)} %bitcast.33), channel_id=1, source_target_pairs={{0,16},{8,24},{16,0},{24,8},{1,17},{9,25},{17,1},{25,9},{2,18},{10... | collective-permute-start | bytes 6152 | tf_op jit(solution)/shard_map/ppermute | solution.py:453
  71.8 9.3 %collective-permute-start.3 = (bf16[8,128]{1,0:T(8,128)(2,1)S(1)}, bf16[8,128]{1,0:T(8,128)(2,1)S(1)}, u32[]{:S(2)}, u32[]{:S(2)}) collective-permute-start(bf16[8,128]{1,0:T(8,128)(2,1)S(1)} %bitcast.34), channel_id=1, source_target_pairs={{0,24},{8,0},{16,8},{24,16},{1,25},{9,1},{17,9},{25,17},{2,26},{10... | collective-permute-start | bytes 6152 | tf_op jit(solution)/shard_map/ppermute | solution.py:453
  73.3 19.5 %collective-permute-start.7 = (bf16[2,512,128]{2,1,0:T(8,128)(2,1)S(1)}, bf16[2,512,128]{2,1,0:T(8,128)(2,1)S(1)}, u32[]{:S(2)}, u32[]{:S(2)}) collective-permute-start(bf16[2,512,128]{2,1,0:T(8,128)(2,1)S(1)} %get-tuple-element.38.mine0_ref), channel_id=1, source_target_pairs={{0,1},{1,0},{2,3},{3,2},{4,5},{5,4},{6,7},{7,6},{8,9},{9,8},{10,11... | collective-permute-start | bytes 786440 | tf_op jit(solution)/shard_map/ppermute | solution.py:470
  80.4 12.3 %collective-permute-start.10 = (bf16[2,512,128]{2,1,0:T(8,128)(2,1)S(1)}, bf16[2,512,128]{2,1,0:T(8,128)(2,1)S(1)}, u32[]{:S(2)}, u32[]{:S(2)}) collective-permute-start(bf16[2,512,128]{2,1,0:T(8,128)(2,1)S(1)} %collective-permute-done.6.mine3_ref), channel_id=1, source_target_pairs={{0,1},{1,0},{2,3},{3,2},{4,5},{5,4},{6,7},{7,6},{8,9},{9,8},{10,11... | collective-permute-start | bytes 786440 | tf_op jit(solution)/shard_map/ppermute | solution.py:470
  80.5 12.3 %collective-permute-start.8 = (bf16[2,512,128]{2,1,0:T(8,128)(2,1)S(1)}, bf16[2,512,128]{2,1,0:T(8,128)(2,1)S(1)}, u32[]{:S(2)}, u32[]{:S(2)}) collective-permute-start(bf16[2,512,128]{2,1,0:T(8,128)(2,1)S(1)} %collective-permute-done.4.mine1_ref), channel_id=1, source_target_pairs={{0,1},{1,0},{2,3},{3,2},{4,5},{5,4},{6,7},{7,6},{8,9},{9,8},{10,11... | collective-permute-start | bytes 786440 | tf_op jit(solution)/shard_map/ppermute | solution.py:470
  81.0 11.8 %collective-permute-start.9 = (bf16[2,512,128]{2,1,0:T(8,128)(2,1)S(1)}, bf16[2,512,128]{2,1,0:T(8,128)(2,1)S(1)}, u32[]{:S(2)}, u32[]{:S(2)}) collective-permute-start(bf16[2,512,128]{2,1,0:T(8,128)(2,1)S(1)} %collective-permute-done.5.mine2_ref), channel_id=1, source_target_pairs={{0,1},{1,0},{2,3},{3,2},{4,5},{5,4},{6,7},{7,6},{8,9},{9,8},{10,11... | collective-permute-start | bytes 786440 | tf_op jit(solution)/shard_map/ppermute | solution.py:470
  115.1 6.2 %collective-permute-start.11 = (f32[2,2048,128]{2,1,0:T(8,128)}, f32[2,2048,128]{2,1,0:T(8,128)}, u32[]{:S(2)}, u32[]{:S(2)}) collective-permute-start(f32[2,2048,128]{2,1,0:T(8,128)} %get-tuple-element.24), channel_id=1, source_target_pairs={{0,1},{1,0},{2,3},{3,2},{4,5},{5,4},{6,7},{7,6},{8,9},{9,8},{10,11... | collective-permute-start | bytes 6291464 | tf_op jit(solution)/shard_map/ppermute | solution.py:504
  115.7 49.7 %all-to-all-start.1 = ((s16[16,528,128]{2,1,0:T(8,128)(2,1)}), s16[16,528,128]{2,1,0:T(8,128)(2,1)S(1)}, u32[]{:S(2)}, u32[]{:S(2)}) async-start(s16[16,528,128]{2,1,0:T(8,128)(2,1)} %get-tuple-element.22), calls=%async_computation.1 | async-start | bytes 4325376 | tf_op jit(solution)/shard_map/all_to_all | solution.py:506
  125.0 11.3 %collective-permute-start.12 = (s16[528,128]{1,0:T(8,128)(2,1)}, s16[528,128]{1,0:T(8,128)(2,1)S(1)}, u32[]{:S(2)}, u32[]{:S(2)}) collective-permute-start(s16[528,128]{1,0:T(8,128)(2,1)} %get-tuple-element.26), channel_id=1, source_target_pairs={{0,32},{32,64},{64,96},{96,128},{128,160},{160,192},{192,224},{224... | collective-permute-start | bytes 405512 | tf_op jit(solution)/shard_map/ppermute | solution.py:508
  125.0 13.7 %collective-permute-start.13 = (s16[528,128]{1,0:T(8,128)(2,1)}, s16[528,128]{1,0:T(8,128)(2,1)S(1)}, u32[]{:S(2)}, u32[]{:S(2)}) collective-permute-start(s16[528,128]{1,0:T(8,128)(2,1)} %get-tuple-element.27), channel_id=1, source_target_pairs={{0,64},{32,96},{64,128},{96,160},{128,192},{160,224},{192,0},{224,... | collective-permute-start | bytes 405512 | tf_op jit(solution)/shard_map/ppermute | solution.py:508
  130.6 12.3 %collective-permute-start.14 = (s16[528,128]{1,0:T(8,128)(2,1)}, s16[528,128]{1,0:T(8,128)(2,1)S(1)}, u32[]{:S(2)}, u32[]{:S(2)}) collective-permute-start(s16[528,128]{1,0:T(8,128)(2,1)} %get-tuple-element.28), channel_id=1, source_target_pairs={{0,96},{32,128},{64,160},{96,192},{128,224},{160,0},{192,32},{224,... | collective-permute-start | bytes 405512 | tf_op jit(solution)/shard_map/ppermute | solution.py:508
  130.6 18.7 %collective-permute-start.15 = (s16[528,128]{1,0:T(8,128)(2,1)}, s16[528,128]{1,0:T(8,128)(2,1)S(1)}, u32[]{:S(2)}, u32[]{:S(2)}) collective-permute-start(s16[528,128]{1,0:T(8,128)(2,1)} %get-tuple-element.29), channel_id=1, source_target_pairs={{0,128},{32,160},{64,192},{96,224},{128,0},{160,32},{192,64},{224,... | collective-permute-start | bytes 405512 | tf_op jit(solution)/shard_map/ppermute | solution.py:508
  136.3 14.2 %collective-permute-start.16 = (s16[528,128]{1,0:T(8,128)(2,1)}, s16[528,128]{1,0:T(8,128)(2,1)S(1)}, u32[]{:S(2)}, u32[]{:S(2)}) collective-permute-start(s16[528,128]{1,0:T(8,128)(2,1)} %get-tuple-element.30), channel_id=1, source_target_pairs={{0,160},{32,192},{64,224},{96,0},{128,32},{160,64},{192,96},{224,1... | collective-permute-start | bytes 405512 | tf_op jit(solution)/shard_map/ppermute | solution.py:508
  136.3 21.5 %collective-permute-start.17 = (s16[528,128]{1,0:T(8,128)(2,1)}, s16[528,128]{1,0:T(8,128)(2,1)S(1)}, u32[]{:S(2)}, u32[]{:S(2)}) collective-permute-start(s16[528,128]{1,0:T(8,128)(2,1)} %get-tuple-element.31), channel_id=1, source_target_pairs={{0,192},{32,224},{64,0},{96,32},{128,64},{160,96},{192,128},{224,1... | collective-permute-start | bytes 405512 | tf_op jit(solution)/shard_map/ppermute | solution.py:508
  138.7 22.2 %collective-permute-start.18 = (s16[528,128]{1,0:T(8,128)(2,1)}, s16[528,128]{1,0:T(8,128)(2,1)S(1)}, u32[]{:S(2)}, u32[]{:S(2)}) collective-permute-start(s16[528,128]{1,0:T(8,128)(2,1)} %get-tuple-element.32), channel_id=1, source_target_pairs={{0,224},{32,0},{64,32},{96,64},{128,96},{160,128},{192,160},{224,1... | collective-permute-start | bytes 405512 | tf_op jit(solution)/shard_map/ppermute | solution.py:508
  180.8 21.1 %collective-permute-start.22 = (f32[64,128]{1,0:T(8,128)S(1)}, f32[64,128]{1,0:T(8,128)S(1)}, u32[]{:S(2)}, u32[]{:S(2)}) collective-permute-start(f32[64,128]{1,0:T(8,128)S(1)} %add.150.over0_ref), channel_id=1, source_target_pairs={{0,2},{2,4},{4,6},{6,0},{1,3},{3,5},{5,7},{7,1},{8,10},{10,12},{12... | collective-permute-start | bytes 98312 | tf_op jit(solution)/shard_map/ppermute | solution.py:437
  187.2 14.6 %collective-permute-start.23 = (f32[64,128]{1,0:T(8,128)S(1)}, f32[64,128]{1,0:T(8,128)S(1)}, u32[]{:S(2)}, u32[]{:S(2)}) collective-permute-start(f32[64,128]{1,0:T(8,128)S(1)} %add.150.over0_ref), channel_id=1, source_target_pairs={{0,4},{2,6},{4,0},{6,2},{1,5},{3,7},{5,1},{7,3},{8,12},{10,14},{12... | collective-permute-start | bytes 98312 | tf_op jit(solution)/shard_map/ppermute | solution.py:437
  (27 other events, 278.9 us)
Sparse Core Ops, SparseCore 0:
  22.1 37.2 all-gather.5
  61.2 54.7 all-gather.3

commit v3 on v2

--- a/solution.py
+++ b/solution.py
@@ -291,9 +291,10 @@
     lax.fori_loop(0, NX * NY, quantize_left, 0)
 
 
-def quantize_right_kernel(z_ref, first_ref, second_ref, *out_refs):
+def quantize_right_kernel(zy_ref, first_ref, second_ref, *out_refs):
     for k in range(NZ):
-        piece = (z_ref[0] + k) & (NZ - 1)
+        step = (zy_ref[0] + k - 2 * zy_ref[1]) & (NZ - 1)
+        piece = jnp.where((step >= 1) & (step <= NY), step + NY - 1, (NZ - step) & (NZ - 1))
 
         def write(rows, value):
             out_refs[k][rows] = value
@@ -335,7 +336,7 @@
     quantize_piece(value_of, write)
 
 
-def quantize_right(z, first, second):
+def quantize_right(zy, first, second):
     return pl.pallas_call(
         quantize_right_kernel,
         out_shape=(jax.ShapeDtypeStruct((528, 128), jnp.int16),) * NZ,
@@ -343,7 +344,7 @@
         out_specs=tuple(vmem_specs(NZ)),
         cost_estimate=pl.CostEstimate(flops=0, bytes_accessed=8 * 1000 * 1000, transcendentals=0),
         name="quantize_right",
-    )(z.astype(jnp.int32).reshape(1), first, second)
+    )(zy, first, second)
 
 
 def combine(left_parts, right_part):
@@ -425,8 +426,14 @@
     return jnp.where((lane < G) == (core == 0), mine, jnp.roll(other, G, axis=-1))
 
 
-def moves():
-    return [(z * NY + y, ((z & 1) * NY + y) * NY + (z >> 1)) for z in range(NZ) for y in range(NY)]
+def home():
+    pairs = []
+    for z in range(NZ):
+        for q in range(NY):
+            y, b = z // 2, z % 2
+            holder = (2 * y + (q + 1 if b else -q)) % NZ
+            pairs.append((holder * NY + y, z * NY + q))
+    return pairs
 
 
 def ring(size, step):
@@ -467,6 +474,7 @@
     for k in range(NY):
         part = lax.dynamic_slice(z_couples, (2 * ((y + k) % NY), 0, 0), (2, 512, 128))
         right.append(lax.ppermute(part, "y", ring(NY, k)) if k else part)
+    *right, tasks = lax.optimization_barrier((*right, tasks))
     right_other = [lax.ppermute(part, "core", ring(2, 1)) for part in right]
     ids = jnp.stack([core, y]).astype(jnp.int32)
 
@@ -502,12 +510,12 @@
     )
 
     other = lax.ppermute(cacc, "core", ring(2, 1))
-    right_parts = quantize_right(z, sacc.reshape(NZ, 512, 128), other.reshape(NZ, 512, 128))
+    right_parts = quantize_right(jnp.stack([z, y]).astype(jnp.int32), sacc.reshape(NZ, 512, 128), other.reshape(NZ, 512, 128))
     left_parts = lax.all_to_all(left_parts, ("x", "y"), split_axis=0, concat_axis=0, tiled=True)
     right_parts = [
         lax.ppermute(part, "z", ring(NZ, k)) if k else part for k, part in enumerate(right_parts)
     ]
-    from_right = lax.ppermute(combine_right(right_parts), ("z", "y"), [(d, s) for s, d in moves()])
+    from_right = lax.ppermute(combine_right(right_parts), ("z", "y"), home())
     action = combine(left_parts, from_right)
     action_other = lax.ppermute(action, "core", ring(2, 1))
 

time: 215 us -> 209 us (0.972)
  starting transfers between devices: 73 us -> 63.9 us
    ppermute x3, starting transfers between devices: 21.1 us -> 16.8 us  [over_y(): lax.ppermute(value, 'y', ring(NY, k))]
    ppermute x7, starting transfers between devices: 18 us -> 14.5 us  [local(): lax.ppermute(part, 'z', ring(NZ, k))]
  transfers between devices with their start and end apart: 29 -> 29, of which waited for: 9 -> 11; matrix products, arithmetic and copies ran while one was open for 3% -> 4% of each run, Pallas kernels for 19% -> 19%
where the time goes in v3:
time: 209 us; the launch traced here: 207 us
  starting transfers between devices  63.9 us (31%)
  waiting for transfers between devices  61.5 us (29%)
  Pallas kernels  50.5 us (24%)
  between operations  13.7 us (7%)
  local copies, waits for them, and re-layouts  10.9 us (5%)
  other arithmetic  6.47 us (3%)
    all_gather x1, waiting for transfers between devices, local(): z_couples = lax.all_gather(z_couples, 'z', axis=0, tiled=True)  39.2 us
    pallas_call x1, Pallas kernels, local(): pl.pallas_call(pairs_kernel, out_shape=(jax.ShapeDtypeStruct((NX * NY, 52...  20.2 us
    ppermute x7, waiting for transfers between devices, local(): lax.ppermute(part, 'z', ring(NZ, k))  17.7 us
    ppermute x3, starting transfers between devices, over_y(): lax.ppermute(value, 'y', ring(NY, k))  16.8 us
    ppermute x7, starting transfers between devices, local(): lax.ppermute(part, 'z', ring(NZ, k))  14.5 us
    pallas_call x1, Pallas kernels, local(): pl.pallas_call(assign_kernel, out_shape=jax.ShapeDtypeStruct((18,), jnp.i...  11 us
    ppermute x4, starting transfers between devices, local(): right_other = [lax.ppermute(part, 'core', ring(2, 1)) for part in right]  7.25 us
    unnamed x45, local copies, waits for them, and re-layouts  6.07 us
  transfers between devices with their start and end apart: 29, of which 11 were waited for; matrix products, arithmetic and copies ran while one was open for 4% of the time, Pallas kernels for 19%

profile of v3, /device:TPU:1, one launch (start us, length us, event | category | flops | bytes accessed | tf_op | source)
XLA Modules:
  0.0 207.1 jit_solution(13067517432063333211)
XLA Ops:
  6.5 3.2 %collective-permute-start = (bf16[8,64,128]{2,1,0:T(8,128)(2,1)}, bf16[8,64,128]{2,1,0:T(8,128)(2,1)S(1)}, u32[]{:S(2)}, u32[]{:S(2)}) collective-permute-start(bf16[8,64,128]{2,1,0:T(8,128)(2,1)} %bitcast.30), channel_id=1, source_target_pairs={{0,1},{1,0},{2,3},{3,2},{4,5},{5,4},{6,7},{7,6},{8,9},{9,8},{10,11... | collective-permute-start | bytes 393224 | tf_op jit(solution)/shard_map/ppermute | solution.py:424
  14.3 5.2 %all-to-all-start = ((bf16[16,8,64,128]{3,2,1,0:T(8,128)(2,1)}), bf16[16,8,64,128]{3,2,1,0:T(8,128)(2,1)S(1)}, u32[]{:S(2)}, u32[]{:S(2)}) async-start(bf16[16,8,64,128]{3,2,1,0:T(8,128)(2,1)} %broadcast_in_dim.23), calls=%async_computation | async-start | bytes 4194304 | tf_op jit(solution)/shard_map/all_to_all | solution.py:456
  20.3 39.2 %all-gather.6.cloned.1.call-done = bf16[4224,128]{1,0:T(8,128)(2,1)} async-done(((bf16[528,128]{1,0:T(8,128)(2,1)}), bf16[4224,128]{1,0:T(8,128)(2,1)}) %all-gather.6.cloned.1.call-update) | async-done | bytes 1081360 | tf_op jit(solution)/shard_map/all_gather | solution.py:453
  62.6 2.0 collective-permute-start.5
  66.2 2.1 %constant_dynamic-slice_fusion = (bf16[2,512,128]{2,1,0:T(8,128)(2,1)}, bf16[2,512,128]{2,1,0:T(8,128)(2,1)}, bf16[2,512,128]{2,1,0:T(8,128)(2,1)}, bf16[2,512,128]{2,1,0:T(8,128)(2,1)S(1)}) fusion(bf16[8,528,128]{2,1,0:T(8,128)(2,1)} %bitcast.29, s32[]{:T(128)S(6)} %select_n.80, s32[]{:T(128)S(6)} %select_n.78, s32[]{:T(128)S(6)} %select_n.76, s32[]{:T(128)S(6)} %select_n.74), kind=kLoop, calls=%fused_computation.94 | loop fusion | bytes 2097168 | tf_op jit(solution)/shard_map/dynamic_slice | solution.py:475
  69.1 2.8 %collective-permute-start.2 = (bf16[2,512,128]{2,1,0:T(8,128)(2,1)}, bf16[2,512,128]{2,1,0:T(8,128)(2,1)S(1)}, u32[]{:S(2)}, u32[]{:S(2)}) collective-permute-start(bf16[2,512,128]{2,1,0:T(8,128)(2,1)} %get-tuple-element.46), channel_id=1, source_target_pairs={{0,4},{2,6},{4,0},{6,2},{1,5},{3,7},{5,1},{7,3},{8,12},{10,14},{12... | collective-permute-start | bytes 786440 | tf_op jit(solution)/shard_map/ppermute | solution.py:476
  73.4 11.0 %assign.1.tasks_ref = s32[18]{0:T(128)} custom-call(s32[2]{0:T(128)} %pad_add_fusion.1.me_ref, s32[32,32]{1,0:T(8,128)} %fusion.36.slots_ref), custom_call_target="tpu_custom_call" | custom-call | bytes 60000000 | tf_op jit(solution)/shard_map/assign/pallas_call | solution.py:463
  84.4 6.6 %collective-permute-start.10 = (bf16[2,512,128]{2,1,0:T(8,128)(2,1)S(1)}, bf16[2,512,128]{2,1,0:T(8,128)(2,1)S(1)}, u32[]{:S(2)}, u32[]{:S(2)}) collective-permute-start(bf16[2,512,128]{2,1,0:T(8,128)(2,1)S(1)} %collective-permute-done.3.mine3_ref), channel_id=1, source_target_pairs={{0,1},{1,0},{2,3},{3,2},{4,5},{5,4},{6,7},{7,6},{8,9},{9,8},{10,11... | collective-permute-start | bytes 786440 | tf_op jit(solution)/shard_map/ppermute | solution.py:478
  94.0 20.2 %pairs.1 = (s16[16,528,128]{2,1,0:T(8,128)(2,1)}, f32[2,2048,128]{2,1,0:T(8,128)S(1)}, f32[2,2048,128]{2,1,0:T(8,128)}) custom-call(s32[2]{0:T(128)S(1)} %pad_add_fusion.ids_ref.core_ref, s32[18]{0:T(128)S(1)} %copy-done.5, bf16[4,2048,128]{2,1,0:T(8,128)(2,1)} %bitcast.26, bf16[2,512,128]{2,1,0:T(8,128)(2,1)S(1)} %get-tuple-element.28.mine0_ref, ...), custom_call_target="tpu_custom_call" | custom-call | bytes 60000000 | tf_op jit(solution)/shard_map/pairs/pallas_call | solution.py:482
  116.0 4.4 %all-to-all-start.1 = ((s16[16,528,128]{2,1,0:T(8,128)(2,1)}), s16[16,528,128]{2,1,0:T(8,128)(2,1)S(1)}, u32[]{:S(2)}, u32[]{:S(2)}) async-start(s16[16,528,128]{2,1,0:T(8,128)(2,1)} %get-tuple-element.32), calls=%async_computation.1 | async-start | bytes 4325376 | tf_op jit(solution)/shard_map/all_to_all | solution.py:514
  121.0 3.7 %quantize_right.1 = (s16[528,128]{1,0:T(8,128)(2,1)}, s16[528,128]{1,0:T(8,128)(2,1)}, s16[528,128]{1,0:T(8,128)(2,1)}, s16[528,128]{1,0:T(8,128)(2,1)}, s16[528...) custom-call(s32[2]{0:T(128)} %pad_add_fusion.2.zy_ref, ...), custom_call_target="tpu_custom_call" | custom-call | bytes 8000000 | tf_op jit(solution)/shard_map/quantize_right/pallas_call | solution.py:340
  124.8 5.1 %collective-permute-start.14 = (s16[528,128]{1,0:T(8,128)(2,1)}, s16[528,128]{1,0:T(8,128)(2,1)S(1)}, u32[]{:S(2)}, u32[]{:S(2)}) collective-permute-start(s16[528,128]{1,0:T(8,128)(2,1)} %get-tuple-element.38), channel_id=1, source_target_pairs={{0,96},{32,128},{64,160},{96,192},{128,224},{160,0},{192,32},{224,... | collective-permute-start | bytes 405512 | tf_op jit(solution)/shard_map/ppermute | solution.py:516
  130.3 4.0 %collective-permute-start.16 = (s16[528,128]{1,0:T(8,128)(2,1)}, s16[528,128]{1,0:T(8,128)(2,1)S(1)}, u32[]{:S(2)}, u32[]{:S(2)}) collective-permute-start(s16[528,128]{1,0:T(8,128)(2,1)} %get-tuple-element.40), channel_id=1, source_target_pairs={{0,160},{32,192},{64,224},{96,0},{128,32},{160,64},{192,96},{224,1... | collective-permute-start | bytes 405512 | tf_op jit(solution)/shard_map/ppermute | solution.py:516
  134.3 3.3 %collective-permute-start.17 = (s16[528,128]{1,0:T(8,128)(2,1)}, s16[528,128]{1,0:T(8,128)(2,1)S(1)}, u32[]{:S(2)}, u32[]{:S(2)}) collective-permute-start(s16[528,128]{1,0:T(8,128)(2,1)} %get-tuple-element.41), channel_id=1, source_target_pairs={{0,192},{32,224},{64,0},{96,32},{128,64},{160,96},{192,128},{224,1... | collective-permute-start | bytes 405512 | tf_op jit(solution)/shard_map/ppermute | solution.py:516
  139.1 2.7 %collective-permute-done.14.refs_3_ = s16[528,128]{1,0:T(8,128)(2,1)S(1)} collective-permute-done((s16[528,128]{1,0:T(8,128)(2,1)}, s16[528,128]{1,0:T(8,128)(2,1)S(1)}, u32[]{:S(2)}, u32[]{:S(2)}) %collective-permute-start.14) | collective-permute-done | bytes 135200 | tf_op jit(solution)/shard_map/ppermute | solution.py:516
  141.8 4.8 %collective-permute-done.15.refs_4_ = s16[528,128]{1,0:T(8,128)(2,1)S(1)} collective-permute-done((s16[528,128]{1,0:T(8,128)(2,1)}, s16[528,128]{1,0:T(8,128)(2,1)S(1)}, u32[]{:S(2)}, u32[]{:S(2)}) %collective-permute-start.15) | collective-permute-done | bytes 135200 | tf_op jit(solution)/shard_map/ppermute | solution.py:516
  146.6 5.3 %collective-permute-done.16.refs_5_ = s16[528,128]{1,0:T(8,128)(2,1)S(1)} collective-permute-done((s16[528,128]{1,0:T(8,128)(2,1)}, s16[528,128]{1,0:T(8,128)(2,1)S(1)}, u32[]{:S(2)}, u32[]{:S(2)}) %collective-permute-start.16) | collective-permute-done | bytes 135200 | tf_op jit(solution)/shard_map/ppermute | solution.py:516
  151.9 4.9 %collective-permute-done.17.refs_6_ = s16[528,128]{1,0:T(8,128)(2,1)S(1)} collective-permute-done((s16[528,128]{1,0:T(8,128)(2,1)}, s16[528,128]{1,0:T(8,128)(2,1)S(1)}, u32[]{:S(2)}, u32[]{:S(2)}) %collective-permute-start.17) | collective-permute-done | bytes 135200 | tf_op jit(solution)/shard_map/ppermute | solution.py:516
  157.5 2.3 %combine_right.1 = s16[528,128]{1,0:T(8,128)(2,1)} custom-call(s16[528,128]{1,0:T(8,128)(2,1)} %get-tuple-element.35.refs_0_, s16[528,128]{1,0:T(8,128)(2,1)} %copy-done.10, s16[528,128]{1,0:T(8,128)(2,1)} %copy-done.11, s16[528,128]{1,0:T(8,128)(2,1)} %copy-done.12, s16[528,128]{1,0:T(8,128)(2,1)} %copy-done.13, s16[528,128]{1,0:T(8,128)(2,1)} %copy-done.14, ...), custom_call_target="tpu_custom_call" | custom-call | bytes 6000000 | tf_op jit(solution)/shard_map/combine_right/pallas_call | solution.py:361
  163.4 2.9 %combine.1.own_ref = f32[512,128]{1,0:T(8,128)} custom-call(s16[16,528,128]{2,1,0:T(8,128)(2,1)} %copy-done.6, s16[528,128]{1,0:T(8,128)(2,1)} %copy-done.17), custom_call_target="tpu_custom_call" | custom-call | tf_op jit(solution)/shard_map/combine/pallas_call | solution.py:351
  169.2 5.6 %overlap.1 = (f32[512,128]{1,0:T(8,128)}, f32[64,128]{1,0:T(8,128)}) custom-call(s32[2]{0:T(128)} %copy-done.4, f32[512,128]{1,0:T(8,128)} %combine.1.own_ref, f32[512,128]{1,0:T(8,128)} %copy-done.9, bf16[32,528,128]{2,1,0:T(8,128)(2,1)} %all-gather.4.cloned.1.call-done.phi_ref), custom_call_target="tpu_custom_call" | custom-call | tf_op jit(solution)/shard_map/overlap/pallas_call | solution.py:522
  177.0 7.8 %collective-permute-start.22 = (f32[64,128]{1,0:T(8,128)S(1)}, f32[64,128]{1,0:T(8,128)S(1)}, u32[]{:S(2)}, u32[]{:S(2)}) collective-permute-start(f32[64,128]{1,0:T(8,128)S(1)} %add.150.over0_ref), channel_id=1, source_target_pairs={{0,2},{2,4},{4,6},{6,0},{1,3},{3,5},{5,7},{7,1},{8,10},{10,12},{12... | collective-permute-start | bytes 98312 | tf_op jit(solution)/shard_map/ppermute | solution.py:444
  184.8 7.0 %collective-permute-start.23 = (f32[64,128]{1,0:T(8,128)S(1)}, f32[64,128]{1,0:T(8,128)S(1)}, u32[]{:S(2)}, u32[]{:S(2)}) collective-permute-start(f32[64,128]{1,0:T(8,128)S(1)} %add.150.over0_ref), channel_id=1, source_target_pairs={{0,4},{2,6},{4,0},{6,2},{1,5},{3,7},{5,1},{7,3},{8,12},{10,14},{12... | collective-permute-start | bytes 98312 | tf_op jit(solution)/shard_map/ppermute | solution.py:444
  195.4 4.8 %project.1 = f32[512,128]{1,0:T(8,128)} custom-call(f32[512,128]{1,0:T(8,128)} %get-tuple-element.43.x_ref, bf16[32,528,128]{2,1,0:T(8,128)(2,1)} %all-gather.4.cloned.1.call-done.phi_ref, f32[64,128]{1,0:T(8,128)} %copy-done.18, f32[64,128]{1,0:T(8,128)} %copy-done.19, f32[64,128]{1,0:T(8,128)} %copy-done.20, f32[64,128]{1,0:T(8,128)} %copy-done.21), custom_call_target="tpu_custom_call" | custom-call | tf_op jit(solution)/shard_map/project/pallas_call | solution.py:533
  (115 shorter events, 32.3 us)
Async XLA Ops:
  6.5 4.8 %collective-permute-start = (bf16[8,64,128]{2,1,0:T(8,128)(2,1)}, bf16[8,64,128]{2,1,0:T(8,128)(2,1)S(1)}, u32[]{:S(2)}, u32[]{:S(2)}) collective-permute-start(bf16[8,64,128]{2,1,0:T(8,128)(2,1)} %bitcast.30), channel_id=1, source_target_pairs={{0,1},{1,0},{2,3},{3,2},{4,5},{5,4},{6,7},{7,6},{8,9},{9,8},{10,11... | collective-permute-start | bytes 393224 | tf_op jit(solution)/shard_map/ppermute | solution.py:424
  14.3 45.1 %all-to-all-start = ((bf16[16,8,64,128]{3,2,1,0:T(8,128)(2,1)}), bf16[16,8,64,128]{3,2,1,0:T(8,128)(2,1)S(1)}, u32[]{:S(2)}, u32[]{:S(2)}) async-start(bf16[16,8,64,128]{3,2,1,0:T(8,128)(2,1)} %broadcast_in_dim.23), calls=%async_computation | async-start | bytes 4194304 | tf_op jit(solution)/shard_map/all_to_all | solution.py:456
  19.5 40.0 %all-gather.6.cloned.1.call-start = ((), (), s32[]{:S(2)}) async-start(), calls=%async_computation.3 | async-start | bytes 1216512 | tf_op jit(solution)/shard_map/all_gather | solution.py:453
  20.2 148.2 %all-gather.4.cloned.1.call-start = ((), (), s32[]{:S(2)}) async-start(), calls=%async_computation.2 | async-start | bytes 5406720 | tf_op jit(solution)/shard_map/all_gather | solution.py:472
  61.0 10.9 %collective-permute-start.4 = (bf16[8,128]{1,0:T(8,128)(2,1)S(1)}, bf16[8,128]{1,0:T(8,128)(2,1)S(1)}, u32[]{:S(2)}, u32[]{:S(2)}) collective-permute-start(bf16[8,128]{1,0:T(8,128)(2,1)S(1)} %bitcast.32), channel_id=1, source_target_pairs={{0,8},{8,16},{16,24},{24,0},{1,9},{9,17},{17,25},{25,1},{2,10},{10... | collective-permute-start | bytes 6152 | tf_op jit(solution)/shard_map/ppermute | solution.py:460
  62.6 10.1 %collective-permute-start.5 = (bf16[8,128]{1,0:T(8,128)(2,1)S(1)}, bf16[8,128]{1,0:T(8,128)(2,1)S(1)}, u32[]{:S(2)}, u32[]{:S(2)}) collective-permute-start(bf16[8,128]{1,0:T(8,128)(2,1)S(1)} %bitcast.33), channel_id=1, source_target_pairs={{0,16},{8,24},{16,0},{24,8},{1,17},{9,25},{17,1},{25,9},{2,18},{10... | collective-permute-start | bytes 6152 | tf_op jit(solution)/shard_map/ppermute | solution.py:460
  64.6 8.1 %collective-permute-start.6 = (bf16[8,128]{1,0:T(8,128)(2,1)S(1)}, bf16[8,128]{1,0:T(8,128)(2,1)S(1)}, u32[]{:S(2)}, u32[]{:S(2)}) collective-permute-start(bf16[8,128]{1,0:T(8,128)(2,1)S(1)} %bitcast.34), channel_id=1, source_target_pairs={{0,24},{8,0},{16,8},{24,16},{1,25},{9,1},{17,9},{25,17},{2,26},{10... | collective-permute-start | bytes 6152 | tf_op jit(solution)/shard_map/ppermute | solution.py:460
  68.3 16.1 %collective-permute-start.1 = (bf16[2,512,128]{2,1,0:T(8,128)(2,1)}, bf16[2,512,128]{2,1,0:T(8,128)(2,1)S(1)}, u32[]{:S(2)}, u32[]{:S(2)}) collective-permute-start(bf16[2,512,128]{2,1,0:T(8,128)(2,1)} %get-tuple-element.47), channel_id=1, source_target_pairs={{0,2},{2,4},{4,6},{6,0},{1,3},{3,5},{5,7},{7,1},{8,10},{10,12},{12... | collective-permute-start | bytes 786440 | tf_op jit(solution)/shard_map/ppermute | solution.py:476
  69.1 15.3 %collective-permute-start.2 = (bf16[2,512,128]{2,1,0:T(8,128)(2,1)}, bf16[2,512,128]{2,1,0:T(8,128)(2,1)S(1)}, u32[]{:S(2)}, u32[]{:S(2)}) collective-permute-start(bf16[2,512,128]{2,1,0:T(8,128)(2,1)} %get-tuple-element.46), channel_id=1, source_target_pairs={{0,4},{2,6},{4,0},{6,2},{1,5},{3,7},{5,1},{7,3},{8,12},{10,14},{12... | collective-permute-start | bytes 786440 | tf_op jit(solution)/shard_map/ppermute | solution.py:476
  71.9 12.5 %collective-permute-start.3 = (bf16[2,512,128]{2,1,0:T(8,128)(2,1)}, bf16[2,512,128]{2,1,0:T(8,128)(2,1)S(1)}, u32[]{:S(2)}, u32[]{:S(2)}) collective-permute-start(bf16[2,512,128]{2,1,0:T(8,128)(2,1)} %get-tuple-element.45), channel_id=1, source_target_pairs={{0,6},{2,0},{4,2},{6,4},{1,7},{3,1},{5,3},{7,5},{8,14},{10,8},{12,... | collective-permute-start | bytes 786440 | tf_op jit(solution)/shard_map/ppermute | solution.py:476
  84.4 7.8 %collective-permute-start.10 = (bf16[2,512,128]{2,1,0:T(8,128)(2,1)S(1)}, bf16[2,512,128]{2,1,0:T(8,128)(2,1)S(1)}, u32[]{:S(2)}, u32[]{:S(2)}) collective-permute-start(bf16[2,512,128]{2,1,0:T(8,128)(2,1)S(1)} %collective-permute-done.3.mine3_ref), channel_id=1, source_target_pairs={{0,1},{1,0},{2,3},{3,2},{4,5},{5,4},{6,7},{7,6},{8,9},{9,8},{10,11... | collective-permute-start | bytes 786440 | tf_op jit(solution)/shard_map/ppermute | solution.py:478
  115.6 5.4 %collective-permute-start.11 = (f32[2,2048,128]{2,1,0:T(8,128)}, f32[2,2048,128]{2,1,0:T(8,128)}, u32[]{:S(2)}, u32[]{:S(2)}) collective-permute-start(f32[2,2048,128]{2,1,0:T(8,128)} %get-tuple-element.34), channel_id=1, source_target_pairs={{0,1},{1,0},{2,3},{3,2},{4,5},{5,4},{6,7},{7,6},{8,9},{9,8},{10,11... | collective-permute-start | bytes 6291464 | tf_op jit(solution)/shard_map/ppermute | solution.py:512
  116.0 45.4 %all-to-all-start.1 = ((s16[16,528,128]{2,1,0:T(8,128)(2,1)}), s16[16,528,128]{2,1,0:T(8,128)(2,1)S(1)}, u32[]{:S(2)}, u32[]{:S(2)}) async-start(s16[16,528,128]{2,1,0:T(8,128)(2,1)} %get-tuple-element.32), calls=%async_computation.1 | async-start | bytes 4325376 | tf_op jit(solution)/shard_map/all_to_all | solution.py:514
  124.6 9.7 %collective-permute-start.12 = (s16[528,128]{1,0:T(8,128)(2,1)}, s16[528,128]{1,0:T(8,128)(2,1)S(1)}, u32[]{:S(2)}, u32[]{:S(2)}) collective-permute-start(s16[528,128]{1,0:T(8,128)(2,1)} %get-tuple-element.36), channel_id=1, source_target_pairs={{0,32},{32,64},{64,96},{96,128},{128,160},{160,192},{192,224},{224... | collective-permute-start | bytes 405512 | tf_op jit(solution)/shard_map/ppermute | solution.py:516
  124.7 12.9 %collective-permute-start.13 = (s16[528,128]{1,0:T(8,128)(2,1)}, s16[528,128]{1,0:T(8,128)(2,1)S(1)}, u32[]{:S(2)}, u32[]{:S(2)}) collective-permute-start(s16[528,128]{1,0:T(8,128)(2,1)} %get-tuple-element.37), channel_id=1, source_target_pairs={{0,64},{32,96},{64,128},{96,160},{128,192},{160,224},{192,0},{224,... | collective-permute-start | bytes 405512 | tf_op jit(solution)/shard_map/ppermute | solution.py:516
  124.8 17.1 %collective-permute-start.14 = (s16[528,128]{1,0:T(8,128)(2,1)}, s16[528,128]{1,0:T(8,128)(2,1)S(1)}, u32[]{:S(2)}, u32[]{:S(2)}) collective-permute-start(s16[528,128]{1,0:T(8,128)(2,1)} %get-tuple-element.38), channel_id=1, source_target_pairs={{0,96},{32,128},{64,160},{96,192},{128,224},{160,0},{192,32},{224,... | collective-permute-start | bytes 405512 | tf_op jit(solution)/shard_map/ppermute | solution.py:516
  129.9 16.8 %collective-permute-start.15 = (s16[528,128]{1,0:T(8,128)(2,1)}, s16[528,128]{1,0:T(8,128)(2,1)S(1)}, u32[]{:S(2)}, u32[]{:S(2)}) collective-permute-start(s16[528,128]{1,0:T(8,128)(2,1)} %get-tuple-element.39), channel_id=1, source_target_pairs={{0,128},{32,160},{64,192},{96,224},{128,0},{160,32},{192,64},{224,... | collective-permute-start | bytes 405512 | tf_op jit(solution)/shard_map/ppermute | solution.py:516
  130.3 21.6 %collective-permute-start.16 = (s16[528,128]{1,0:T(8,128)(2,1)}, s16[528,128]{1,0:T(8,128)(2,1)S(1)}, u32[]{:S(2)}, u32[]{:S(2)}) collective-permute-start(s16[528,128]{1,0:T(8,128)(2,1)} %get-tuple-element.40), channel_id=1, source_target_pairs={{0,160},{32,192},{64,224},{96,0},{128,32},{160,64},{192,96},{224,1... | collective-permute-start | bytes 405512 | tf_op jit(solution)/shard_map/ppermute | solution.py:516
  134.3 22.5 %collective-permute-start.17 = (s16[528,128]{1,0:T(8,128)(2,1)}, s16[528,128]{1,0:T(8,128)(2,1)S(1)}, u32[]{:S(2)}, u32[]{:S(2)}) collective-permute-start(s16[528,128]{1,0:T(8,128)(2,1)} %get-tuple-element.41), channel_id=1, source_target_pairs={{0,192},{32,224},{64,0},{96,32},{128,64},{160,96},{192,128},{224,1... | collective-permute-start | bytes 405512 | tf_op jit(solution)/shard_map/ppermute | solution.py:516
  137.7 19.1 %collective-permute-start.18 = (s16[528,128]{1,0:T(8,128)(2,1)}, s16[528,128]{1,0:T(8,128)(2,1)S(1)}, u32[]{:S(2)}, u32[]{:S(2)}) collective-permute-start(s16[528,128]{1,0:T(8,128)(2,1)} %get-tuple-element.42), channel_id=1, source_target_pairs={{0,224},{32,0},{64,32},{96,64},{128,96},{160,128},{192,160},{224,1... | collective-permute-start | bytes 405512 | tf_op jit(solution)/shard_map/ppermute | solution.py:516
  166.3 2.1 %collective-permute-start.20 = (f32[512,128]{1,0:T(8,128)}, f32[512,128]{1,0:T(8,128)S(1)}, u32[]{:S(2)}, u32[]{:S(2)}) collective-permute-start(f32[512,128]{1,0:T(8,128)} %combine.1.own_ref), channel_id=1, source_target_pairs={{0,1},{1,0},{2,3},{3,2},{4,5},{5,4},{6,7},{7,6},{8,9},{9,8},{10,11... | collective-permute-start | bytes 786440 | tf_op jit(solution)/shard_map/ppermute | solution.py:520
  177.0 16.8 %collective-permute-start.22 = (f32[64,128]{1,0:T(8,128)S(1)}, f32[64,128]{1,0:T(8,128)S(1)}, u32[]{:S(2)}, u32[]{:S(2)}) collective-permute-start(f32[64,128]{1,0:T(8,128)S(1)} %add.150.over0_ref), channel_id=1, source_target_pairs={{0,2},{2,4},{4,6},{6,0},{1,3},{3,5},{5,7},{7,1},{8,10},{10,12},{12... | collective-permute-start | bytes 98312 | tf_op jit(solution)/shard_map/ppermute | solution.py:444
  184.8 8.9 %collective-permute-start.23 = (f32[64,128]{1,0:T(8,128)S(1)}, f32[64,128]{1,0:T(8,128)S(1)}, u32[]{:S(2)}, u32[]{:S(2)}) collective-permute-start(f32[64,128]{1,0:T(8,128)S(1)} %add.150.over0_ref), channel_id=1, source_target_pairs={{0,4},{2,6},{4,0},{6,2},{1,5},{3,7},{5,1},{7,3},{8,12},{10,14},{12... | collective-permute-start | bytes 98312 | tf_op jit(solution)/shard_map/ppermute | solution.py:444
  191.8 3.0 %collective-permute-start.24 = (f32[64,128]{1,0:T(8,128)S(1)}, f32[64,128]{1,0:T(8,128)S(1)}, u32[]{:S(2)}, u32[]{:S(2)}) collective-permute-start(f32[64,128]{1,0:T(8,128)S(1)} %add.150.over0_ref), channel_id=1, source_target_pairs={{0,6},{2,0},{4,2},{6,4},{1,7},{3,1},{5,3},{7,5},{8,14},{10,8},{12,... | collective-permute-start | bytes 98312 | tf_op jit(solution)/shard_map/ppermute | solution.py:444
  (27 other events, 268.1 us)
Sparse Core Ops, SparseCore 0:
  22.1 37.2 all-gather.5
  61.2 54.7 all-gather.3

commit v4 on v3

--- a/solution.py
+++ b/solution.py
@@ -66,10 +66,7 @@
     return jnp.where(squared > 0, -exchange_fraction / safe, 0.0)
 
 
-def packed_slots(left_id, right_id):
-    m = left_id.astype(jnp.int32)
-    rest = right_id.astype(jnp.int32)
-    n, flip = rest & 31, rest >> 5
+def packed_slots(m, n, flip):
     mz, mx, nz, nx = m >> 2, m & 3, n >> 2, n & 3
     shared = 8 * flip + 16 * (m == n).astype(jnp.int32)
     first = (mz * 16 + nx * 4 + (nz >> 1)) | (mx + 4 * (nz & 1) + shared) << 7
@@ -87,8 +84,6 @@
     lax.fori_loop(0, NZ * NX * NY, clear, 0, unroll=8)
 
     def one_block(b, count):
-        row = ((me_ref[1] - (b & 3)) & 3) * NZ + (b >> 2)
-
         def step(state):
             s, slot, cnt = state
             first = slot & 127
@@ -99,10 +94,10 @@
             chip = jnp.where(use_a, first, second)
             load_ref[chip] = jnp.minimum(load_a, load_b) + 1
             out_ref[1 + cnt] = jnp.where(use_a, slot >> 7, slot >> 23) & 31
-            slot = jnp.where(s < 31, slots_ref[row, jnp.minimum(s + 1, 31)], -1)
+            slot = jnp.where(s < 31, slots_ref[b, jnp.minimum(s + 1, 31)], -1)
             return s + 1, slot, cnt + (chip == me).astype(jnp.int32)
 
-        return lax.while_loop(lambda state: state[1] >= 0, step, (0, slots_ref[row, 0], count))[2]
+        return lax.while_loop(lambda state: state[1] >= 0, step, (0, slots_ref[b, 0], count))[2]
 
     out_ref[0] = lax.fori_loop(0, 32, one_block, 0)
 
@@ -447,19 +442,15 @@
 def local(orbitals, pair_table):
     z, x, y, core = (lax.axis_index(a) for a in ("z", "x", "y", "core"))
     mine = orbitals[0]
-    slots = jnp.concatenate([pair_table[:, 0], pair_table[:, 1] + 32 * pair_table[:, 2]])
-    slots = jnp.pad(slots.astype(bf16)[None], ((0, 15), (0, 64)))
-    z_couples = jnp.concatenate([mine.reshape(512, 128), slots], axis=0)[None]
-    z_couples = lax.all_gather(z_couples, "z", axis=0, tiled=True)
+    slots = packed_slots(pair_table[:, 0], pair_table[:, 1], pair_table[:, 2])
+    slots = lax.all_gather(slots[None], ("z", "x"), axis=0, tiled=True)
+    z_couples = lax.all_gather(mine.reshape(1, 512, 128), "z", axis=0, tiled=True)
     own = lane_exchange(mine, core)
     spread = jnp.broadcast_to(own[None], (NX * NY,) + own.shape)
     left = lax.all_to_all(spread, ("x", "y"), split_axis=0, concat_axis=0, tiled=True)
 
-    z_couples, left = lax.optimization_barrier((z_couples, left))
-    slots = z_couples[:, 512, :]
-    slots = jnp.concatenate([slots] + [lax.ppermute(slots, "x", ring(NX, k)) for k in range(1, NX)])
-    slots = packed_slots(slots[:, :32], slots[:, 32:64])
-    me = jnp.stack([z * 16 + x * 4 + y, x]).astype(jnp.int32)
+    z_couples, left, slots = lax.optimization_barrier((z_couples, left, slots))
+    me = (z * 16 + x * 4 + y).astype(jnp.int32).reshape(1)
     tasks = pl.pallas_call(
         assign_kernel,
         out_shape=jax.ShapeDtypeStruct((18,), jnp.int32),

time: 209 us -> 202 us (0.967)
  blocking collectives: 0 us -> 40.8 us
  waiting for transfers between devices: 61.5 us -> 24.5 us
  starting transfers between devices: 63.9 us -> 55.6 us
  other arithmetic: 6.47 us -> 3.08 us
    unnamed x0 -> x1, blocking collectives: none -> 40.8 us
    all_gather x1, waiting for transfers between devices: 39.2 us -> 0.01 us  [local(): lax.all_gather(mine.reshape(1, 512, 128), 'z', axis=0, tiled=True)]
    ppermute x3 -> x0, starting transfers between devices: 5.14 us -> none  [local(): lax.ppermute(slots, 'x', ring(NX, k))]
    ppermute x7, starting transfers between devices: 14.5 us -> 12.3 us  [local(): lax.ppermute(part, 'z', ring(NZ, k))]
    unnamed x45 -> x48, local copies, waits for them, and re-layouts: 6.07 us -> 6.72 us
  transfers between devices with their start and end apart: 29 -> 26, of which waited for: 11 -> 11; matrix products, arithmetic and copies ran while one was open for 4% -> 3% of each run, Pallas kernels for 19% -> 20%
where the time goes in v4:
time: 202 us; the launch traced here: 201 us
  starting transfers between devices  55.6 us (28%)
  Pallas kernels  50.3 us (25%)
  blocking collectives  40.8 us (20%)
  waiting for transfers between devices  24.5 us (12%)
  between operations  14.4 us (7%)
  local copies, waits for them, and re-layouts  12.2 us (6%)
  other arithmetic  3.08 us (2%)
    unnamed x1, blocking collectives  40.8 us
    pallas_call x1, Pallas kernels, local(): pl.pallas_call(pairs_kernel, out_shape=(jax.ShapeDtypeStruct((NX * NY, 52...  20.2 us
    ppermute x7, waiting for transfers between devices, local(): lax.ppermute(part, 'z', ring(NZ, k))  17.9 us
    ppermute x3, starting transfers between devices, over_y(): lax.ppermute(value, 'y', ring(NY, k))  17.1 us
    ppermute x7, starting transfers between devices, local(): lax.ppermute(part, 'z', ring(NZ, k))  12.3 us
    pallas_call x1, Pallas kernels, local(): pl.pallas_call(assign_kernel, out_shape=jax.ShapeDtypeStruct((18,), jnp.i...  10.8 us
    ppermute x4, starting transfers between devices, local(): right_other = [lax.ppermute(part, 'core', ring(2, 1)) for part in right]  6.92 us
    unnamed x48, local copies, waits for them, and re-layouts  6.72 us
  transfers between devices with their start and end apart: 26, of which 11 were waited for; matrix products, arithmetic and copies ran while one was open for 3% of the time, Pallas kernels for 20%

profile of v4, /device:TPU:1, one launch (start us, length us, event | category | flops | bytes accessed | tf_op | source)
XLA Modules:
  0.0 200.8 jit_solution(12351110178550740062)
XLA Ops:
  6.5 3.2 %collective-permute-start = (bf16[8,64,128]{2,1,0:T(8,128)(2,1)}, bf16[8,64,128]{2,1,0:T(8,128)(2,1)S(1)}, u32[]{:S(2)}, u32[]{:S(2)}) collective-permute-start(bf16[8,64,128]{2,1,0:T(8,128)(2,1)} %bitcast.23), channel_id=1, source_target_pairs={{0,1},{1,0},{2,3},{3,2},{4,5},{5,4},{6,7},{7,6},{8,9},{9,8},{10,11... | collective-permute-start | bytes 393224 | tf_op jit(solution)/shard_map/ppermute | solution.py:419
  12.1 1.9 broadcast_in_dim.19
  14.0 5.2 %all-to-all-start = ((bf16[16,8,64,128]{3,2,1,0:T(8,128)(2,1)}), bf16[16,8,64,128]{3,2,1,0:T(8,128)(2,1)S(1)}, u32[]{:S(2)}, u32[]{:S(2)}) async-start(bf16[16,8,64,128]{3,2,1,0:T(8,128)(2,1)} %broadcast_in_dim.19), calls=%async_computation | async-start | bytes 4194304 | tf_op jit(solution)/shard_map/all_to_all | solution.py:450
  21.3 40.8 %all-reduce = s32[1024]{0:T(1024)S(1)} all-reduce(s32[1024]{0:T(1024)S(1)} %fusion.21), channel_id=2, replica_groups=mesh['z'=8,'x'=4,'y'=4,'core'=2] {'z','x'}, use_global_device_ids=true, to_apply=%add | all-reduce | flops 1024 | bytes 8192
  63.0 2.8 %constant_dynamic-slice_fusion = (bf16[2,512,128]{2,1,0:T(8,128)(2,1)}, bf16[2,512,128]{2,1,0:T(8,128)(2,1)}, bf16[2,512,128]{2,1,0:T(8,128)(2,1)}, bf16[2,512,128]{2,1,0:T(8,128)(2,1)S(1)}) fusion(bf16[8,512,128]{2,1,0:T(8,128)(2,1)} %all-gather.4.cloned.1.call-done, s32[]{:T(128)S(6)} %select_n.88, s32[]{:T(128)S(6)} %select_n.86, s32[]{:T(128)S(6)} %select_n.84, ...), kind=kLoop, calls=%fused_computation.50 | loop fusion | bytes 2097168 | tf_op jit(solution)/shard_map/dynamic_slice | solution.py:466
  68.5 10.8 %assign.1.tasks_ref = s32[18]{0:T(128)} custom-call(s32[1]{0:T(128)} %bitcast.9.me_ref, s32[32,32]{1,0:T(8,128)} %reshape.231.slots_ref), custom_call_target="tpu_custom_call" | custom-call | bytes 60000000 | tf_op jit(solution)/shard_map/assign/pallas_call | solution.py:454
  79.3 6.3 %collective-permute-start.4 = (bf16[2,512,128]{2,1,0:T(8,128)(2,1)S(1)}, bf16[2,512,128]{2,1,0:T(8,128)(2,1)S(1)}, u32[]{:S(2)}, u32[]{:S(2)}) collective-permute-start(bf16[2,512,128]{2,1,0:T(8,128)(2,1)S(1)} %get-tuple-element.30.mine0_ref), channel_id=1, source_target_pairs={{0,1},{1,0},{2,3},{3,2},{4,5},{5,4},{6,7},{7,6},{8,9},{9,8},{10,11... | collective-permute-start | bytes 786440 | tf_op jit(solution)/shard_map/ppermute | solution.py:469
  88.6 20.2 %pairs.1 = (s16[16,528,128]{2,1,0:T(8,128)(2,1)}, f32[2,2048,128]{2,1,0:T(8,128)S(1)}, f32[2,2048,128]{2,1,0:T(8,128)}) custom-call(s32[2]{0:T(128)S(1)} %pad_add_fusion.ids_ref.core_ref, s32[18]{0:T(128)S(1)} %copy-done.5, bf16[4,2048,128]{2,1,0:T(8,128)(2,1)} %bitcast.22, bf16[2,512,128]{2,1,0:T(8,128)(2,1)S(1)} %get-tuple-element.30.mine0_ref, ...), custom_call_target="tpu_custom_call" | custom-call | bytes 60000000 | tf_op jit(solution)/shard_map/pairs/pallas_call | solution.py:473
  110.5 5.4 %all-to-all-start.1 = ((s16[16,528,128]{2,1,0:T(8,128)(2,1)}), s16[16,528,128]{2,1,0:T(8,128)(2,1)S(1)}, u32[]{:S(2)}, u32[]{:S(2)}) async-start(s16[16,528,128]{2,1,0:T(8,128)(2,1)} %get-tuple-element.34), calls=%async_computation.1 | async-start | bytes 4325376 | tf_op jit(solution)/shard_map/all_to_all | solution.py:505
  116.5 3.7 %quantize_right.1 = (s16[528,128]{1,0:T(8,128)(2,1)}, s16[528,128]{1,0:T(8,128)(2,1)}, s16[528,128]{1,0:T(8,128)(2,1)}, s16[528,128]{1,0:T(8,128)(2,1)}, s16[528...) custom-call(s32[2]{0:T(128)} %pad_add_fusion.1.zy_ref, ...), custom_call_target="tpu_custom_call" | custom-call | bytes 8000000 | tf_op jit(solution)/shard_map/quantize_right/pallas_call | solution.py:335
  120.9 3.6 %collective-permute-start.12 = (s16[528,128]{1,0:T(8,128)(2,1)}, s16[528,128]{1,0:T(8,128)(2,1)S(1)}, u32[]{:S(2)}, u32[]{:S(2)}) collective-permute-start(s16[528,128]{1,0:T(8,128)(2,1)} %get-tuple-element.41), channel_id=1, source_target_pairs={{0,128},{32,160},{64,192},{96,224},{128,0},{160,32},{192,64},{224,... | collective-permute-start | bytes 405512 | tf_op jit(solution)/shard_map/ppermute | solution.py:507
  124.6 2.6 %collective-permute-start.13 = (s16[528,128]{1,0:T(8,128)(2,1)}, s16[528,128]{1,0:T(8,128)(2,1)S(1)}, u32[]{:S(2)}, u32[]{:S(2)}) collective-permute-start(s16[528,128]{1,0:T(8,128)(2,1)} %get-tuple-element.42), channel_id=1, source_target_pairs={{0,160},{32,192},{64,224},{96,0},{128,32},{160,64},{192,96},{224,1... | collective-permute-start | bytes 405512 | tf_op jit(solution)/shard_map/ppermute | solution.py:507
  128.2 3.3 %collective-permute-done.10.refs_2_ = s16[528,128]{1,0:T(8,128)(2,1)S(1)} collective-permute-done((s16[528,128]{1,0:T(8,128)(2,1)}, s16[528,128]{1,0:T(8,128)(2,1)S(1)}, u32[]{:S(2)}, u32[]{:S(2)}) %collective-permute-start.10) | collective-permute-done | bytes 135200 | tf_op jit(solution)/shard_map/ppermute | solution.py:507
  131.6 4.2 %collective-permute-start.9 = (s16[528,128]{1,0:T(8,128)(2,1)}, s16[528,128]{1,0:T(8,128)(2,1)S(1)}, u32[]{:S(2)}, u32[]{:S(2)}) collective-permute-start(s16[528,128]{1,0:T(8,128)(2,1)} %get-tuple-element.38), channel_id=1, source_target_pairs={{0,32},{32,64},{64,96},{96,128},{128,160},{160,192},{192,224},{224... | collective-permute-start | bytes 405512 | tf_op jit(solution)/shard_map/ppermute | solution.py:507
  135.8 7.1 %collective-permute-done.12.refs_4_ = s16[528,128]{1,0:T(8,128)(2,1)S(1)} collective-permute-done((s16[528,128]{1,0:T(8,128)(2,1)}, s16[528,128]{1,0:T(8,128)(2,1)S(1)}, u32[]{:S(2)}, u32[]{:S(2)}) %collective-permute-start.12) | collective-permute-done | bytes 135200 | tf_op jit(solution)/shard_map/ppermute | solution.py:507
  142.9 4.6 %collective-permute-done.14.refs_6_ = s16[528,128]{1,0:T(8,128)(2,1)S(1)} collective-permute-done((s16[528,128]{1,0:T(8,128)(2,1)}, s16[528,128]{1,0:T(8,128)(2,1)S(1)}, u32[]{:S(2)}, u32[]{:S(2)}) %collective-permute-start.14) | collective-permute-done | bytes 135200 | tf_op jit(solution)/shard_map/ppermute | solution.py:507
  147.5 2.8 %collective-permute-done.15.refs_7_ = s16[528,128]{1,0:T(8,128)(2,1)S(1)} collective-permute-done((s16[528,128]{1,0:T(8,128)(2,1)}, s16[528,128]{1,0:T(8,128)(2,1)S(1)}, u32[]{:S(2)}, u32[]{:S(2)}) %collective-permute-start.15) | collective-permute-done | bytes 135200 | tf_op jit(solution)/shard_map/ppermute | solution.py:507
  151.0 2.3 %combine_right.1 = s16[528,128]{1,0:T(8,128)(2,1)} custom-call(s16[528,128]{1,0:T(8,128)(2,1)} %get-tuple-element.37.refs_0_, s16[528,128]{1,0:T(8,128)(2,1)} %copy-done.15, s16[528,128]{1,0:T(8,128)(2,1)} %copy-done.9, s16[528,128]{1,0:T(8,128)(2,1)} %copy-done.10, s16[528,128]{1,0:T(8,128)(2,1)} %copy-done.11, s16[528,128]{1,0:T(8,128)(2,1)} %copy-done.12, ...), custom_call_target="tpu_custom_call" | custom-call | bytes 6000000 | tf_op jit(solution)/shard_map/combine_right/pallas_call | solution.py:356
  153.4 1.6 collective-permute-start.16
  157.0 2.9 %combine.1.own_ref = f32[512,128]{1,0:T(8,128)} custom-call(s16[16,528,128]{2,1,0:T(8,128)(2,1)} %copy-done.6, s16[528,128]{1,0:T(8,128)(2,1)} %copy-done.16), custom_call_target="tpu_custom_call" | custom-call | tf_op jit(solution)/shard_map/combine/pallas_call | solution.py:346
  162.5 5.6 %overlap.1 = (f32[512,128]{1,0:T(8,128)}, f32[64,128]{1,0:T(8,128)}) custom-call(s32[2]{0:T(128)} %copy-done.4, f32[512,128]{1,0:T(8,128)} %combine.1.own_ref, f32[512,128]{1,0:T(8,128)} %copy-done.8, bf16[32,512,128]{2,1,0:T(8,128)(2,1)} %all-gather.6.cloned.1.call-done.phi_ref), custom_call_target="tpu_custom_call" | custom-call | tf_op jit(solution)/shard_map/overlap/pallas_call | solution.py:513
  170.3 13.9 %collective-permute-start.19 = (f32[64,128]{1,0:T(8,128)S(1)}, f32[64,128]{1,0:T(8,128)S(1)}, u32[]{:S(2)}, u32[]{:S(2)}) collective-permute-start(f32[64,128]{1,0:T(8,128)S(1)} %add.212.over0_ref), channel_id=1, source_target_pairs={{0,2},{2,4},{4,6},{6,0},{1,3},{3,5},{5,7},{7,1},{8,10},{10,12},{12... | collective-permute-start | bytes 98312 | tf_op jit(solution)/shard_map/ppermute | solution.py:439
  185.6 1.8 collective-permute-start.21
  189.1 4.8 %project.1 = f32[512,128]{1,0:T(8,128)} custom-call(f32[512,128]{1,0:T(8,128)} %get-tuple-element.45.x_ref, bf16[32,512,128]{2,1,0:T(8,128)(2,1)} %all-gather.6.cloned.1.call-done.phi_ref, f32[64,128]{1,0:T(8,128)} %copy-done.17, f32[64,128]{1,0:T(8,128)} %copy-done.18, f32[64,128]{1,0:T(8,128)} %copy-done.19, f32[64,128]{1,0:T(8,128)} %copy-done.20), custom_call_target="tpu_custom_call" | custom-call | tf_op jit(solution)/shard_map/project/pallas_call | solution.py:524
  (106 shorter events, 25.0 us)
Async XLA Ops:
  6.5 4.4 %collective-permute-start = (bf16[8,64,128]{2,1,0:T(8,128)(2,1)}, bf16[8,64,128]{2,1,0:T(8,128)(2,1)S(1)}, u32[]{:S(2)}, u32[]{:S(2)}) collective-permute-start(bf16[8,64,128]{2,1,0:T(8,128)(2,1)} %bitcast.23), channel_id=1, source_target_pairs={{0,1},{1,0},{2,3},{3,2},{4,5},{5,4},{6,7},{7,6},{8,9},{9,8},{10,11... | collective-permute-start | bytes 393224 | tf_op jit(solution)/shard_map/ppermute | solution.py:419
  14.0 48.8 %all-to-all-start = ((bf16[16,8,64,128]{3,2,1,0:T(8,128)(2,1)}), bf16[16,8,64,128]{3,2,1,0:T(8,128)(2,1)S(1)}, u32[]{:S(2)}, u32[]{:S(2)}) async-start(bf16[16,8,64,128]{3,2,1,0:T(8,128)(2,1)} %broadcast_in_dim.19), calls=%async_computation | async-start | bytes 4194304 | tf_op jit(solution)/shard_map/all_to_all | solution.py:450
  19.2 43.6 %all-gather.4.cloned.1.call-start = ((), (), s32[]{:S(2)}) async-start(), calls=%async_computation.2 | async-start | bytes 1179648 | tf_op jit(solution)/shard_map/all_gather | solution.py:447
  19.9 141.9 %all-gather.6.cloned.1.call-start = ((), (), s32[]{:S(2)}) async-start(), calls=%async_computation.3 | async-start | bytes 5242880 | tf_op jit(solution)/shard_map/all_gather | solution.py:463
  65.8 13.5 %collective-permute-start.1 = (bf16[2,512,128]{2,1,0:T(8,128)(2,1)}, bf16[2,512,128]{2,1,0:T(8,128)(2,1)S(1)}, u32[]{:S(2)}, u32[]{:S(2)}) collective-permute-start(bf16[2,512,128]{2,1,0:T(8,128)(2,1)} %get-tuple-element.49), channel_id=1, source_target_pairs={{0,2},{2,4},{4,6},{6,0},{1,3},{3,5},{5,7},{7,1},{8,10},{10,12},{12... | collective-permute-start | bytes 786440 | tf_op jit(solution)/shard_map/ppermute | solution.py:467
  66.0 13.3 %collective-permute-start.2 = (bf16[2,512,128]{2,1,0:T(8,128)(2,1)}, bf16[2,512,128]{2,1,0:T(8,128)(2,1)S(1)}, u32[]{:S(2)}, u32[]{:S(2)}) collective-permute-start(bf16[2,512,128]{2,1,0:T(8,128)(2,1)} %get-tuple-element.48), channel_id=1, source_target_pairs={{0,4},{2,6},{4,0},{6,2},{1,5},{3,7},{5,1},{7,3},{8,12},{10,14},{12... | collective-permute-start | bytes 786440 | tf_op jit(solution)/shard_map/ppermute | solution.py:467
  67.3 12.0 %collective-permute-start.3 = (bf16[2,512,128]{2,1,0:T(8,128)(2,1)}, bf16[2,512,128]{2,1,0:T(8,128)(2,1)S(1)}, u32[]{:S(2)}, u32[]{:S(2)}) collective-permute-start(bf16[2,512,128]{2,1,0:T(8,128)(2,1)} %get-tuple-element.47), channel_id=1, source_target_pairs={{0,6},{2,0},{4,2},{6,4},{1,7},{3,1},{5,3},{7,5},{8,14},{10,8},{12,... | collective-permute-start | bytes 786440 | tf_op jit(solution)/shard_map/ppermute | solution.py:467
  79.3 7.5 %collective-permute-start.4 = (bf16[2,512,128]{2,1,0:T(8,128)(2,1)S(1)}, bf16[2,512,128]{2,1,0:T(8,128)(2,1)S(1)}, u32[]{:S(2)}, u32[]{:S(2)}) collective-permute-start(bf16[2,512,128]{2,1,0:T(8,128)(2,1)S(1)} %get-tuple-element.30.mine0_ref), channel_id=1, source_target_pairs={{0,1},{1,0},{2,3},{3,2},{4,5},{5,4},{6,7},{7,6},{8,9},{9,8},{10,11... | collective-permute-start | bytes 786440 | tf_op jit(solution)/shard_map/ppermute | solution.py:469
  85.7 1.8 collective-permute-start.6
  86.1 1.8 collective-permute-start.7
  110.1 6.3 %collective-permute-start.8 = (f32[2,2048,128]{2,1,0:T(8,128)}, f32[2,2048,128]{2,1,0:T(8,128)}, u32[]{:S(2)}, u32[]{:S(2)}) collective-permute-start(f32[2,2048,128]{2,1,0:T(8,128)} %get-tuple-element.36), channel_id=1, source_target_pairs={{0,1},{1,0},{2,3},{3,2},{4,5},{5,4},{6,7},{7,6},{8,9},{9,8},{10,11... | collective-permute-start | bytes 6291464 | tf_op jit(solution)/shard_map/ppermute | solution.py:503
  110.5 44.4 %all-to-all-start.1 = ((s16[16,528,128]{2,1,0:T(8,128)(2,1)}), s16[16,528,128]{2,1,0:T(8,128)(2,1)S(1)}, u32[]{:S(2)}, u32[]{:S(2)}) async-start(s16[16,528,128]{2,1,0:T(8,128)(2,1)} %get-tuple-element.34), calls=%async_computation.1 | async-start | bytes 4325376 | tf_op jit(solution)/shard_map/all_to_all | solution.py:505
  120.1 11.4 %collective-permute-start.10 = (s16[528,128]{1,0:T(8,128)(2,1)}, s16[528,128]{1,0:T(8,128)(2,1)S(1)}, u32[]{:S(2)}, u32[]{:S(2)}) collective-permute-start(s16[528,128]{1,0:T(8,128)(2,1)} %get-tuple-element.39), channel_id=1, source_target_pairs={{0,64},{32,96},{64,128},{96,160},{128,192},{160,224},{192,0},{224,... | collective-permute-start | bytes 405512 | tf_op jit(solution)/shard_map/ppermute | solution.py:507
  120.1 11.4 %collective-permute-start.11 = (s16[528,128]{1,0:T(8,128)(2,1)}, s16[528,128]{1,0:T(8,128)(2,1)S(1)}, u32[]{:S(2)}, u32[]{:S(2)}) collective-permute-start(s16[528,128]{1,0:T(8,128)(2,1)} %get-tuple-element.40), channel_id=1, source_target_pairs={{0,96},{32,128},{64,160},{96,192},{128,224},{160,0},{192,32},{224,... | collective-permute-start | bytes 405512 | tf_op jit(solution)/shard_map/ppermute | solution.py:507
  120.9 22.0 %collective-permute-start.12 = (s16[528,128]{1,0:T(8,128)(2,1)}, s16[528,128]{1,0:T(8,128)(2,1)S(1)}, u32[]{:S(2)}, u32[]{:S(2)}) collective-permute-start(s16[528,128]{1,0:T(8,128)(2,1)} %get-tuple-element.41), channel_id=1, source_target_pairs={{0,128},{32,160},{64,192},{96,224},{128,0},{160,32},{192,64},{224,... | collective-permute-start | bytes 405512 | tf_op jit(solution)/shard_map/ppermute | solution.py:507
  124.6 18.3 %collective-permute-start.13 = (s16[528,128]{1,0:T(8,128)(2,1)}, s16[528,128]{1,0:T(8,128)(2,1)S(1)}, u32[]{:S(2)}, u32[]{:S(2)}) collective-permute-start(s16[528,128]{1,0:T(8,128)(2,1)} %get-tuple-element.42), channel_id=1, source_target_pairs={{0,160},{32,192},{64,224},{96,0},{128,32},{160,64},{192,96},{224,1... | collective-permute-start | bytes 405512 | tf_op jit(solution)/shard_map/ppermute | solution.py:507
  127.2 20.3 %collective-permute-start.14 = (s16[528,128]{1,0:T(8,128)(2,1)}, s16[528,128]{1,0:T(8,128)(2,1)S(1)}, u32[]{:S(2)}, u32[]{:S(2)}) collective-permute-start(s16[528,128]{1,0:T(8,128)(2,1)} %get-tuple-element.43), channel_id=1, source_target_pairs={{0,192},{32,224},{64,0},{96,32},{128,64},{160,96},{192,128},{224,1... | collective-permute-start | bytes 405512 | tf_op jit(solution)/shard_map/ppermute | solution.py:507
  131.5 18.8 %collective-permute-start.15 = (s16[528,128]{1,0:T(8,128)(2,1)}, s16[528,128]{1,0:T(8,128)(2,1)S(1)}, u32[]{:S(2)}, u32[]{:S(2)}) collective-permute-start(s16[528,128]{1,0:T(8,128)(2,1)} %get-tuple-element.44), channel_id=1, source_target_pairs={{0,224},{32,0},{64,32},{96,64},{128,96},{160,128},{192,160},{224,1... | collective-permute-start | bytes 405512 | tf_op jit(solution)/shard_map/ppermute | solution.py:507
  131.6 18.8 %collective-permute-start.9 = (s16[528,128]{1,0:T(8,128)(2,1)}, s16[528,128]{1,0:T(8,128)(2,1)S(1)}, u32[]{:S(2)}, u32[]{:S(2)}) collective-permute-start(s16[528,128]{1,0:T(8,128)(2,1)} %get-tuple-element.38), channel_id=1, source_target_pairs={{0,32},{32,64},{64,96},{96,128},{128,160},{160,192},{192,224},{224... | collective-permute-start | bytes 405512 | tf_op jit(solution)/shard_map/ppermute | solution.py:507
  153.4 1.6 collective-permute-start.16
  159.9 1.9 collective-permute-start.17
  170.3 17.1 %collective-permute-start.19 = (f32[64,128]{1,0:T(8,128)S(1)}, f32[64,128]{1,0:T(8,128)S(1)}, u32[]{:S(2)}, u32[]{:S(2)}) collective-permute-start(f32[64,128]{1,0:T(8,128)S(1)} %add.212.over0_ref), channel_id=1, source_target_pairs={{0,2},{2,4},{4,6},{6,0},{1,3},{3,5},{5,7},{7,1},{8,10},{10,12},{12... | collective-permute-start | bytes 98312 | tf_op jit(solution)/shard_map/ppermute | solution.py:439
  184.2 4.3 %collective-permute-start.20 = (f32[64,128]{1,0:T(8,128)S(1)}, f32[64,128]{1,0:T(8,128)S(1)}, u32[]{:S(2)}, u32[]{:S(2)}) collective-permute-start(f32[64,128]{1,0:T(8,128)S(1)} %add.212.over0_ref), channel_id=1, source_target_pairs={{0,4},{2,6},{4,0},{6,2},{1,5},{3,7},{5,1},{7,3},{8,12},{10,14},{12... | collective-permute-start | bytes 98312 | tf_op jit(solution)/shard_map/ppermute | solution.py:439
  185.6 2.9 %collective-permute-start.21 = (f32[64,128]{1,0:T(8,128)S(1)}, f32[64,128]{1,0:T(8,128)S(1)}, u32[]{:S(2)}, u32[]{:S(2)}) collective-permute-start(f32[64,128]{1,0:T(8,128)S(1)} %add.212.over0_ref), channel_id=1, source_target_pairs={{0,6},{2,0},{4,2},{6,4},{1,7},{3,1},{5,3},{7,5},{8,14},{10,8},{12,... | collective-permute-start | bytes 98312 | tf_op jit(solution)/shard_map/ppermute | solution.py:439
  (25 other events, 219.4 us)
Sparse Core Ops, SparseCore 0:
  21.8 37.5 all-gather.3
  63.0 51.7 all-gather.5

commit v5 on v4

--- a/solution.py
+++ b/solution.py
@@ -446,10 +446,10 @@
     slots = lax.all_gather(slots[None], ("z", "x"), axis=0, tiled=True)
     z_couples = lax.all_gather(mine.reshape(1, 512, 128), "z", axis=0, tiled=True)
     own = lane_exchange(mine, core)
+    own, slots = lax.optimization_barrier((own, slots))
     spread = jnp.broadcast_to(own[None], (NX * NY,) + own.shape)
     left = lax.all_to_all(spread, ("x", "y"), split_axis=0, concat_axis=0, tiled=True)
 
-    z_couples, left, slots = lax.optimization_barrier((z_couples, left, slots))
     me = (z * 16 + x * 4 + y).astype(jnp.int32).reshape(1)
     tasks = pl.pallas_call(
         assign_kernel,
@@ -460,12 +460,12 @@
         cost_estimate=pl.CostEstimate(flops=0, bytes_accessed=60 * 1000 * 1000, transcendentals=0),
         name="assign",
     )(me, slots)
+    z_couples, tasks = lax.optimization_barrier((z_couples, tasks))
     phi_all = lax.all_gather(z_couples, "x", axis=0, tiled=True)
     right = []
     for k in range(NY):
         part = lax.dynamic_slice(z_couples, (2 * ((y + k) % NY), 0, 0), (2, 512, 128))
         right.append(lax.ppermute(part, "y", ring(NY, k)) if k else part)
-    *right, tasks = lax.optimization_barrier((*right, tasks))
     right_other = [lax.ppermute(part, "core", ring(2, 1)) for part in right]
     ids = jnp.stack([core, y]).astype(jnp.int32)
 

time: 202 us -> 217 us (1.074)
  starting transfers between devices: 55.6 us -> 79.6 us
  blocking collectives: 40.8 us -> 17.1 us
  waiting for transfers between devices: 24.5 us -> 43.4 us
  Pallas kernels: 50.3 us -> 47.6 us
  local copies, waits for them, and re-layouts: 12.2 us -> 9.52 us
    unnamed x1, blocking collectives: 40.8 us -> 17.1 us
    ppermute x3, waiting for transfers between devices: 0.01 us -> 16 us  [local(): right.append(lax.ppermute(part, 'y', ring(NY, k)) if k else part)]
    ppermute x4, starting transfers between devices: 6.92 us -> 14.7 us  [local(): right_other = [lax.ppermute(part, 'core', ring(2, 1)) for part in right]]
    all_to_all x1, starting transfers between devices: 5.35 us -> 13 us  [local(): lax.all_to_all(left_parts, ('x', 'y'), split_axis=0, concat_axis=0, tiled...]
    ppermute x1, starting transfers between devices: 0.37 us -> 5.61 us  [local(): other = lax.ppermute(cacc, 'core', ring(2, 1))]
    all_gather x1, waiting for transfers between devices: 0.01 us -> 4.21 us  [local(): lax.all_gather(mine.reshape(1, 512, 128), 'z', axis=0, tiled=True)]
    dynamic_slice x1, local copies, waits for them, and re-layouts: 2.81 us -> 0.08 us  [local(): lax.dynamic_slice(z_couples, (2 * ((y + k) % NY), 0, 0), (2, 512, 128))]
    pallas_call x1, Pallas kernels: 20.2 us -> 17.5 us  [local(): pl.pallas_call(pairs_kernel, out_shape=(jax.ShapeDtypeStruct((NX * NY, 52...]
  transfers between devices with their start and end apart: 26 -> 26, of which waited for: 11 -> 10; matrix products, arithmetic and copies ran while one was open for 3% -> 3% of each run, Pallas kernels for 20% -> 17%
where the time goes in v5:
time: 217 us; the launch traced here: 216 us
  starting transfers between devices  79.6 us (37%)
  Pallas kernels  47.6 us (22%)
  waiting for transfers between devices  43.4 us (20%)
  blocking collectives  17.1 us (8%)
  between operations  14.4 us (7%)
  local copies, waits for them, and re-layouts  9.52 us (4%)
  other arithmetic  3.93 us (2%)
    pallas_call x1, Pallas kernels, local(): pl.pallas_call(pairs_kernel, out_shape=(jax.ShapeDtypeStruct((NX * NY, 52...  17.5 us
    ppermute x7, waiting for transfers between devices, local(): lax.ppermute(part, 'z', ring(NZ, k))  17.4 us
    unnamed x1, blocking collectives  17.1 us
    ppermute x3, starting transfers between devices, over_y(): lax.ppermute(value, 'y', ring(NY, k))  16 us
    ppermute x3, waiting for transfers between devices, local(): right.append(lax.ppermute(part, 'y', ring(NY, k)) if k else part)  16 us
    ppermute x4, starting transfers between devices, local(): right_other = [lax.ppermute(part, 'core', ring(2, 1)) for part in right]  14.7 us
    all_to_all x1, starting transfers between devices, local(): lax.all_to_all(left_parts, ('x', 'y'), split_axis=0, concat_axis=0, tiled...  13 us
    ppermute x7, starting transfers between devices, local(): lax.ppermute(part, 'z', ring(NZ, k))  12.1 us
  transfers between devices with their start and end apart: 26, of which 10 were waited for; matrix products, arithmetic and copies ran while one was open for 3% of the time, Pallas kernels for 17%

profile of v5, /device:TPU:1, one launch (start us, length us, event | category | flops | bytes accessed | tf_op | source)
XLA Modules:
  0.0 215.5 jit_solution(4863080822768095302)
XLA Ops:
  7.3 3.3 %collective-permute-start = (bf16[8,64,128]{2,1,0:T(8,128)(2,1)}, bf16[8,64,128]{2,1,0:T(8,128)(2,1)S(1)}, u32[]{:S(2)}, u32[]{:S(2)}) collective-permute-start(bf16[8,64,128]{2,1,0:T(8,128)(2,1)} %bitcast.18), channel_id=1, source_target_pairs={{0,1},{1,0},{2,3},{3,2},{4,5},{5,4},{6,7},{7,6},{8,9},{9,8},{10,11... | collective-permute-start | bytes 393224 | tf_op jit(solution)/shard_map/ppermute | solution.py:419
  13.5 17.1 %all-reduce = s32[1024]{0:T(1024)S(1)} all-reduce(s32[1024]{0:T(1024)S(1)} %fusion.20), channel_id=2, replica_groups=mesh['z'=8,'x'=4,'y'=4,'core'=2] {'z','x'}, use_global_device_ids=true, to_apply=%add | all-reduce | flops 1024 | bytes 8192
  32.4 10.8 %assign.1.tasks_ref = s32[18]{0:T(128)} custom-call(s32[1]{0:T(128)} %bitcast.3.me_ref, s32[32,32]{1,0:T(8,128)} %reshape.230.slots_ref), custom_call_target="tpu_custom_call" | custom-call | bytes 60000000 | tf_op jit(solution)/shard_map/assign/pallas_call | solution.py:454
  43.2 4.2 %all-gather.4.cloned.1.call-done = bf16[8,512,128]{2,1,0:T(8,128)(2,1)} async-done(((bf16[1,512,128]{2,1,0:T(8,128)(2,1)}), bf16[8,512,128]{2,1,0:T(8,128)(2,1)}) %all-gather.4.cloned.1.call-update) | async-done | bytes 1048592 | tf_op jit(solution)/shard_map/all_gather | solution.py:447
  49.3 6.6 %all-to-all-start = ((bf16[16,8,64,128]{3,2,1,0:T(8,128)(2,1)}), bf16[16,8,64,128]{3,2,1,0:T(8,128)(2,1)}, u32[]{:S(2)}, u32[]{:S(2)}) async-start(bf16[16,8,64,128]{3,2,1,0:T(8,128)(2,1)} %broadcast_in_dim.17), calls=%async_computation | async-start | bytes 4194304 | tf_op jit(solution)/shard_map/all_to_all | solution.py:451
  57.6 2.4 %collective-permute-start.2 = (bf16[2,512,128]{2,1,0:T(8,128)(2,1)S(1)}, bf16[2,512,128]{2,1,0:T(8,128)(2,1)S(1)}, u32[]{:S(2)}, u32[]{:S(2)}) collective-permute-start(bf16[2,512,128]{2,1,0:T(8,128)(2,1)S(1)} %get-tuple-element.40), channel_id=1, source_target_pairs={{0,4},{2,6},{4,0},{6,2},{1,5},{3,7},{5,1},{7,3},{8,12},{10,14},{12... | collective-permute-start | bytes 786440 | tf_op jit(solution)/shard_map/ppermute | solution.py:468
  61.2 6.5 %collective-permute-start.4 = (bf16[2,512,128]{2,1,0:T(8,128)(2,1)S(1)}, bf16[2,512,128]{2,1,0:T(8,128)(2,1)S(1)}, u32[]{:S(2)}, u32[]{:S(2)}) collective-permute-start(bf16[2,512,128]{2,1,0:T(8,128)(2,1)S(1)} %get-tuple-element.42.mine0_ref), channel_id=1, source_target_pairs={{0,1},{1,0},{2,3},{3,2},{4,5},{5,4},{6,7},{7,6},{8,9},{9,8},{10,11... | collective-permute-start | bytes 786440 | tf_op jit(solution)/shard_map/ppermute | solution.py:469
  67.7 16.0 %collective-permute-done.1.mine1_ref = bf16[2,512,128]{2,1,0:T(8,128)(2,1)S(1)} collective-permute-done((bf16[2,512,128]{2,1,0:T(8,128)(2,1)S(1)}, bf16[2,512,128]{2,1,0:T(8,128)(2,1)S(1)}, u32[]{:S(2)}, u32[]{:S(2)}) %collective-permute-start.1) | collective-permute-done | bytes 262176 | tf_op jit(solution)/shard_map/ppermute | solution.py:468
  83.7 3.8 %collective-permute-start.5 = (bf16[2,512,128]{2,1,0:T(8,128)(2,1)S(1)}, bf16[2,512,128]{2,1,0:T(8,128)(2,1)S(1)}, u32[]{:S(2)}, u32[]{:S(2)}) collective-permute-start(bf16[2,512,128]{2,1,0:T(8,128)(2,1)S(1)} %collective-permute-done.1.mine1_ref), channel_id=1, source_target_pairs={{0,1},{1,0},{2,3},{3,2},{4,5},{5,4},{6,7},{7,6},{8,9},{9,8},{10,11... | collective-permute-start | bytes 786440 | tf_op jit(solution)/shard_map/ppermute | solution.py:469
  87.5 4.3 %collective-permute-start.6 = (bf16[2,512,128]{2,1,0:T(8,128)(2,1)S(1)}, bf16[2,512,128]{2,1,0:T(8,128)(2,1)S(1)}, u32[]{:S(2)}, u32[]{:S(2)}) collective-permute-start(bf16[2,512,128]{2,1,0:T(8,128)(2,1)S(1)} %collective-permute-done.2.mine2_ref), channel_id=1, source_target_pairs={{0,1},{1,0},{2,3},{3,2},{4,5},{5,4},{6,7},{7,6},{8,9},{9,8},{10,11... | collective-permute-start | bytes 786440 | tf_op jit(solution)/shard_map/ppermute | solution.py:469
  93.4 17.5 %pairs.1 = (s16[16,528,128]{2,1,0:T(8,128)(2,1)}, f32[2,2048,128]{2,1,0:T(8,128)S(1)}, f32[2,2048,128]{2,1,0:T(8,128)}) custom-call(s32[2]{0:T(128)S(1)} %pad_add_fusion.ids_ref.core_ref, s32[18]{0:T(128)S(1)} %copy-done.5, bf16[4,2048,128]{2,1,0:T(8,128)(2,1)} %bitcast.7.left_ref, bf16[2,512,128]{2,1,0:T(8,128)(2,1)S(1)} %get-tuple-element.42.mine0_ref, ...), custom_call_target="tpu_custom_call" | custom-call | bytes 60000000 | tf_op jit(solution)/shard_map/pairs/pallas_call | solution.py:473
  112.3 5.6 %collective-permute-start.8 = (f32[2,2048,128]{2,1,0:T(8,128)}, f32[2,2048,128]{2,1,0:T(8,128)}, u32[]{:S(2)}, u32[]{:S(2)}) collective-permute-start(f32[2,2048,128]{2,1,0:T(8,128)} %get-tuple-element.28), channel_id=1, source_target_pairs={{0,1},{1,0},{2,3},{3,2},{4,5},{5,4},{6,7},{7,6},{8,9},{9,8},{10,11... | collective-permute-start | bytes 6291464 | tf_op jit(solution)/shard_map/ppermute | solution.py:503
  117.9 13.0 %all-to-all-start.1 = ((s16[16,528,128]{2,1,0:T(8,128)(2,1)}), s16[16,528,128]{2,1,0:T(8,128)(2,1)S(1)}, u32[]{:S(2)}, u32[]{:S(2)}) async-start(s16[16,528,128]{2,1,0:T(8,128)(2,1)} %get-tuple-element.26), calls=%async_computation.1 | async-start | bytes 4325376 | tf_op jit(solution)/shard_map/all_to_all | solution.py:505
  131.6 3.6 %quantize_right.1 = (s16[528,128]{1,0:T(8,128)(2,1)}, s16[528,128]{1,0:T(8,128)(2,1)}, s16[528,128]{1,0:T(8,128)(2,1)}, s16[528,128]{1,0:T(8,128)(2,1)}, s16[528...) custom-call(s32[2]{0:T(128)} %pad_add_fusion.1.zy_ref, ...), custom_call_target="tpu_custom_call" | custom-call | bytes 8000000 | tf_op jit(solution)/shard_map/quantize_right/pallas_call | solution.py:335
  135.3 3.0 %collective-permute-start.12 = (s16[528,128]{1,0:T(8,128)(2,1)}, s16[528,128]{1,0:T(8,128)(2,1)S(1)}, u32[]{:S(2)}, u32[]{:S(2)}) collective-permute-start(s16[528,128]{1,0:T(8,128)(2,1)} %get-tuple-element.33), channel_id=1, source_target_pairs={{0,128},{32,160},{64,192},{96,224},{128,0},{160,32},{192,64},{224,... | collective-permute-start | bytes 405512 | tf_op jit(solution)/shard_map/ppermute | solution.py:507
  139.8 3.5 %collective-permute-start.14 = (s16[528,128]{1,0:T(8,128)(2,1)}, s16[528,128]{1,0:T(8,128)(2,1)S(1)}, u32[]{:S(2)}, u32[]{:S(2)}) collective-permute-start(s16[528,128]{1,0:T(8,128)(2,1)} %get-tuple-element.35), channel_id=1, source_target_pairs={{0,192},{32,224},{64,0},{96,32},{128,64},{160,96},{192,128},{224,1... | collective-permute-start | bytes 405512 | tf_op jit(solution)/shard_map/ppermute | solution.py:507
  143.3 8.3 %collective-permute-done.10.refs_2_ = s16[528,128]{1,0:T(8,128)(2,1)S(1)} collective-permute-done((s16[528,128]{1,0:T(8,128)(2,1)}, s16[528,128]{1,0:T(8,128)(2,1)S(1)}, u32[]{:S(2)}, u32[]{:S(2)}) %collective-permute-start.10) | collective-permute-done | bytes 135200 | tf_op jit(solution)/shard_map/ppermute | solution.py:507
  151.7 4.1 %collective-permute-start.9 = (s16[528,128]{1,0:T(8,128)(2,1)}, s16[528,128]{1,0:T(8,128)(2,1)S(1)}, u32[]{:S(2)}, u32[]{:S(2)}) collective-permute-start(s16[528,128]{1,0:T(8,128)(2,1)} %get-tuple-element.30), channel_id=1, source_target_pairs={{0,32},{32,64},{64,96},{96,128},{128,160},{160,192},{192,224},{224... | collective-permute-start | bytes 405512 | tf_op jit(solution)/shard_map/ppermute | solution.py:507
  155.7 5.0 %collective-permute-done.14.refs_6_ = s16[528,128]{1,0:T(8,128)(2,1)S(1)} collective-permute-done((s16[528,128]{1,0:T(8,128)(2,1)}, s16[528,128]{1,0:T(8,128)(2,1)S(1)}, u32[]{:S(2)}, u32[]{:S(2)}) %collective-permute-start.14) | collective-permute-done | bytes 135200 | tf_op jit(solution)/shard_map/ppermute | solution.py:507
  160.8 4.0 %collective-permute-done.15.refs_7_ = s16[528,128]{1,0:T(8,128)(2,1)S(1)} collective-permute-done((s16[528,128]{1,0:T(8,128)(2,1)}, s16[528,128]{1,0:T(8,128)(2,1)S(1)}, u32[]{:S(2)}, u32[]{:S(2)}) %collective-permute-start.15) | collective-permute-done | bytes 135200 | tf_op jit(solution)/shard_map/ppermute | solution.py:507
  171.4 2.9 %combine.1.own_ref = f32[512,128]{1,0:T(8,128)} custom-call(s16[16,528,128]{2,1,0:T(8,128)(2,1)} %copy-done.6, s16[528,128]{1,0:T(8,128)(2,1)} %copy-done.16), custom_call_target="tpu_custom_call" | custom-call | tf_op jit(solution)/shard_map/combine/pallas_call | solution.py:346
  177.7 5.6 %overlap.1 = (f32[512,128]{1,0:T(8,128)}, f32[64,128]{1,0:T(8,128)}) custom-call(s32[2]{0:T(128)} %copy-done.4, f32[512,128]{1,0:T(8,128)} %combine.1.own_ref, f32[512,128]{1,0:T(8,128)} %copy-done.8, bf16[32,512,128]{2,1,0:T(8,128)(2,1)} %all-gather.6.cloned.1.call-done.phi_ref), custom_call_target="tpu_custom_call" | custom-call | tf_op jit(solution)/shard_map/overlap/pallas_call | solution.py:513
  185.5 13.4 %collective-permute-start.19 = (f32[64,128]{1,0:T(8,128)S(1)}, f32[64,128]{1,0:T(8,128)S(1)}, u32[]{:S(2)}, u32[]{:S(2)}) collective-permute-start(f32[64,128]{1,0:T(8,128)S(1)} %add.212.over0_ref), channel_id=1, source_target_pairs={{0,2},{2,4},{4,6},{6,0},{1,3},{3,5},{5,7},{7,1},{8,10},{10,12},{12... | collective-permute-start | bytes 98312 | tf_op jit(solution)/shard_map/ppermute | solution.py:439
  203.8 4.8 %project.1 = f32[512,128]{1,0:T(8,128)} custom-call(f32[512,128]{1,0:T(8,128)} %get-tuple-element.37.x_ref, bf16[32,512,128]{2,1,0:T(8,128)(2,1)} %all-gather.6.cloned.1.call-done.phi_ref, f32[64,128]{1,0:T(8,128)} %copy-done.17, f32[64,128]{1,0:T(8,128)} %copy-done.18, f32[64,128]{1,0:T(8,128)} %copy-done.19, f32[64,128]{1,0:T(8,128)} %copy-done.20), custom_call_target="tpu_custom_call" | custom-call | tf_op jit(solution)/shard_map/project/pallas_call | solution.py:524
  (102 shorter events, 31.6 us)
Async XLA Ops:
  6.5 40.9 %all-gather.4.cloned.1.call-start = ((), (), s32[]{:S(2)}) async-start(), calls=%async_computation.2 | async-start | bytes 1179648 | tf_op jit(solution)/shard_map/all_gather | solution.py:447
  7.3 169.7 %all-gather.6.cloned.1.call-start = ((), (), s32[]{:S(2)}) async-start(), calls=%async_computation.3 | async-start | bytes 5242880 | tf_op jit(solution)/shard_map/all_gather | solution.py:464
  7.3 23.9 %collective-permute-start = (bf16[8,64,128]{2,1,0:T(8,128)(2,1)}, bf16[8,64,128]{2,1,0:T(8,128)(2,1)S(1)}, u32[]{:S(2)}, u32[]{:S(2)}) collective-permute-start(bf16[8,64,128]{2,1,0:T(8,128)(2,1)} %bitcast.18), channel_id=1, source_target_pairs={{0,1},{1,0},{2,3},{3,2},{4,5},{5,4},{6,7},{7,6},{8,9},{9,8},{10,11... | collective-permute-start | bytes 393224 | tf_op jit(solution)/shard_map/ppermute | solution.py:419
  49.3 43.1 %all-to-all-start = ((bf16[16,8,64,128]{3,2,1,0:T(8,128)(2,1)}), bf16[16,8,64,128]{3,2,1,0:T(8,128)(2,1)}, u32[]{:S(2)}, u32[]{:S(2)}) async-start(bf16[16,8,64,128]{3,2,1,0:T(8,128)(2,1)} %broadcast_in_dim.17), calls=%async_computation | async-start | bytes 4194304 | tf_op jit(solution)/shard_map/all_to_all | solution.py:451
  56.2 27.4 %collective-permute-start.1 = (bf16[2,512,128]{2,1,0:T(8,128)(2,1)S(1)}, bf16[2,512,128]{2,1,0:T(8,128)(2,1)S(1)}, u32[]{:S(2)}, u32[]{:S(2)}) collective-permute-start(bf16[2,512,128]{2,1,0:T(8,128)(2,1)S(1)} %get-tuple-element.41), channel_id=1, source_target_pairs={{0,2},{2,4},{4,6},{6,0},{1,3},{3,5},{5,7},{7,1},{8,10},{10,12},{12... | collective-permute-start | bytes 786440 | tf_op jit(solution)/shard_map/ppermute | solution.py:468
  57.6 29.9 %collective-permute-start.2 = (bf16[2,512,128]{2,1,0:T(8,128)(2,1)S(1)}, bf16[2,512,128]{2,1,0:T(8,128)(2,1)S(1)}, u32[]{:S(2)}, u32[]{:S(2)}) collective-permute-start(bf16[2,512,128]{2,1,0:T(8,128)(2,1)S(1)} %get-tuple-element.40), channel_id=1, source_target_pairs={{0,4},{2,6},{4,0},{6,2},{1,5},{3,7},{5,1},{7,3},{8,12},{10,14},{12... | collective-permute-start | bytes 786440 | tf_op jit(solution)/shard_map/ppermute | solution.py:468
  60.0 31.9 %collective-permute-start.3 = (bf16[2,512,128]{2,1,0:T(8,128)(2,1)S(1)}, bf16[2,512,128]{2,1,0:T(8,128)(2,1)S(1)}, u32[]{:S(2)}, u32[]{:S(2)}) collective-permute-start(bf16[2,512,128]{2,1,0:T(8,128)(2,1)S(1)} %get-tuple-element.39), channel_id=1, source_target_pairs={{0,6},{2,0},{4,2},{6,4},{1,7},{3,1},{5,3},{7,5},{8,14},{10,8},{12,... | collective-permute-start | bytes 786440 | tf_op jit(solution)/shard_map/ppermute | solution.py:468
  61.2 31.2 %collective-permute-start.4 = (bf16[2,512,128]{2,1,0:T(8,128)(2,1)S(1)}, bf16[2,512,128]{2,1,0:T(8,128)(2,1)S(1)}, u32[]{:S(2)}, u32[]{:S(2)}) collective-permute-start(bf16[2,512,128]{2,1,0:T(8,128)(2,1)S(1)} %get-tuple-element.42.mine0_ref), channel_id=1, source_target_pairs={{0,1},{1,0},{2,3},{3,2},{4,5},{5,4},{6,7},{7,6},{8,9},{9,8},{10,11... | collective-permute-start | bytes 786440 | tf_op jit(solution)/shard_map/ppermute | solution.py:469
  83.7 8.7 %collective-permute-start.5 = (bf16[2,512,128]{2,1,0:T(8,128)(2,1)S(1)}, bf16[2,512,128]{2,1,0:T(8,128)(2,1)S(1)}, u32[]{:S(2)}, u32[]{:S(2)}) collective-permute-start(bf16[2,512,128]{2,1,0:T(8,128)(2,1)S(1)} %collective-permute-done.1.mine1_ref), channel_id=1, source_target_pairs={{0,1},{1,0},{2,3},{3,2},{4,5},{5,4},{6,7},{7,6},{8,9},{9,8},{10,11... | collective-permute-start | bytes 786440 | tf_op jit(solution)/shard_map/ppermute | solution.py:469
  87.5 5.5 %collective-permute-start.6 = (bf16[2,512,128]{2,1,0:T(8,128)(2,1)S(1)}, bf16[2,512,128]{2,1,0:T(8,128)(2,1)S(1)}, u32[]{:S(2)}, u32[]{:S(2)}) collective-permute-start(bf16[2,512,128]{2,1,0:T(8,128)(2,1)S(1)} %collective-permute-done.2.mine2_ref), channel_id=1, source_target_pairs={{0,1},{1,0},{2,3},{3,2},{4,5},{5,4},{6,7},{7,6},{8,9},{9,8},{10,11... | collective-permute-start | bytes 786440 | tf_op jit(solution)/shard_map/ppermute | solution.py:469
  112.3 19.3 %collective-permute-start.8 = (f32[2,2048,128]{2,1,0:T(8,128)}, f32[2,2048,128]{2,1,0:T(8,128)}, u32[]{:S(2)}, u32[]{:S(2)}) collective-permute-start(f32[2,2048,128]{2,1,0:T(8,128)} %get-tuple-element.28), channel_id=1, source_target_pairs={{0,1},{1,0},{2,3},{3,2},{4,5},{5,4},{6,7},{7,6},{8,9},{9,8},{10,11... | collective-permute-start | bytes 6291464 | tf_op jit(solution)/shard_map/ppermute | solution.py:503
  117.9 51.5 %all-to-all-start.1 = ((s16[16,528,128]{2,1,0:T(8,128)(2,1)}), s16[16,528,128]{2,1,0:T(8,128)(2,1)S(1)}, u32[]{:S(2)}, u32[]{:S(2)}) async-start(s16[16,528,128]{2,1,0:T(8,128)(2,1)} %get-tuple-element.26), calls=%async_computation.1 | async-start | bytes 4325376 | tf_op jit(solution)/shard_map/all_to_all | solution.py:505
  135.2 16.4 %collective-permute-start.10 = (s16[528,128]{1,0:T(8,128)(2,1)}, s16[528,128]{1,0:T(8,128)(2,1)S(1)}, u32[]{:S(2)}, u32[]{:S(2)}) collective-permute-start(s16[528,128]{1,0:T(8,128)(2,1)} %get-tuple-element.31), channel_id=1, source_target_pairs={{0,64},{32,96},{64,128},{96,160},{128,192},{160,224},{192,0},{224,... | collective-permute-start | bytes 405512 | tf_op jit(solution)/shard_map/ppermute | solution.py:507
  135.2 16.4 %collective-permute-start.11 = (s16[528,128]{1,0:T(8,128)(2,1)}, s16[528,128]{1,0:T(8,128)(2,1)S(1)}, u32[]{:S(2)}, u32[]{:S(2)}) collective-permute-start(s16[528,128]{1,0:T(8,128)(2,1)} %get-tuple-element.32), channel_id=1, source_target_pairs={{0,96},{32,128},{64,160},{96,192},{128,224},{160,0},{192,32},{224,... | collective-permute-start | bytes 405512 | tf_op jit(solution)/shard_map/ppermute | solution.py:507
  135.3 20.4 %collective-permute-start.12 = (s16[528,128]{1,0:T(8,128)(2,1)}, s16[528,128]{1,0:T(8,128)(2,1)S(1)}, u32[]{:S(2)}, u32[]{:S(2)}) collective-permute-start(s16[528,128]{1,0:T(8,128)(2,1)} %get-tuple-element.33), channel_id=1, source_target_pairs={{0,128},{32,160},{64,192},{96,224},{128,0},{160,32},{192,64},{224,... | collective-permute-start | bytes 405512 | tf_op jit(solution)/shard_map/ppermute | solution.py:507
  138.3 17.4 %collective-permute-start.13 = (s16[528,128]{1,0:T(8,128)(2,1)}, s16[528,128]{1,0:T(8,128)(2,1)S(1)}, u32[]{:S(2)}, u32[]{:S(2)}) collective-permute-start(s16[528,128]{1,0:T(8,128)(2,1)} %get-tuple-element.34), channel_id=1, source_target_pairs={{0,160},{32,192},{64,224},{96,0},{128,32},{160,64},{192,96},{224,1... | collective-permute-start | bytes 405512 | tf_op jit(solution)/shard_map/ppermute | solution.py:507
  139.8 21.0 %collective-permute-start.14 = (s16[528,128]{1,0:T(8,128)(2,1)}, s16[528,128]{1,0:T(8,128)(2,1)S(1)}, u32[]{:S(2)}, u32[]{:S(2)}) collective-permute-start(s16[528,128]{1,0:T(8,128)(2,1)} %get-tuple-element.35), channel_id=1, source_target_pairs={{0,192},{32,224},{64,0},{96,32},{128,64},{160,96},{192,128},{224,1... | collective-permute-start | bytes 405512 | tf_op jit(solution)/shard_map/ppermute | solution.py:507
  151.6 13.1 %collective-permute-start.15 = (s16[528,128]{1,0:T(8,128)(2,1)}, s16[528,128]{1,0:T(8,128)(2,1)S(1)}, u32[]{:S(2)}, u32[]{:S(2)}) collective-permute-start(s16[528,128]{1,0:T(8,128)(2,1)} %get-tuple-element.36), channel_id=1, source_target_pairs={{0,224},{32,0},{64,32},{96,64},{128,96},{160,128},{192,160},{224,1... | collective-permute-start | bytes 405512 | tf_op jit(solution)/shard_map/ppermute | solution.py:507
  151.7 13.1 %collective-permute-start.9 = (s16[528,128]{1,0:T(8,128)(2,1)}, s16[528,128]{1,0:T(8,128)(2,1)S(1)}, u32[]{:S(2)}, u32[]{:S(2)}) collective-permute-start(s16[528,128]{1,0:T(8,128)(2,1)} %get-tuple-element.30), channel_id=1, source_target_pairs={{0,32},{32,64},{64,96},{96,128},{128,160},{160,192},{192,224},{224... | collective-permute-start | bytes 405512 | tf_op jit(solution)/shard_map/ppermute | solution.py:507
  167.8 1.6 collective-permute-start.16
  174.3 2.6 %collective-permute-start.17 = (f32[512,128]{1,0:T(8,128)}, f32[512,128]{1,0:T(8,128)S(1)}, u32[]{:S(2)}, u32[]{:S(2)}) collective-permute-start(f32[512,128]{1,0:T(8,128)} %combine.1.own_ref), channel_id=1, source_target_pairs={{0,1},{1,0},{2,3},{3,2},{4,5},{5,4},{6,7},{7,6},{8,9},{9,8},{10,11... | collective-permute-start | bytes 786440 | tf_op jit(solution)/shard_map/ppermute | solution.py:511
  185.5 16.0 %collective-permute-start.19 = (f32[64,128]{1,0:T(8,128)S(1)}, f32[64,128]{1,0:T(8,128)S(1)}, u32[]{:S(2)}, u32[]{:S(2)}) collective-permute-start(f32[64,128]{1,0:T(8,128)S(1)} %add.212.over0_ref), channel_id=1, source_target_pairs={{0,2},{2,4},{4,6},{6,0},{1,3},{3,5},{5,7},{7,1},{8,10},{10,12},{12... | collective-permute-start | bytes 98312 | tf_op jit(solution)/shard_map/ppermute | solution.py:439
  198.9 4.3 %collective-permute-start.20 = (f32[64,128]{1,0:T(8,128)S(1)}, f32[64,128]{1,0:T(8,128)S(1)}, u32[]{:S(2)}, u32[]{:S(2)}) collective-permute-start(f32[64,128]{1,0:T(8,128)S(1)} %add.212.over0_ref), channel_id=1, source_target_pairs={{0,4},{2,6},{4,0},{6,2},{1,5},{3,7},{5,1},{7,3},{8,12},{10,14},{12... | collective-permute-start | bytes 98312 | tf_op jit(solution)/shard_map/ppermute | solution.py:439
  199.5 3.7 %collective-permute-start.21 = (f32[64,128]{1,0:T(8,128)S(1)}, f32[64,128]{1,0:T(8,128)S(1)}, u32[]{:S(2)}, u32[]{:S(2)}) collective-permute-start(f32[64,128]{1,0:T(8,128)S(1)} %add.212.over0_ref), channel_id=1, source_target_pairs={{0,6},{2,0},{4,2},{6,4},{1,7},{3,1},{5,3},{7,5},{8,14},{10,8},{12,... | collective-permute-start | bytes 98312 | tf_op jit(solution)/shard_map/ppermute | solution.py:439
  (23 other events, 252.5 us)
Sparse Core Ops, SparseCore 0:
  9.1 38.2 all-gather.3
  49.2 67.1 all-gather.5

commit v6 on v4

--- a/solution.py
+++ b/solution.py
@@ -173,14 +173,8 @@
     ids_ref,
     tasks_ref,
     left_ref,
-    mine0_ref,
-    mine1_ref,
-    mine2_ref,
-    mine3_ref,
-    other0_ref,
-    other1_ref,
-    other2_ref,
-    other3_ref,
+    mine_ref,
+    other_ref,
     wz_ref,
     wy_ref,
     wx_ref,
@@ -204,17 +198,14 @@
 
     lax.fori_loop(0, ROWS // CHUNK, clear, 0)
     keep = (lax.broadcasted_iota(jnp.int32, (G, 128), 1) < G) == (ids_ref[0] == 0)
-    mine_refs = (mine0_ref, mine1_ref, mine2_ref, mine3_ref)
-    other_refs = (other0_ref, other1_ref, other2_ref, other3_ref)
 
     def exchange(i, carry):
         source = pl.ds(pl.multiple_of(i * G, G), G)
-        for k in range(NY):
-            quarter = (ids_ref[1] - k) & (NY - 1)
+        for quarter in range(NY):
             rows = pl.ds(pl.multiple_of(quarter * 512 + i * G, G), G)
             for j in range(2):
-                mine = mine_refs[k][j, source].astype(f32)
-                other = other_refs[k][j, source].astype(f32)
+                mine = mine_ref[2 * quarter + j, source].astype(f32)
+                other = other_ref[2 * quarter + j, source].astype(f32)
                 same_ref[j, rows] = jnp.where(keep, mine, pltpu.roll(other, G, 1)).astype(bf16)
                 cross_ref[j, rows] = jnp.where(keep, pltpu.roll(mine, G, 1), other).astype(bf16)
         return carry
@@ -461,12 +452,9 @@
         name="assign",
     )(me, slots)
     phi_all = lax.all_gather(z_couples, "x", axis=0, tiled=True)
-    right = []
-    for k in range(NY):
-        part = lax.dynamic_slice(z_couples, (2 * ((y + k) % NY), 0, 0), (2, 512, 128))
-        right.append(lax.ppermute(part, "y", ring(NY, k)) if k else part)
-    *right, tasks = lax.optimization_barrier((*right, tasks))
-    right_other = [lax.ppermute(part, "core", ring(2, 1)) for part in right]
+    right = lax.all_to_all(z_couples, "y", split_axis=0, concat_axis=0, tiled=True)
+    right, tasks = lax.optimization_barrier((right, tasks))
+    right_other = lax.ppermute(right, "core", ring(2, 1))
     ids = jnp.stack([core, y]).astype(jnp.int32)
 
     w_depth, w_rows, w_planes = (jnp.asarray(w) for w in weights())
@@ -477,7 +465,7 @@
             jax.ShapeDtypeStruct((2, ROWS, 128), f32),
             jax.ShapeDtypeStruct((2, ROWS, 128), f32),
         ),
-        in_specs=smem_specs(2) + vmem_specs(5 + 2 * NY),
+        in_specs=smem_specs(2) + vmem_specs(7),
         out_specs=tuple(vmem_specs(3)),
         scratch_shapes=[
             pltpu.VMEM((ROWS, 128), f32),
@@ -492,8 +480,8 @@
         ids,
         tasks,
         left.reshape(4, ROWS, 128),
-        *right,
-        *right_other,
+        right,
+        right_other,
         w_depth,
         w_rows,
         w_planes,

time: 202 us -> 201 us (level)
  waiting for transfers between devices: 24.5 us -> 27.9 us
  local copies, waits for them, and re-layouts: 12.2 us -> 9.27 us
  Pallas kernels: 50.3 us -> 47.5 us
  starting transfers between devices: 55.6 us -> 58.4 us
    ppermute x7 -> x1, starting transfers between devices: 9.6 us -> 5.3 us  [local(): right_other = lax.ppermute(right, 'core', ring(2, 1))]
    all_to_all x0 -> x1, starting transfers between devices: none -> 3.66 us  [local(): lax.all_to_all(z_couples, 'y', split_axis=0, concat_axis=0, tiled=True)]
    pallas_call x1, Pallas kernels: 20.2 us -> 17.4 us  [local(): pl.pallas_call(pairs_kernel, out_shape=(jax.ShapeDtypeStruct((NX * NY, 52...]
    dynamic_slice x1 -> x0, local copies, waits for them, and re-layouts: 2.81 us -> none  [local(): lax.dynamic_slice(z_couples, (2 * ((y + k) % NY), 0, 0), (2, 512, 128))]
    ppermute x7, starting transfers between devices: 12.3 us -> 14.7 us  [local(): lax.ppermute(part, 'z', ring(NZ, k))]
    ppermute x7, waiting for transfers between devices: 17.9 us -> 20 us  [local(): lax.ppermute(part, 'z', ring(NZ, k))]
  transfers between devices with their start and end apart: 26 -> 21, of which waited for: 11 -> 9; matrix products, arithmetic and copies ran while one was open for 3% -> 1% of each run, Pallas kernels for 20% -> 18%
where the time goes in v6:
time: 201 us
  starting transfers between devices  58.4 us (29%)
  Pallas kernels  47.5 us (24%)
  blocking collectives  40.8 us (20%)
  waiting for transfers between devices  27.9 us (14%)
  between operations  14.3 us (7%)
  local copies, waits for them, and re-layouts  9.27 us (5%)
  other arithmetic  3.14 us (2%)
    unnamed x1, blocking collectives  40.8 us
    ppermute x7, waiting for transfers between devices, local(): lax.ppermute(part, 'z', ring(NZ, k))  20 us
    pallas_call x1, Pallas kernels, local(): pl.pallas_call(pairs_kernel, out_shape=(jax.ShapeDtypeStruct((NX * NY, 52...  17.4 us
    ppermute x3, starting transfers between devices, over_y(): lax.ppermute(value, 'y', ring(NY, k))  16 us
    ppermute x7, starting transfers between devices, local(): lax.ppermute(part, 'z', ring(NZ, k))  14.7 us
    pallas_call x1, Pallas kernels, local(): pl.pallas_call(assign_kernel, out_shape=jax.ShapeDtypeStruct((18,), jnp.i...  10.8 us
    unnamed x48, local copies, waits for them, and re-layouts  6.6 us
    all_to_all x1, starting transfers between devices, local(): lax.all_to_all(left_parts, ('x', 'y'), split_axis=0, concat_axis=0, tiled...  6.42 us
  transfers between devices with their start and end apart: 21, of which 9 were waited for; matrix products, arithmetic and copies ran while one was open for 1% of the time, Pallas kernels for 18%

profile of v6, /device:TPU:1, one launch (start us, length us, event | category | flops | bytes accessed | tf_op | source)
XLA Modules:
  0.0 201.3 jit_solution(6824592079622312239)
XLA Ops:
  6.5 3.2 %collective-permute-start = (bf16[8,64,128]{2,1,0:T(8,128)(2,1)}, bf16[8,64,128]{2,1,0:T(8,128)(2,1)S(1)}, u32[]{:S(2)}, u32[]{:S(2)}) collective-permute-start(bf16[8,64,128]{2,1,0:T(8,128)(2,1)} %bitcast.23), channel_id=1, source_target_pairs={{0,1},{1,0},{2,3},{3,2},{4,5},{5,4},{6,7},{7,6},{8,9},{9,8},{10,11... | collective-permute-start | bytes 393224 | tf_op jit(solution)/shard_map/ppermute | solution.py:410
  12.1 1.9 broadcast_in_dim.19
  14.0 5.2 %all-to-all-start = ((bf16[16,8,64,128]{3,2,1,0:T(8,128)(2,1)}), bf16[16,8,64,128]{3,2,1,0:T(8,128)(2,1)S(1)}, u32[]{:S(2)}, u32[]{:S(2)}) async-start(bf16[16,8,64,128]{3,2,1,0:T(8,128)(2,1)} %broadcast_in_dim.19), calls=%async_computation | async-start | bytes 4194304 | tf_op jit(solution)/shard_map/all_to_all | solution.py:441
  21.3 40.8 %all-reduce = s32[1024]{0:T(1024)S(1)} all-reduce(s32[1024]{0:T(1024)S(1)} %fusion.21), channel_id=2, replica_groups=mesh['z'=8,'x'=4,'y'=4,'core'=2] {'z','x'}, use_global_device_ids=true, to_apply=%add | all-reduce | flops 1024 | bytes 8192
  62.8 3.7 %all-to-all-start.1 = ((bf16[8,512,128]{2,1,0:T(8,128)(2,1)}), bf16[8,512,128]{2,1,0:T(8,128)(2,1)S(1)}, u32[]{:S(2)}, u32[]{:S(2)}) async-start(bf16[8,512,128]{2,1,0:T(8,128)(2,1)} %all-gather.4.cloned.1.call-done), calls=%async_computation.1 | async-start | bytes 2097152 | tf_op jit(solution)/shard_map/all_to_all | solution.py:455
  66.6 10.8 %assign.1.tasks_ref = s32[18]{0:T(128)} custom-call(s32[1]{0:T(128)} %bitcast.9.me_ref, s32[32,32]{1,0:T(8,128)} %reshape.231.slots_ref), custom_call_target="tpu_custom_call" | custom-call | bytes 60000000 | tf_op jit(solution)/shard_map/assign/pallas_call | solution.py:445
  77.4 5.3 %collective-permute-start.1 = (bf16[8,512,128]{2,1,0:T(8,128)(2,1)S(1)}, bf16[8,512,128]{2,1,0:T(8,128)(2,1)S(1)}, u32[]{:S(2)}, u32[]{:S(2)}) collective-permute-start(bf16[8,512,128]{2,1,0:T(8,128)(2,1)S(1)} %all-to-all-done.1.mine_ref), channel_id=1, source_target_pairs={{0,1},{1,0},{2,3},{3,2},{4,5},{5,4},{6,7},{7,6},{8,9},{9,8},{10,11... | collective-permute-start | bytes 3145736 | tf_op jit(solution)/shard_map/ppermute | solution.py:457
  83.2 1.7 collective-permute-done.1.other_ref
  85.6 17.4 %pairs.1 = (s16[16,528,128]{2,1,0:T(8,128)(2,1)}, f32[2,2048,128]{2,1,0:T(8,128)S(1)}, f32[2,2048,128]{2,1,0:T(8,128)}) custom-call(s32[2]{0:T(128)S(1)} %pad_add_fusion.ids_ref.core_ref, s32[18]{0:T(128)S(1)} %copy-done.5, bf16[4,2048,128]{2,1,0:T(8,128)(2,1)} %bitcast.22, bf16[8,512,128]{2,1,0:T(8,128)(2,1)S(1)} %all-to-all-done.1.mine_ref, ...), custom_call_target="tpu_custom_call" | custom-call | bytes 60000000 | tf_op jit(solution)/shard_map/pairs/pallas_call | solution.py:461
  104.8 6.4 %all-to-all-start.2 = ((s16[16,528,128]{2,1,0:T(8,128)(2,1)}), s16[16,528,128]{2,1,0:T(8,128)(2,1)S(1)}, u32[]{:S(2)}, u32[]{:S(2)}) async-start(s16[16,528,128]{2,1,0:T(8,128)(2,1)} %get-tuple-element.28), calls=%async_computation.2 | async-start | bytes 4325376 | tf_op jit(solution)/shard_map/all_to_all | solution.py:493
  111.9 3.7 %quantize_right.1 = (s16[528,128]{1,0:T(8,128)(2,1)}, s16[528,128]{1,0:T(8,128)(2,1)}, s16[528,128]{1,0:T(8,128)(2,1)}, s16[528,128]{1,0:T(8,128)(2,1)}, s16[528...) custom-call(s32[2]{0:T(128)} %pad_add_fusion.1.zy_ref, ...), custom_call_target="tpu_custom_call" | custom-call | bytes 8000000 | tf_op jit(solution)/shard_map/quantize_right/pallas_call | solution.py:326
  117.2 3.9 %collective-permute-start.4 = (s16[528,128]{1,0:T(8,128)(2,1)}, s16[528,128]{1,0:T(8,128)(2,1)S(1)}, u32[]{:S(2)}, u32[]{:S(2)}) collective-permute-start(s16[528,128]{1,0:T(8,128)(2,1)} %get-tuple-element.33), channel_id=1, source_target_pairs={{0,64},{32,96},{64,128},{96,160},{128,192},{160,224},{192,0},{224,... | collective-permute-start | bytes 405512 | tf_op jit(solution)/shard_map/ppermute | solution.py:495
  121.2 3.3 %collective-permute-start.6 = (s16[528,128]{1,0:T(8,128)(2,1)}, s16[528,128]{1,0:T(8,128)(2,1)S(1)}, u32[]{:S(2)}, u32[]{:S(2)}) collective-permute-start(s16[528,128]{1,0:T(8,128)(2,1)} %get-tuple-element.35), channel_id=1, source_target_pairs={{0,128},{32,160},{64,192},{96,224},{128,0},{160,32},{192,64},{224,... | collective-permute-start | bytes 405512 | tf_op jit(solution)/shard_map/ppermute | solution.py:495
  125.7 3.3 %collective-permute-start.8 = (s16[528,128]{1,0:T(8,128)(2,1)}, s16[528,128]{1,0:T(8,128)(2,1)S(1)}, u32[]{:S(2)}, u32[]{:S(2)}) collective-permute-start(s16[528,128]{1,0:T(8,128)(2,1)} %get-tuple-element.37), channel_id=1, source_target_pairs={{0,192},{32,224},{64,0},{96,32},{128,64},{160,96},{192,128},{224,1... | collective-permute-start | bytes 405512 | tf_op jit(solution)/shard_map/ppermute | solution.py:495
  130.2 9.3 %collective-permute-done.5.refs_3_ = s16[528,128]{1,0:T(8,128)(2,1)S(1)} collective-permute-done((s16[528,128]{1,0:T(8,128)(2,1)}, s16[528,128]{1,0:T(8,128)(2,1)S(1)}, u32[]{:S(2)}, u32[]{:S(2)}) %collective-permute-start.5) | collective-permute-done | bytes 135200 | tf_op jit(solution)/shard_map/ppermute | solution.py:495
  141.2 7.0 %collective-permute-done.8.refs_6_ = s16[528,128]{1,0:T(8,128)(2,1)S(1)} collective-permute-done((s16[528,128]{1,0:T(8,128)(2,1)}, s16[528,128]{1,0:T(8,128)(2,1)S(1)}, u32[]{:S(2)}, u32[]{:S(2)}) %collective-permute-start.8) | collective-permute-done | bytes 135200 | tf_op jit(solution)/shard_map/ppermute | solution.py:495
  148.2 2.0 %collective-permute-done.9.refs_7_ = s16[528,128]{1,0:T(8,128)(2,1)S(1)} collective-permute-done((s16[528,128]{1,0:T(8,128)(2,1)}, s16[528,128]{1,0:T(8,128)(2,1)S(1)}, u32[]{:S(2)}, u32[]{:S(2)}) %collective-permute-start.9) | collective-permute-done | bytes 135200 | tf_op jit(solution)/shard_map/ppermute | solution.py:495
  150.9 2.3 %combine_right.1 = s16[528,128]{1,0:T(8,128)(2,1)} custom-call(s16[528,128]{1,0:T(8,128)(2,1)} %get-tuple-element.31.refs_0_, s16[528,128]{1,0:T(8,128)(2,1)} %copy-done.9, s16[528,128]{1,0:T(8,128)(2,1)} %copy-done.10, s16[528,128]{1,0:T(8,128)(2,1)} %copy-done.11, s16[528,128]{1,0:T(8,128)(2,1)} %copy-done.12, s16[528,128]{1,0:T(8,128)(2,1)} %copy-done.13, ...), custom_call_target="tpu_custom_call" | custom-call | bytes 6000000 | tf_op jit(solution)/shard_map/combine_right/pallas_call | solution.py:347
  156.8 2.9 %combine.1.own_ref = f32[512,128]{1,0:T(8,128)} custom-call(s16[16,528,128]{2,1,0:T(8,128)(2,1)} %copy-done.6, s16[528,128]{1,0:T(8,128)(2,1)} %copy-done.16), custom_call_target="tpu_custom_call" | custom-call | tf_op jit(solution)/shard_map/combine/pallas_call | solution.py:337
  163.5 5.6 %overlap.1 = (f32[512,128]{1,0:T(8,128)}, f32[64,128]{1,0:T(8,128)}) custom-call(s32[2]{0:T(128)} %copy-done.4, f32[512,128]{1,0:T(8,128)} %combine.1.own_ref, f32[512,128]{1,0:T(8,128)} %copy-done.8, bf16[32,512,128]{2,1,0:T(8,128)(2,1)} %all-gather.6.cloned.1.call-done.phi_ref), custom_call_target="tpu_custom_call" | custom-call | tf_op jit(solution)/shard_map/overlap/pallas_call | solution.py:501
  171.3 13.4 %collective-permute-start.13 = (f32[64,128]{1,0:T(8,128)S(1)}, f32[64,128]{1,0:T(8,128)S(1)}, u32[]{:S(2)}, u32[]{:S(2)}) collective-permute-start(f32[64,128]{1,0:T(8,128)S(1)} %add.167.over0_ref), channel_id=1, source_target_pairs={{0,2},{2,4},{4,6},{6,0},{1,3},{3,5},{5,7},{7,1},{8,10},{10,12},{12... | collective-permute-start | bytes 98312 | tf_op jit(solution)/shard_map/ppermute | solution.py:430
  185.2 2.0 collective-permute-start.15
  187.2 1.7 collective-permute-done.14.over2_ref
  189.6 4.8 %project.1 = f32[512,128]{1,0:T(8,128)} custom-call(f32[512,128]{1,0:T(8,128)} %get-tuple-element.39.x_ref, bf16[32,512,128]{2,1,0:T(8,128)(2,1)} %all-gather.6.cloned.1.call-done.phi_ref, f32[64,128]{1,0:T(8,128)} %copy-done.17, f32[64,128]{1,0:T(8,128)} %copy-done.18, f32[64,128]{1,0:T(8,128)} %copy-done.19, f32[64,128]{1,0:T(8,128)} %copy-done.20), custom_call_target="tpu_custom_call" | custom-call | tf_op jit(solution)/shard_map/project/pallas_call | solution.py:512
  (95 shorter events, 25.2 us)
Async XLA Ops:
  6.5 4.4 %collective-permute-start = (bf16[8,64,128]{2,1,0:T(8,128)(2,1)}, bf16[8,64,128]{2,1,0:T(8,128)(2,1)S(1)}, u32[]{:S(2)}, u32[]{:S(2)}) collective-permute-start(bf16[8,64,128]{2,1,0:T(8,128)(2,1)} %bitcast.23), channel_id=1, source_target_pairs={{0,1},{1,0},{2,3},{3,2},{4,5},{5,4},{6,7},{7,6},{8,9},{9,8},{10,11... | collective-permute-start | bytes 393224 | tf_op jit(solution)/shard_map/ppermute | solution.py:410
  14.0 48.8 %all-to-all-start = ((bf16[16,8,64,128]{3,2,1,0:T(8,128)(2,1)}), bf16[16,8,64,128]{3,2,1,0:T(8,128)(2,1)S(1)}, u32[]{:S(2)}, u32[]{:S(2)}) async-start(bf16[16,8,64,128]{3,2,1,0:T(8,128)(2,1)} %broadcast_in_dim.19), calls=%async_computation | async-start | bytes 4194304 | tf_op jit(solution)/shard_map/all_to_all | solution.py:441
  19.2 43.6 %all-gather.4.cloned.1.call-start = ((), (), s32[]{:S(2)}) async-start(), calls=%async_computation.3 | async-start | bytes 1179648 | tf_op jit(solution)/shard_map/all_gather | solution.py:438
  19.9 142.9 %all-gather.6.cloned.1.call-start = ((), (), s32[]{:S(2)}) async-start(), calls=%async_computation.4 | async-start | bytes 5242880 | tf_op jit(solution)/shard_map/all_gather | solution.py:454
  62.8 22.2 %copy-start.2 = (bf16[256,256]{1,0:T(8,128)(2,1)S(1)}, bf16[256,256]{1,0:T(8,128)(2,1)}, u32[]{:S(2)}) copy-start(bf16[256,256]{1,0:T(8,128)(2,1)} %constant.132.clone.wy_ref) | copy-start | bytes 393220
  62.8 22.2 %copy-start.3 = (bf16[128,128]{1,0:T(8,128)(2,1)S(1)}, bf16[128,128]{1,0:T(8,128)(2,1)}, u32[]{:S(2)}) copy-start(bf16[128,128]{1,0:T(8,128)(2,1)} %constant.133.clone.wx_ref) | copy-start | bytes 98308
  62.8 14.5 %all-to-all-start.1 = ((bf16[8,512,128]{2,1,0:T(8,128)(2,1)}), bf16[8,512,128]{2,1,0:T(8,128)(2,1)S(1)}, u32[]{:S(2)}, u32[]{:S(2)}) async-start(bf16[8,512,128]{2,1,0:T(8,128)(2,1)} %all-gather.4.cloned.1.call-done), calls=%async_computation.1 | async-start | bytes 2097152 | tf_op jit(solution)/shard_map/all_to_all | solution.py:455
  77.4 7.6 %collective-permute-start.1 = (bf16[8,512,128]{2,1,0:T(8,128)(2,1)S(1)}, bf16[8,512,128]{2,1,0:T(8,128)(2,1)S(1)}, u32[]{:S(2)}, u32[]{:S(2)}) collective-permute-start(bf16[8,512,128]{2,1,0:T(8,128)(2,1)S(1)} %all-to-all-done.1.mine_ref), channel_id=1, source_target_pairs={{0,1},{1,0},{2,3},{3,2},{4,5},{5,4},{6,7},{7,6},{8,9},{9,8},{10,11... | collective-permute-start | bytes 3145736 | tf_op jit(solution)/shard_map/ppermute | solution.py:457
  104.4 7.5 %collective-permute-start.2 = (f32[2,2048,128]{2,1,0:T(8,128)}, f32[2,2048,128]{2,1,0:T(8,128)}, u32[]{:S(2)}, u32[]{:S(2)}) collective-permute-start(f32[2,2048,128]{2,1,0:T(8,128)} %get-tuple-element.30), channel_id=1, source_target_pairs={{0,1},{1,0},{2,3},{3,2},{4,5},{5,4},{6,7},{7,6},{8,9},{9,8},{10,11... | collective-permute-start | bytes 6291464 | tf_op jit(solution)/shard_map/ppermute | solution.py:491
  104.8 50.0 %all-to-all-start.2 = ((s16[16,528,128]{2,1,0:T(8,128)(2,1)}), s16[16,528,128]{2,1,0:T(8,128)(2,1)S(1)}, u32[]{:S(2)}, u32[]{:S(2)}) async-start(s16[16,528,128]{2,1,0:T(8,128)(2,1)} %get-tuple-element.28), calls=%async_computation.2 | async-start | bytes 4325376 | tf_op jit(solution)/shard_map/all_to_all | solution.py:493
  115.5 10.2 %collective-permute-start.3 = (s16[528,128]{1,0:T(8,128)(2,1)}, s16[528,128]{1,0:T(8,128)(2,1)S(1)}, u32[]{:S(2)}, u32[]{:S(2)}) collective-permute-start(s16[528,128]{1,0:T(8,128)(2,1)} %get-tuple-element.32), channel_id=1, source_target_pairs={{0,32},{32,64},{64,96},{96,128},{128,160},{160,192},{192,224},{224... | collective-permute-start | bytes 405512 | tf_op jit(solution)/shard_map/ppermute | solution.py:495
  117.2 11.8 %collective-permute-start.4 = (s16[528,128]{1,0:T(8,128)(2,1)}, s16[528,128]{1,0:T(8,128)(2,1)S(1)}, u32[]{:S(2)}, u32[]{:S(2)}) collective-permute-start(s16[528,128]{1,0:T(8,128)(2,1)} %get-tuple-element.33), channel_id=1, source_target_pairs={{0,64},{32,96},{64,128},{96,160},{128,192},{160,224},{192,0},{224,... | collective-permute-start | bytes 405512 | tf_op jit(solution)/shard_map/ppermute | solution.py:495
  121.2 18.3 %collective-permute-start.5 = (s16[528,128]{1,0:T(8,128)(2,1)}, s16[528,128]{1,0:T(8,128)(2,1)S(1)}, u32[]{:S(2)}, u32[]{:S(2)}) collective-permute-start(s16[528,128]{1,0:T(8,128)(2,1)} %get-tuple-element.34), channel_id=1, source_target_pairs={{0,96},{32,128},{64,160},{96,192},{128,224},{160,0},{192,32},{224,... | collective-permute-start | bytes 405512 | tf_op jit(solution)/shard_map/ppermute | solution.py:495
  121.2 18.3 %collective-permute-start.6 = (s16[528,128]{1,0:T(8,128)(2,1)}, s16[528,128]{1,0:T(8,128)(2,1)S(1)}, u32[]{:S(2)}, u32[]{:S(2)}) collective-permute-start(s16[528,128]{1,0:T(8,128)(2,1)} %get-tuple-element.35), channel_id=1, source_target_pairs={{0,128},{32,160},{64,192},{96,224},{128,0},{160,32},{192,64},{224,... | collective-permute-start | bytes 405512 | tf_op jit(solution)/shard_map/ppermute | solution.py:495
  124.5 16.7 %collective-permute-start.7 = (s16[528,128]{1,0:T(8,128)(2,1)}, s16[528,128]{1,0:T(8,128)(2,1)S(1)}, u32[]{:S(2)}, u32[]{:S(2)}) collective-permute-start(s16[528,128]{1,0:T(8,128)(2,1)} %get-tuple-element.36), channel_id=1, source_target_pairs={{0,160},{32,192},{64,224},{96,0},{128,32},{160,64},{192,96},{224,1... | collective-permute-start | bytes 405512 | tf_op jit(solution)/shard_map/ppermute | solution.py:495
  125.7 24.6 %copy-start.9 = (s16[528,128]{1,0:T(8,128)(2,1)}, s16[528,128]{1,0:T(8,128)(2,1)S(1)}, u32[]{:S(2)}) copy-start(s16[528,128]{1,0:T(8,128)(2,1)S(1)} %collective-permute-done.3.refs_1_) | copy-start | bytes 405508
  125.7 22.5 %collective-permute-start.8 = (s16[528,128]{1,0:T(8,128)(2,1)}, s16[528,128]{1,0:T(8,128)(2,1)S(1)}, u32[]{:S(2)}, u32[]{:S(2)}) collective-permute-start(s16[528,128]{1,0:T(8,128)(2,1)} %get-tuple-element.37), channel_id=1, source_target_pairs={{0,192},{32,224},{64,0},{96,32},{128,64},{160,96},{192,128},{224,1... | collective-permute-start | bytes 405512 | tf_op jit(solution)/shard_map/ppermute | solution.py:495
  129.0 21.2 %collective-permute-start.9 = (s16[528,128]{1,0:T(8,128)(2,1)}, s16[528,128]{1,0:T(8,128)(2,1)S(1)}, u32[]{:S(2)}, u32[]{:S(2)}) collective-permute-start(s16[528,128]{1,0:T(8,128)(2,1)} %get-tuple-element.38), channel_id=1, source_target_pairs={{0,224},{32,0},{64,32},{96,64},{128,96},{160,128},{192,160},{224,1... | collective-permute-start | bytes 405512 | tf_op jit(solution)/shard_map/ppermute | solution.py:495
  153.2 1.6 collective-permute-start.10
  159.7 3.0 %collective-permute-start.11 = (f32[512,128]{1,0:T(8,128)}, f32[512,128]{1,0:T(8,128)S(1)}, u32[]{:S(2)}, u32[]{:S(2)}) collective-permute-start(f32[512,128]{1,0:T(8,128)} %combine.1.own_ref), channel_id=1, source_target_pairs={{0,1},{1,0},{2,3},{3,2},{4,5},{5,4},{6,7},{7,6},{8,9},{9,8},{10,11... | collective-permute-start | bytes 786440 | tf_op jit(solution)/shard_map/ppermute | solution.py:499
  169.0 1.4 collective-permute-start.12
  171.3 16.0 %collective-permute-start.13 = (f32[64,128]{1,0:T(8,128)S(1)}, f32[64,128]{1,0:T(8,128)S(1)}, u32[]{:S(2)}, u32[]{:S(2)}) collective-permute-start(f32[64,128]{1,0:T(8,128)S(1)} %add.167.over0_ref), channel_id=1, source_target_pairs={{0,2},{2,4},{4,6},{6,0},{1,3},{3,5},{5,7},{7,1},{8,10},{10,12},{12... | collective-permute-start | bytes 98312 | tf_op jit(solution)/shard_map/ppermute | solution.py:430
  184.7 4.3 %collective-permute-start.14 = (f32[64,128]{1,0:T(8,128)S(1)}, f32[64,128]{1,0:T(8,128)S(1)}, u32[]{:S(2)}, u32[]{:S(2)}) collective-permute-start(f32[64,128]{1,0:T(8,128)S(1)} %add.167.over0_ref), channel_id=1, source_target_pairs={{0,4},{2,6},{4,0},{6,2},{1,5},{3,7},{5,1},{7,3},{8,12},{10,14},{12... | collective-permute-start | bytes 98312 | tf_op jit(solution)/shard_map/ppermute | solution.py:430
  185.2 3.7 %collective-permute-start.15 = (f32[64,128]{1,0:T(8,128)S(1)}, f32[64,128]{1,0:T(8,128)S(1)}, u32[]{:S(2)}, u32[]{:S(2)}) collective-permute-start(f32[64,128]{1,0:T(8,128)S(1)} %add.167.over0_ref), channel_id=1, source_target_pairs={{0,6},{2,0},{4,2},{6,4},{1,7},{3,1},{5,3},{7,5},{8,14},{10,8},{12,... | collective-permute-start | bytes 98312 | tf_op jit(solution)/shard_map/ppermute | solution.py:430
  (20 other events, 155.9 us)
Sparse Core Ops, SparseCore 0:
  21.8 37.5 all-gather.3
  63.0 51.7 all-gather.5
